TPU v7x, 32 devices: a whole 2x2x4 slice. The times are simulated.
32 devices in a mesh: groups: 2 (over y), latent: 8 (over z, x), hidden: 2 (over core).
Axes of the slice: x: 2, y: 2, z: 4, core: 2. Of those that a mesh axis runs over, the one named last changes fastest.
Arguments:
- tokens: bfloat16 [32, 8192], P(('groups', 'latent'), 'hidden'), parts along dimension 0, may hold values from -6 to 6
- b_dec: float32 [16384], P(('groups', 'hidden')), parts along dimension 0, may hold values from -3 to 3
- w_enc: bfloat16 [2048, 8192], P(('groups', 'latent'), 'hidden'), parts along dimension 0
- b_enc: float32 [2048], P(('groups', 'latent')), parts along dimension 0, may hold values from -3 to 3
- w_dec: bfloat16 [2048, 8192], P(('groups', 'latent'), 'hidden'), parts along dimension 0
- bias_moments: float32 [2, 2048], P(None, ('groups', 'latent')), parts along dimension 1, may hold values from 0.001 to 1
- pool: bfloat16 [128, 8192], P(('groups', 'latent'), 'hidden'), parts along dimension 0, may hold values from -6 to 6
- active_blocks: int32 [8, 16], P('groups'), parts along dimension 0, may hold values from 0 to 31, as said below
- dead_ids: int32 [64], P('groups'), parts along dimension 0, may hold values from 0 to 1023, as said below
- row_ids: int32 [64], P('groups'), parts along dimension 0, may hold values from 0 to 63, as said below
Outputs:
- losses: float32 [32], P(('groups', 'latent')), parts along dimension 0
- new_enc: bfloat16 [2048, 8192], P(('groups', 'latent'), 'hidden'), parts along dimension 0
- new_dec: bfloat16 [2048, 8192], P(('groups', 'latent'), 'hidden'), parts along dimension 0
- new_b_enc: float32 [2048], P(('groups', 'latent')), parts along dimension 0
- new_moments: float32 [2, 2048], P(None, ('groups', 'latent')), parts along dimension 1
There are 2 independent parts, one for each index of `groups`. A program takes and returns all parts, laid end to end along the dimension named above; each array names one. Nothing has to cross between parts.
Inputs may be any that keep to these rules, and one draw needn't show every extreme that they name: `active_blocks`: each row names 16 distinct blocks. `dead_ids`: distinct latents; latent index i owns latents i * 128 to (i + 1) * 128 - 1, at most 8 of them are dead, and some index has exactly that many. `row_ids`: row r is held by latent index r // 8; the dead latents of one latent index take their rows from distinct holding indices; a row may serve several dead latents.
All inputs are finite; a program needn't handle non-finite values.
Results may differ from a plain program's by a relative error of at most 0.0004.
The roundings to bfloat16 on the way count: a program that leaves them out, or rounds other values in their place, can miss the bound.
Values may be sent and summed in bfloat16 or wider, within the bound.
No kernel may reach another device: no remote copies, remote signals or barrier semaphores. Data moves between devices by JAX's collectives and lax.ppermute only.
A program may use at most 64 MiB of HBM per device.

v0:
```python
import jax
import jax.numpy as jnp
from jax import lax
from jax.sharding import PartitionSpec as P

BLOCK = 32


epsilon = 1e-06


def local(tokens, b_dec, w_enc, b_enc, w_dec, bias_moments, pool, active_blocks, dead_ids, row_ids):
    lat_dev, half_width = w_enc.shape
    owners = lax.axis_size("latent")
    my_index = lax.axis_index("latent")
    latents = lat_dev * owners
    tok_dev = tokens.shape[0]
    all_tokens = tok_dev * owners
    tile_count = active_blocks.shape[0]
    blocks_here = lat_dev // BLOCK
    first_id = my_index * lat_dev
    local_ids = first_id + jnp.arange(lat_dev, dtype=jnp.int32)
    dec_wide = w_dec.astype(jnp.float32)
    dec_part = jnp.sum(dec_wide * dec_wide, axis=1)
    enc_part = jnp.sum(jnp.square(w_enc.astype(jnp.float32)), axis=1)
    centered = (
        lax.all_gather(tokens, "latent", axis=0, tiled=True).astype(jnp.float32) - b_dec[None, :]
    ).astype(jnp.bfloat16)
    partial_pre = lax.dot_general(
        centered, w_enc, (((1,), (1,)), ((), ())), preferred_element_type=jnp.float32
    )
    dec_sq, enc_sq = lax.psum((dec_part, enc_part), "hidden")
    pre_sum = lax.psum(partial_pre, "hidden")
    pre_act = pre_sum + b_enc[None, :]
    local_blocks = my_index * blocks_here + jnp.arange(blocks_here, dtype=jnp.int32)
    listed = jnp.any(active_blocks[:, :, None] == local_blocks[None, None, :], axis=1).astype(
        jnp.float32
    )
    latent_mask = jnp.repeat(listed, BLOCK, axis=1)
    shaped = jnp.maximum(pre_act, 0.0).reshape(tile_count, all_tokens // tile_count, lat_dev)
    latent_codes = (
        (shaped * latent_mask[:, None, :]).reshape(all_tokens, lat_dev).astype(jnp.bfloat16)
    )
    rebuilt = (
        lax.psum_scatter(
            jnp.dot(latent_codes, w_dec, preferred_element_type=jnp.float32),
            "latent",
            scatter_dimension=0,
            tiled=True,
        )
        + b_dec[None, :]
    )
    tokens_wide = tokens.astype(jnp.float32)
    residual = tokens_wide - rebuilt
    centered_wide = tokens_wide - b_dec[None, :]
    error_sum, input_sum = lax.psum(
        (jnp.sum(residual * residual, axis=1), jnp.sum(centered_wide * centered_wide, axis=1)),
        "hidden",
    )
    dec_norm = jnp.sqrt(dec_sq)
    enc_norm = jnp.sqrt(enc_sq)
    penalty_part = jnp.dot(
        latent_codes.astype(jnp.float32), dec_norm, precision=lax.Precision.HIGHEST
    )
    dead_hit = dead_ids[:, None] == local_ids[None, :]
    is_dead = jnp.any(dead_hit, axis=0)
    alive_part = jnp.sum(jnp.where(is_dead, 0.0, enc_norm))
    penalty, alive_total = lax.psum((penalty_part, alive_part), "latent")
    own_penalty = lax.dynamic_slice_in_dim(penalty, my_index * tok_dev, tok_dev, 0)
    full_width = half_width * lax.axis_size("hidden")
    losses = (
        error_sum / full_width / (input_sum / full_width + epsilon) + 5.0 * own_penalty / latents
    )
    alive_mean = alive_total / (latents - dead_ids.shape[0])
    hit_matrix = dead_hit.astype(jnp.bfloat16)
    pool_dev = pool.shape[0]
    pick_row = (row_ids[:, None] == jnp.arange(pool_dev * owners, dtype=jnp.int32)[None, :]).astype(
        jnp.bfloat16
    )
    choose = jnp.dot(hit_matrix.T, pick_row, preferred_element_type=jnp.float32).astype(
        jnp.bfloat16
    )
    fresh_rows = jnp.dot(
        choose,
        lax.all_gather(pool, "latent", axis=0, tiled=True),
        preferred_element_type=jnp.float32,
    )
    fresh_rows = jnp.where(is_dead[:, None], fresh_rows - b_dec[None, :], 0.0)
    fresh_sq = lax.psum(jnp.sum(fresh_rows * fresh_rows, axis=1), "hidden")
    unit_rows = fresh_rows * lax.rsqrt(fresh_sq + epsilon)[:, None]
    new_enc = jnp.where(
        is_dead[:, None], 0.2 * alive_mean * unit_rows, w_enc.astype(jnp.float32)
    ).astype(jnp.bfloat16)
    unit_sq = fresh_sq / (fresh_sq + epsilon)
    direction_sq = jnp.where(is_dead, unit_sq, dec_sq)
    direction = jnp.where(is_dead[:, None], unit_rows, dec_wide)
    new_dec = (direction * lax.rsqrt(direction_sq + epsilon)[:, None]).astype(jnp.bfloat16)
    keep_mask = jnp.where(is_dead, 0.0, 1.0)
    new_b_enc = b_enc * keep_mask
    new_moments = bias_moments * keep_mask[None, :]
    return (losses, new_enc, new_dec, new_b_enc, new_moments)


def solution(mesh):
    return jax.shard_map(
        local,
        mesh=mesh,
        in_specs=(
            P(("groups", "latent"), "hidden"),
            P(("groups", "hidden")),
            P(("groups", "latent"), "hidden"),
            P(("groups", "latent")),
            P(("groups", "latent"), "hidden"),
            P(None, ("groups", "latent")),
            P(("groups", "latent"), "hidden"),
            P("groups", None),
            P("groups"),
            P("groups"),
        ),
        out_specs=(
            P(("groups", "latent")),
            P(("groups", "latent"), "hidden"),
            P(("groups", "latent"), "hidden"),
            P(("groups", "latent")),
            P(None, ("groups", "latent")),
        ),
        check_vma=False,
    )
```

profile of v0, /device:TPU:0, one launch (start us, length us, event | category | flops | bytes accessed | tf_op | source)
XLA Modules:
  0.0 157.0 jit_solution(5097286681464416475)
XLA Ops:
  7.2 0.0 copy-start.1
  7.2 0.0 all-reduce.5.cloned.1.call-start
  7.2 1.0 compare_reduce_fusion.1
  8.2 0.1 broadcast_in_dim.31
  8.3 0.1 mul.69
  8.4 32.5 %all-gather = bf16[8,2,4096]{2,1,0:T(2,128)(2,1)S(1)} all-gather(bf16[1,2,4096]{2,1,0:T(2,128)(2,1)} %bitcast.13), channel_id=1, replica_groups=mesh['groups'=2,'latent'=8,'hidden'=2] {'latent'}, dimensions={0}, use_global_device_ids=true | all-gather | bytes 147456 | tf_op jit(solution)/shard_map/all_gather | solution.py:27
  40.9 0.0 copy-start
  40.9 1.7 %fusion.6 = f32[16,128]{1,0:T(8,128)S(1)} fusion(bf16[128,4096]{1,0:T(8,128)(2,1)} %param.12, f32[16,4096]{1,0:T(8,128)S(1)} %reshape.35, f32[4096]{0:T(1024)} %param.11), kind=kOutput, calls=%fused_computation.15 | convolution fusion | flops 16908288 | bytes 1335296 | tf_op jit(solution)/shard_map/dot_general | solution.py:29
  42.7 0.0 copy-start.3
  42.7 2.6 %psum.56 = f32[16,128]{1,0:T(8,128)S(1)} all-reduce(f32[16,128]{1,0:T(8,128)S(1)} %fusion.6), channel_id=1, replica_groups=mesh['groups'=2,'latent'=8,'hidden'=2] {'hidden'}, use_global_device_ids=true, to_apply=%region_0.0 | all-reduce | flops 2048 | bytes 16384 | tf_op jit(solution)/shard_map/psum | solution.py:33
  45.3 0.7 multiply_convert_fusion
  45.9 0.0 copy-done.1
  46.0 0.0 copy-start.9
  46.0 0.0 copy-start.8
  46.0 0.0 copy-start.2
  46.0 0.0 copy-start.7
  46.0 1.0 fusion.26
  47.0 0.0 all-reduce.5.cloned.1.call-update
  47.0 0.3 fusion.1
  47.3 0.0 copy-done
  47.3 0.0 copy-start.4
  47.3 0.0 copy-start.5
  47.3 0.0 copy-start.6
  47.3 0.3 fusion.4
  47.6 0.0 copy-done.3
  47.6 31.5 %all_gather.7 = bf16[64,4096]{1,0:T(8,128)(2,1)S(1)} all-gather(bf16[8,4096]{1,0:T(8,128)(2,1)S(1)} %copy-done.3), channel_id=1, replica_groups=mesh['groups'=2,'latent'=8,'hidden'=2] {'latent'}, dimensions={0}, use_global_device_ids=true | all-gather | bytes 589824 | tf_op jit(solution)/shard_map/all_gather | solution.py:85
  79.1 0.0 copy-done.9
  79.1 0.6 dynamic-slice
  80.4 0.0 copy-done.8
  80.4 0.1 compare_reduce_fusion
  80.5 0.0 copy-done.2
  80.5 0.0 copy-done.7
  80.5 2.1 %multiply_reduce_fusion = (f32[128]{0:T(128)S(1)}, f32[128,4096]{1,0:T(8,128)}) fusion(f32[4096]{0:T(1024)S(1)} %copy-done.2, bf16[64,4096]{1,0:T(8,128)(2,1)S(1)} %all_gather.7, s32[32]{0:T(128)S(1)} %copy-done.7, s32[128]{0:T(128)S(1)} %iota_add_fusion, s32[32]{0:T(128)S(1)} %copy-done.8, pred[128]{0:T(512)(128)(4,1)S(1)} %compare_reduce_fusion), kind=kOutput, calls=%fused_computation.11 | convolution fusion | flops 69744512 | bytes 2639232 | tf_op jit(solution)/shard_map/dot_general | solution.py:83
  82.6 36.9 %all-reduce.5.cloned.1.call-done = f32[16,4096]{1,0:T(8,128)} async-done(((f32[16,4096]{1,0:T(8,128)}), f32[16,4096]{1,0:T(8,128)}) %all-reduce.5.cloned.1.call-update) | async-done | bytes 262160
  119.4 0.0 copy-done.4
  119.4 1.1 fusion.9
  120.5 2.5 %all-reduce.2 = (f32[128]{0:T(128)S(1)}, f32[128]{0:T(128)S(1)}, f32[2]{0:T(128)S(1)}, f32[2]{0:T(128)S(1)}, f32[128]{0:T(128)S(1)}) all-reduce(f32[128]{0:T(128)S(1)} %fusion.1, f32[128]{0:T(128)S(1)} %fusion.4, f32[2]{0:T(128)S(1)} %get-tuple-element.6, ...), channel_id=1, replica_groups=mesh['groups'=2,'latent'=8,'hidden'=2] {'hidden'}, use_global_device_ids=true, to_apply=%region_8.0 | all-reduce | flops 388 | bytes 3104 | tf_op jit(solution)/shard_map/psum | solution.py:32
  123.0 0.1 convolution_bitcast_fusion
  123.1 0.0 copy-done.5
  123.1 1.1 broadcast_select_fusion
  124.3 20.3 %all-reduce.1 = (f32[16]{0:T(128)S(1)}, f32[]{:T(128)}) all-reduce(f32[16]{0:T(128)S(1)} %convolution_bitcast_fusion, f32[]{:T(128)} %get-tuple-element.20), channel_id=1, replica_groups=mesh['groups'=2,'latent'=8,'hidden'=2] {'latent'}, use_global_device_ids=true, to_apply=%region_9.0 | all-reduce | flops 17 | bytes 136 | tf_op jit(solution)/shard_map/psum | solution.py:68
  145.2 0.0 copy-done.6
  145.2 0.6 broadcast_multiply_fusion
  145.8 0.6 multiply_add_fusion
  146.4 3.8 %fusion.3 = (bf16[128,4096]{1,0:T(8,128)(2,1)}, bf16[128,4096]{1,0:T(8,128)(2,1)}) fusion(bf16[128,4096]{1,0:T(8,128)(2,1)S(1)} %copy-done.1, f32[128,4096]{1,0:T(8,128)} %get-tuple-element.22, f32[128]{0:T(128)S(1)} %get-tuple-element.18, f32[128]{0:T(128)S(1)} %get-tuple-element.19, pred[128]{0:T(512)(128)(4,1)S(1)} %compare_reduce_fusion, ...), kind=kLoop, calls=%fused_computation.8 | loop fusion | flops 4718592 | bytes 6292612 | tf_op jit(solution)/shard_map/convert_element_type | solution.py:97
  (5 shorter events, 0.1 us)
Async XLA Ops:
  7.2 38.8 %copy-start.1 = (bf16[128,4096]{1,0:T(8,128)(2,1)S(1)}, bf16[128,4096]{1,0:T(8,128)(2,1)}, u32[]{:S(2)}) copy-start(bf16[128,4096]{1,0:T(8,128)(2,1)} %param.14) | copy-start | bytes 3145732
  7.2 112.3 %all-reduce.5.cloned.1.call-start = ((), (), s32[]{:S(2)}) async-start(), calls=%async_computation | async-start | bytes 524288
  40.9 6.3 %copy-start = (bf16[128,4096]{1,0:T(8,128)(2,1)S(1)}, bf16[128,4096]{1,0:T(8,128)(2,1)}, u32[]{:S(2)}) copy-start(bf16[128,4096]{1,0:T(8,128)(2,1)} %param.12) | copy-start | bytes 3145732
  42.7 4.9 %copy-start.3 = (bf16[8,4096]{1,0:T(8,128)(2,1)S(1)}, bf16[8,4096]{1,0:T(8,128)(2,1)}, u32[]{:S(2)}) copy-start(bf16[8,4096]{1,0:T(8,128)(2,1)} %param.16) | copy-start | bytes 196612
  46.0 33.2 %copy-start.9 = (u32[32]{0:T(128)S(1)}, u32[32]{0:T(128)}, u32[]{:S(2)}) copy-start(u32[32]{0:T(128)} %constant.44) | copy-start | bytes 388
  46.0 34.4 %copy-start.8 = (s32[32]{0:T(128)S(1)}, s32[32]{0:T(128)}, u32[]{:S(2)}) copy-start(s32[32]{0:T(128)} %param.18) | copy-start | bytes 388
  46.0 34.5 %copy-start.2 = (f32[4096]{0:T(1024)S(1)}, f32[4096]{0:T(1024)}, u32[]{:S(2)}) copy-start(f32[4096]{0:T(1024)} %param.11) | copy-start | bytes 49156
  46.0 34.5 %copy-start.7 = (s32[32]{0:T(128)S(1)}, s32[32]{0:T(128)}, u32[]{:S(2)}) copy-start(s32[32]{0:T(128)} %param.19) | copy-start | bytes 388
  47.3 72.2 %copy-start.4 = (bf16[2,4096]{1,0:T(2,128)(2,1)S(1)}, bf16[2,4096]{1,0:T(2,128)(2,1)}, u32[]{:S(2)}) copy-start(bf16[2,4096]{1,0:T(2,128)(2,1)} %param.10) | copy-start | bytes 49156
  47.3 75.8 %copy-start.5 = (f32[128]{0:T(128)S(1)}, f32[128]{0:T(128)}, u32[]{:S(2)}) copy-start(f32[128]{0:T(128)} %param.13) | copy-start | bytes 1540
  47.3 97.9 %copy-start.6 = (f32[2,128]{1,0:T(2,128)S(1)}, f32[2,128]{1,0:T(2,128)}, u32[]{:S(2)}) copy-start(f32[2,128]{1,0:T(2,128)} %param.15) | copy-start | bytes 3076
Sparse Core Ops, SparseCore 0:
  47.1 72.2 all-reduce.4
where the time goes:
time: 157 us
  blocking collectives  89.4 us (57%)
  waiting for transfers between devices  36.9 us (24%)
  between operations  15.5 us (10%)
  other arithmetic  9.46 us (6%)
  matrix products  4.87 us (3%)
    unnamed x2, waiting for transfers between devices  36.9 us
    all_gather x1, blocking collectives, local(): lax.all_gather(tokens, 'latent', axis=0, tiled=True).astype(jnp.float32)  32.5 us
    all_gather x1, blocking collectives, local(): lax.all_gather(pool, 'latent', axis=0, tiled=True)  31.5 us
    psum x1, blocking collectives, local(): penalty, alive_total = lax.psum((penalty_part, alive_part), 'latent')  20.3 us
    convert_element_type x1, other arithmetic, local(): (direction * lax.rsqrt(direction_sq + epsilon)[:, None]).astype(jnp.bfloa...  3.78 us
  transfers between devices with their start and end apart: 1, of which 1 were waited for; matrix products, arithmetic and copies ran while one was open for 2% of the time, Pallas kernels for 0%

commit v1 on v0

v1 whole, which is shorter than its diff:
```python
import jax
import jax.numpy as jnp
from jax import lax
from jax.sharding import PartitionSpec as P

BLOCK = 32
EPS = 1e-06
F32, BF16 = jnp.float32, jnp.bfloat16


def swap(x, axis, mask):
    size = lax.axis_size(axis)
    return lax.ppermute(x, axis, [(i, i ^ mask) for i in range(size)])


def halves(x):
    high = lax.reduce_precision(x, 8, 7)
    return high.astype(BF16), (x - high).astype(BF16)


def local(tokens, b_dec, w_enc, b_enc, w_dec, bias_moments, pool, active_blocks, dead_ids, row_ids):
    lat_dev, width = w_enc.shape
    owners = lax.axis_size("latent")
    me = lax.axis_index("latent")
    tok_dev, pool_dev = tokens.shape[0], pool.shape[0]
    latents, count = lat_dev * owners, tok_dev * owners
    dead = dead_ids.shape[0]
    tiles = active_blocks.shape[0]
    masks = []
    while 1 << len(masks) < owners:
        masks.append(1 << len(masks))
    order = [0]
    for mask in reversed(masks):
        order = order + [i ^ mask for i in order]
    peer = me ^ jnp.array(order, jnp.int32)

    owner_of, holder_of = dead_ids // lat_dev, row_ids // pool_dev
    slots = me * pool_dev + jnp.arange(pool_dev, dtype=jnp.int32)
    take = jnp.any(
        (owner_of[None, None, :] == peer[:, None, None]) & (row_ids[None, None, :] == slots[None, :, None]),
        axis=2,
    ).astype(BF16)
    rows = jnp.dot(take, pool, preferred_element_type=F32).astype(BF16)

    gathered = tokens
    rows = rows.reshape((2,) * len(masks) + (width,))
    for step, mask in enumerate(reversed(masks)):
        axis = len(masks) - 1 - step
        kept, sent = lax.index_in_dim(rows, 0, axis), lax.index_in_dim(rows, 1, axis)
        n_tok = gathered.shape[0]
        got = swap(jnp.concatenate([gathered, sent.reshape(-1, width)], axis=0), "latent", mask)
        gathered = jnp.concatenate([gathered, got[:n_tok]], axis=0)
        rows = jnp.concatenate([kept, got[n_tok:].reshape(kept.shape)], axis=axis)
    rows = rows.reshape(owners, width)

    local_ids = me * lat_dev + jnp.arange(lat_dev, dtype=jnp.int32)
    dead_hit = dead_ids[None, :] == local_ids[:, None]
    is_dead = jnp.any(dead_hit, axis=1)
    place = jnp.any(dead_hit[:, None, :] & (holder_of[None, None, :] == peer[None, :, None]), axis=2).astype(BF16)

    centered = (gathered.astype(F32) - b_dec[None, :]).astype(BF16)
    partial_pre = lax.dot_general(centered, w_enc, (((1,), (1,)), ((), ())), preferred_element_type=F32)
    dec_wide = w_dec.astype(F32)
    dec_part = jnp.sum(dec_wide * dec_wide, axis=1)
    enc_part = jnp.sum(jnp.square(w_enc.astype(F32)), axis=1)
    fresh = rows.astype(F32) - b_dec[None, :]
    fresh_part = jnp.sum(fresh * fresh, axis=1)
    own_centered = tokens.astype(F32) - b_dec[None, :]
    input_part = jnp.sum(own_centered * own_centered, axis=1)
    tail = jnp.concatenate([fresh_part, input_part])
    pad = -tail.shape[0] % lat_dev
    tail = jnp.pad(tail, (0, pad)).reshape(-1, lat_dev)
    message = jnp.concatenate([partial_pre, dec_part[None], enc_part[None], tail], axis=0)
    total = message + swap(message, "hidden", 1)
    pre = total[:count] + b_enc[None, :]
    dec_sq, enc_sq = total[count], total[count + 1]
    tail = total[count + 2 :].reshape(-1)
    fresh_sq, input_sum = tail[:owners], tail[owners : owners + tok_dev]

    row_tile = (peer[:, None] * tok_dev + jnp.arange(tok_dev, dtype=jnp.int32)[None, :]).reshape(-1) // (count // tiles)
    my_block = local_ids // BLOCK
    listed = jnp.any(active_blocks[:, :, None] == my_block[None, None, :], axis=1).astype(F32)
    mask = jnp.zeros((count, lat_dev), F32)
    for tile in range(tiles):
        mask = jnp.where(row_tile[:, None] == tile, listed[tile][None, :], mask)
    codes = lax.reduce_precision(jnp.maximum(pre, 0.0) * mask, 8, 7)
    dec_norm = jnp.sqrt(dec_sq)
    enc_norm = jnp.sqrt(enc_sq)
    side = jnp.concatenate(
        [codes * dec_norm[None, :], jnp.broadcast_to(jnp.where(is_dead, 0.0, enc_norm)[None, :], (count, lat_dev))], axis=1
    )
    rebuilt = jnp.dot(codes.astype(BF16), w_dec, preferred_element_type=F32)
    for mask_bit in masks:
        half = rebuilt.shape[0] // 2
        high, low = halves(side[half:])
        got = swap(jnp.concatenate([rebuilt[half:].astype(BF16), high, low], axis=1), "latent", mask_bit).astype(F32)
        rebuilt = rebuilt[:half] + got[:, :width]
        side = side[:half] + (got[:, width : width + 2 * lat_dev] + got[:, width + 2 * lat_dev :])
    penalty = jnp.sum(side[:, :lat_dev], axis=1)
    alive = jnp.sum(side[:1, lat_dev:], axis=1, keepdims=True)

    residual = own_centered - rebuilt
    error_part = jnp.sum(residual * residual, axis=1)
    error_sum = error_part + swap(error_part, "hidden", 1)
    full = width * lax.axis_size("hidden")
    losses = error_sum / full / (input_sum / full + EPS) + 5.0 * penalty / latents

    alive_mean = alive / (latents - dead)
    unit = fresh * lax.rsqrt(fresh_sq + EPS)[:, None]
    enc_rows = (0.2 * alive_mean * unit).astype(BF16)
    unit_sq = fresh_sq / (fresh_sq + EPS)
    dec_rows = (unit * lax.rsqrt(unit_sq + EPS)[:, None]).astype(BF16)
    placed_dec = jnp.dot(place, dec_rows, preferred_element_type=F32)
    new_dec = jnp.where(is_dead[:, None], placed_dec, dec_wide * lax.rsqrt(dec_sq + EPS)[:, None]).astype(BF16)
    placed_enc = jnp.dot(place, enc_rows, preferred_element_type=F32).astype(BF16)
    new_enc = jnp.where(is_dead[:, None], placed_enc, w_enc)
    keep = jnp.where(is_dead, 0.0, 1.0)
    return losses, new_enc, new_dec, b_enc * keep, bias_moments * keep[None, :]


def solution(mesh):
    both = P(("groups", "latent"), "hidden")
    one = P(("groups", "latent"))
    return jax.shard_map(
        local,
        mesh=mesh,
        in_specs=(both, P(("groups", "hidden")), both, one, both, P(None, ("groups", "latent")), both,
                  P("groups", None), P("groups"), P("groups")),
        out_specs=(one, both, both, one, P(None, ("groups", "latent"))),
        check_vma=False,
    )
```

time: 157 us -> 44.6 us (0.28)
  blocking collectives: 89.4 us -> 0 us
  waiting for transfers between devices: 36.9 us -> 14.9 us
  between operations: 15.5 us -> 1.71 us
  starting transfers between devices: 0.04 us -> 10.7 us
  other arithmetic: 9.46 us -> 11.7 us
    all_gather x2 -> x0, blocking collectives: 64 us -> none  [the longest x1 32.5 us: local(): lax.all_gather(tokens, 'latent', axis=0, tiled=True).astype(jnp.float32)]
    unnamed x2 -> x0, waiting for transfers between devices: 36.9 us -> none
    psum x3 -> x0, blocking collectives: 25.4 us -> none  [the longest x1 20.3 us: local(): penalty, alive_total = lax.psum((penalty_part, alive_part), 'latent')]
    ppermute x0 -> x8, waiting for transfers between devices: none -> 14.9 us  [swap(): return lax.ppermute(x, axis, [(i, i ^ mask) for i in range(size)])]
    ppermute x0 -> x8, starting transfers between devices: none -> 10.7 us  [swap(): return lax.ppermute(x, axis, [(i, i ^ mask) for i in range(size)])]
    convert_element_type x3 -> x7, other arithmetic: 4.45 us -> 0.06 us  [the longest x3 0.04 us: local(): swap(jnp.concatenate([rebuilt[half:].astype(BF16), high, low], axis=1), '...]
    eq x0 -> x5, other arithmetic: none -> 1.6 us  [the longest x1 0.76 us: local(): row_ids[None, None, :] == slots[None, :, None]]
    dot_general x3 -> x4, matrix products: 3.16 us -> 3.39 us  [the longest x1 1.47 us: local(): jnp.dot(place, enc_rows, preferred_element_type=F32).astype(BF16)]
  transfers between devices with their start and end apart: 1 -> 8, of which waited for: 1 -> 6; matrix products, arithmetic and copies ran while one was open for 2% -> 21% of each run, Pallas kernels for 0% -> 0%
where the time goes in v1:
time: 44.6 us; the launch traced here: 44.2 us
  waiting for transfers between devices  14.9 us (33%)
  other arithmetic  11.7 us (26%)
  starting transfers between devices  10.7 us (24%)
  matrix products  3.77 us (8%)
  between operations  1.71 us (4%)
  local copies, waits for them, and re-layouts  1.44 us (3%)
    ppermute x8, waiting for transfers between devices, swap(): return lax.ppermute(x, axis, [(i, i ^ mask) for i in range(size)])  14.9 us
    ppermute x8, starting transfers between devices, swap(): return lax.ppermute(x, axis, [(i, i ^ mask) for i in range(size)])  10.7 us
    reduce_sum x1, other arithmetic, local(): enc_part = jnp.sum(jnp.square(w_enc.astype(F32)), axis=1)  1.52 us
    dot_general x1, matrix products, local(): jnp.dot(place, enc_rows, preferred_element_type=F32).astype(BF16)  1.47 us
    dot_general x1, matrix products, local(): placed_dec = jnp.dot(place, dec_rows, preferred_element_type=F32)  1.47 us
    mul x1, other arithmetic, local(): bias_moments * keep[None, :]  1.24 us
    select_n x1, other arithmetic, local(): keep = jnp.where(is_dead, 0.0, 1.0)  1.17 us
    concatenate x3, other arithmetic, local(): jnp.concatenate([gathered, sent.reshape(-1, width)], axis=0)  1 us
  transfers between devices with their start and end apart: 8, of which 6 were waited for; matrix products, arithmetic and copies ran while one was open for 21% of the time, Pallas kernels for 0%

profile of v1, /device:TPU:0, one launch (start us, length us, event | category | flops | bytes accessed | tf_op | source)
XLA Modules:
  0.0 44.2 jit_solution(236059269129770045)
XLA Ops:
  0.7 0.8 %broadcast_compare_fusion.2 = pred[8,32]{1,0:T(8,128)(4,1)S(1)} fusion(s32[32]{0:T(128)} %param.20, s32[8]{0:T(128)S(1)} %iota_add_fusion.2), kind=kLoop, calls=%fused_computation.88 | loop fusion | flops 256 | bytes 416 | tf_op jit(solution)/shard_map/eq | solution.py:40
  1.4 0.7 %and_select_fusion = (s32[32]{0:T(128)S(1)}, s32[32]{0:T(128)S(1)}) fusion(s32[32]{0:T(128)} %param.20, s32[32]{0:T(128)} %param.19), kind=kLoop, calls=%fused_computation.91 | loop fusion | flops 960 | bytes 512 | tf_op jit(solution)/shard_map/jit(floor_divide)/jit(_where)/select_n | solution.py:37
  2.1 0.7 %broadcast_multiply_fusion.2 = (s32[8]{0:T(128)S(1)}, s32[8]{0:T(128)S(1)}) fusion(s32[8]{0:T(128)} %constant.94.clone, s32[]{:T(128)S(6)} %axis_index.15), kind=kLoop, calls=%fused_computation.139 | loop fusion | flops 16 | bytes 100 | tf_op jit(solution)/shard_map/mul | solution.py:80
  2.8 0.1 broadcast_compare_fusion.1
  2.8 0.2 and_reduce_fusion.1
  3.1 0.1 convolution_convert_fusion.1
  3.3 0.2 slice_reduce_fusion
  3.6 0.8 %pad_maximum_fusion.2 = bf16[6,4096]{1,0:T(8,128)(2,1)S(1)} fusion(bf16[4,4096]{1,0:T(4,128)(2,1)S(1)} %reshape.285, bf16[2,4096]{1,0:T(2,128)(2,1)} %param.11), kind=kLoop, calls=%fused_computation.36 | loop fusion | flops 98304 | bytes 98304 | tf_op jit(solution)/shard_map/concatenate | solution.py:51
  4.4 4.1 %collective-permute-start = (bf16[6,4096]{1,0:T(8,128)(2,1)S(1)}, bf16[6,4096]{1,0:T(8,128)(2,1)S(1)}, u32[]{:S(2)}, u32[]{:S(2)}) collective-permute-start(bf16[6,4096]{1,0:T(8,128)(2,1)S(1)} %pad_maximum_fusion.2), channel_id=1, source_target_pairs={{0,8},{2,10},{4,12},{6,14},{8,0},{10,2},{12,4},{14,6},{1,9},{3,11}... | collective-permute-start | bytes 147464 | tf_op jit(solution)/shard_map/ppermute | solution.py:13
  8.6 0.7 %broadcast_compare_fusion = (pred[128,32]{0,1:T(8,128)(4,1)S(1)}, pred[128]{0:T(512)(128)(4,1)S(1)}) fusion(s32[128]{0:T(128)S(1)} %get-tuple-element.44, s32[32]{0:T(128)} %param.19), kind=kLoop, calls=%fused_computation.71 | loop fusion | flops 8064 | bytes 4864 | tf_op jit(solution)/shard_map/eq | solution.py:57
  9.3 0.8 %compare_reduce_fusion = pred[4,128]{1,0:T(4,128)(4,1)S(1)} fusion(s32[128]{0:T(128)S(1)} %get-tuple-element.43, s32[4,16]{1,0:T(4,128)} %param.18), kind=kLoop, calls=%fused_computation.56 | loop fusion | flops 15872 | bytes 1280 | tf_op jit(solution)/shard_map/reduce_or | solution.py:82
  10.1 0.1 iota_add_fusion
  10.2 0.1 add.164
  10.3 1.2 %broadcast_select_fusion = (f32[128]{0:T(128)S(1)}, f32[128]{0:T(128)}) fusion(pred[128]{0:T(512)(128)(4,1)S(1)} %get-tuple-element.31, f32[128]{0:T(128)} %param.14), kind=kLoop, calls=%fused_computation.134 | loop fusion | flops 256 | bytes 1664 | tf_op jit(solution)/shard_map/jit(_where)/select_n | solution.py:117
  11.5 1.2 %broadcast_multiply_fusion.1 = f32[2,128]{1,0:T(2,128)} fusion(f32[2,128]{1,0:T(2,128)} %param.16, f32[128]{0:T(128)S(1)} %get-tuple-element.32), kind=kLoop, calls=%fused_computation.124 | loop fusion | flops 256 | bytes 2560 | tf_op jit(solution)/shard_map/mul | solution.py:118
  12.7 1.5 %multiply_reduce_fusion = f32[128]{0:T(128)S(1)} fusion(bf16[128,4096]{1,0:T(8,128)(2,1)} %param.13), kind=kLoop, calls=%fused_computation.8 | loop fusion | flops 1572736 | bytes 1049088 | tf_op jit(solution)/shard_map/reduce_sum | solution.py:65
  14.3 0.1 fusion.54
  14.7 1.6 %collective-permute-start.1 = (bf16[8,4096]{1,0:T(8,128)(2,1)S(1)}, bf16[8,4096]{1,0:T(8,128)(2,1)S(1)}, u32[]{:S(2)}, u32[]{:S(2)}) collective-permute-start(bf16[8,4096]{1,0:T(8,128)(2,1)S(1)} %pad_maximum_fusion.3), channel_id=1, source_target_pairs={{0,4},{2,6},{4,0},{6,2},{8,12},{10,14},{12,8},{14,10},{1,5},{3,7},... | collective-permute-start | bytes 196616 | tf_op jit(solution)/shard_map/ppermute | solution.py:13
  16.3 0.3 fusion.2
  16.6 2.4 %collective-permute-done.1 = bf16[8,4096]{1,0:T(8,128)(2,1)S(1)} collective-permute-done((bf16[8,4096]{1,0:T(8,128)(2,1)S(1)}, bf16[8,4096]{1,0:T(8,128)(2,1)S(1)}, u32[]{:S(2)}, u32[]{:S(2)}) %collective-permute-start.1) | collective-permute-done | bytes 65568 | tf_op jit(solution)/shard_map/ppermute | solution.py:13
  19.1 0.1 fusion.23
  19.3 0.1 pad_maximum_fusion
  19.4 1.6 %collective-permute-start.2 = (bf16[12,4096]{1,0:T(8,128)(2,1)S(1)}, bf16[12,4096]{1,0:T(8,128)(2,1)S(1)}, u32[]{:S(2)}, u32[]{:S(2)}) collective-permute-start(bf16[12,4096]{1,0:T(8,128)(2,1)S(1)} %pad_maximum_fusion), channel_id=1, source_target_pairs={{0,2},{2,0},{4,6},{6,4},{8,10},{10,8},{12,14},{14,12},{1,3},{3,1},... | collective-permute-start | bytes 294920 | tf_op jit(solution)/shard_map/ppermute | solution.py:13
  20.9 0.1 multiply_reduce_fusion.2
  21.1 3.3 %collective-permute-done.2 = bf16[12,4096]{1,0:T(8,128)(2,1)S(1)} collective-permute-done((bf16[12,4096]{1,0:T(8,128)(2,1)S(1)}, bf16[12,4096]{1,0:T(8,128)(2,1)S(1)}, u32[]{:S(2)}, u32[]{:S(2)}) %collective-permute-start.2) | collective-permute-done | bytes 98336 | tf_op jit(solution)/shard_map/ppermute | solution.py:13
  24.5 0.2 multiply_reduce_fusion.1
  24.7 0.1 copy.39
  24.8 0.1 reduce_sum.68
  24.9 0.4 fusion.3
  25.3 0.1 fusion.46
  25.5 1.2 %collective-permute-done.3 = f32[19,128]{1,0:T(8,128)S(1)} collective-permute-done((f32[19,128]{1,0:T(8,128)S(1)}, f32[19,128]{1,0:T(8,128)S(1)}, u32[]{:S(2)}, u32[]{:S(2)}) %collective-permute-start.3) | collective-permute-done | bytes 9760 | tf_op jit(solution)/shard_map/ppermute | solution.py:13
  26.7 0.3 fusion.34
  27.0 0.1 broadcast_multiply_fusion
  27.2 1.6 %collective-permute-start.4 = (bf16[8,4608]{1,0:T(8,128)(2,1)S(1)}, bf16[8,4608]{1,0:T(8,128)(2,1)S(1)}, u32[]{:S(2)}, u32[]{:S(2)}) collective-permute-start(bf16[8,4608]{1,0:T(8,128)(2,1)S(1)} %pad_maximum_fusion.1), channel_id=1, source_target_pairs={{0,2},{2,0},{4,6},{6,4},{8,10},{10,8},{12,14},{14,12},{1,3},{3,1},... | collective-permute-start | bytes 221192 | tf_op jit(solution)/shard_map/ppermute | solution.py:13
  28.7 0.1 and_reduce_fusion
  28.8 0.1 copy.40
  29.0 0.1 reshape.292
  29.1 2.5 %collective-permute-done.4 = bf16[8,4608]{1,0:T(8,128)(2,1)S(1)} collective-permute-done((bf16[8,4608]{1,0:T(8,128)(2,1)S(1)}, bf16[8,4608]{1,0:T(8,128)(2,1)S(1)}, u32[]{:S(2)}, u32[]{:S(2)}) %collective-permute-start.4) | collective-permute-done | bytes 73760 | tf_op jit(solution)/shard_map/ppermute | solution.py:13
  31.7 1.6 %collective-permute-start.5 = (bf16[4,4608]{1,0:T(4,128)(2,1)S(1)}, bf16[4,4608]{1,0:T(4,128)(2,1)S(1)}, u32[]{:S(2)}, u32[]{:S(2)}) collective-permute-start(bf16[4,4608]{1,0:T(4,128)(2,1)S(1)} %pad_maximum_fusion.4), channel_id=1, source_target_pairs={{0,4},{2,6},{4,0},{6,2},{8,12},{10,14},{12,8},{14,10},{1,5},{3,7},... | collective-permute-start | bytes 110600 | tf_op jit(solution)/shard_map/ppermute | solution.py:13
  33.4 2.4 %collective-permute-done.5 = bf16[4,4608]{1,0:T(4,128)(2,1)S(1)} collective-permute-done((bf16[4,4608]{1,0:T(4,128)(2,1)S(1)}, bf16[4,4608]{1,0:T(4,128)(2,1)S(1)}, u32[]{:S(2)}, u32[]{:S(2)}) %collective-permute-start.5) | collective-permute-done | bytes 36896 | tf_op jit(solution)/shard_map/ppermute | solution.py:13
  35.9 0.1 collective-permute-start.6
  36.0 1.5 %fusion = bf16[128,4096]{1,0:T(8,128)(2,1)} fusion(pred[128,8]{0,1:T(8,128)(4,1)S(1)} %and_reduce_fusion, bf16[128,4096]{1,0:T(8,128)(2,1)S(1)} %copy-done.2, f32[128]{0:T(128)S(1)} %get-tuple-element.19, pred[128]{0:T(512)(128)(4,1)S(1)} %get-tuple-element.31, f32[8,4096]{1,0:T(8,128)S(1)} %reshape.292, f32[8]{0:T(128)S(1)} %get-tuple-element.17, ...), kind=kOutput, calls=%fused_computation.1 | convolution fusion | flops 10616832 | bytes 2246336 | tf_op jit(solution)/shard_map/dot_general | solution.py:113
  37.5 3.1 %collective-permute-done.6 = bf16[2,4608]{1,0:T(2,128)(2,1)S(1)} collective-permute-done((bf16[2,4608]{1,0:T(2,128)(2,1)S(1)}, bf16[2,4608]{1,0:T(2,128)(2,1)S(1)}, u32[]{:S(2)}, u32[]{:S(2)}) %collective-permute-start.6) | collective-permute-done | bytes 18464 | tf_op jit(solution)/shard_map/ppermute | solution.py:13
  40.6 0.2 fusion.26
  40.8 0.1 slice_reduce_fusion.1
  40.9 0.6 %slice_reduce_fusion.2 = f32[]{:T(128)} fusion(f32[2,256]{1,0:T(2,128)S(1)} %fusion.37), kind=kLoop, calls=%fused_computation.117 | loop fusion | flops 127 | bytes 516 | tf_op jit(solution)/shard_map/reduce_sum | solution.py:100
  42.1 1.5 %fusion.1 = bf16[128,4096]{1,0:T(8,128)(2,1)} fusion(bf16[128,4096]{1,0:T(8,128)(2,1)S(1)} %copy-done.1, pred[128,8]{0,1:T(8,128)(4,1)S(1)} %and_reduce_fusion, pred[128]{0:T(512)(128)(4,1)S(1)} %get-tuple-element.31, f32[8,4096]{1,0:T(8,128)S(1)} %reshape.292, f32[8]{0:T(128)S(1)} %get-tuple-element.18, f32[4096]{0:T(1024)S(1)} %copy-done.4, f32[]{:T(128)S(6)} %mul.95), kind=kOutput, calls=%fused_computation.3 | convolution fusion | flops 9568256 | bytes 2245796 | tf_op jit(solution)/shard_map/dot_general | solution.py:115
  43.6 0.6 %fusion.45 = f32[2]{0:T(128)} fusion(f32[19,128]{1,0:T(8,128)S(1)} %fusion.49, f32[2]{0:T(128)S(1)} %slice_reduce_fusion.1, f32[2]{0:T(128)S(1)} %fusion.26, f32[2]{0:T(128)S(1)} %collective-permute-done.7), kind=kLoop, calls=%fused_computation.122 | loop fusion | flops 14 | bytes 40 | tf_op jit(solution)/shard_map/add | solution.py:106
  (64 shorter events, 1.0 us)
Async XLA Ops:
  0.6 2.4 %copy-start = (bf16[8,4096]{1,0:T(8,128)(2,1)S(1)}, bf16[8,4096]{1,0:T(8,128)(2,1)}, u32[]{:S(2)}) copy-start(bf16[8,4096]{1,0:T(8,128)(2,1)} %param.17) | copy-start | bytes 196612
  3.5 11.0 %copy-start.3 = (bf16[2,4096]{1,0:T(2,128)(2,1)S(1)}, bf16[2,4096]{1,0:T(2,128)(2,1)}, u32[]{:S(2)}) copy-start(bf16[2,4096]{1,0:T(2,128)(2,1)} %param.11) | copy-start | bytes 49156
  3.6 12.7 %copy-start.2 = (bf16[128,4096]{1,0:T(8,128)(2,1)S(1)}, bf16[128,4096]{1,0:T(8,128)(2,1)}, u32[]{:S(2)}) copy-start(bf16[128,4096]{1,0:T(8,128)(2,1)} %param.15) | copy-start | bytes 3145732
  4.4 9.8 %collective-permute-start = (bf16[6,4096]{1,0:T(8,128)(2,1)S(1)}, bf16[6,4096]{1,0:T(8,128)(2,1)S(1)}, u32[]{:S(2)}, u32[]{:S(2)}) collective-permute-start(bf16[6,4096]{1,0:T(8,128)(2,1)S(1)} %pad_maximum_fusion.2), channel_id=1, source_target_pairs={{0,8},{2,10},{4,12},{6,14},{8,0},{10,2},{12,4},{14,6},{1,9},{3,11}... | collective-permute-start | bytes 147464 | tf_op jit(solution)/shard_map/ppermute | solution.py:13
  14.5 6.4 %copy-start.4 = (f32[4096]{0:T(1024)S(1)}, f32[4096]{0:T(1024)}, u32[]{:S(2)}) copy-start(f32[4096]{0:T(1024)} %param.12) | copy-start | bytes 49156
  14.6 10.3 %copy-start.1 = (bf16[128,4096]{1,0:T(8,128)(2,1)S(1)}, bf16[128,4096]{1,0:T(8,128)(2,1)}, u32[]{:S(2)}) copy-start(bf16[128,4096]{1,0:T(8,128)(2,1)} %param.13) | copy-start | bytes 3145732
  14.7 4.3 %collective-permute-start.1 = (bf16[8,4096]{1,0:T(8,128)(2,1)S(1)}, bf16[8,4096]{1,0:T(8,128)(2,1)S(1)}, u32[]{:S(2)}, u32[]{:S(2)}) collective-permute-start(bf16[8,4096]{1,0:T(8,128)(2,1)S(1)} %pad_maximum_fusion.3), channel_id=1, source_target_pairs={{0,4},{2,6},{4,0},{6,2},{8,12},{10,14},{12,8},{14,10},{1,5},{3,7},... | collective-permute-start | bytes 196616 | tf_op jit(solution)/shard_map/ppermute | solution.py:13
  19.3 7.4 %copy-start.5 = (f32[128]{0:T(128)S(1)}, f32[128]{0:T(128)}, u32[]{:S(2)}) copy-start(f32[128]{0:T(128)} %param.14) | copy-start | bytes 1540
  19.4 5.0 %collective-permute-start.2 = (bf16[12,4096]{1,0:T(8,128)(2,1)S(1)}, bf16[12,4096]{1,0:T(8,128)(2,1)S(1)}, u32[]{:S(2)}, u32[]{:S(2)}) collective-permute-start(bf16[12,4096]{1,0:T(8,128)(2,1)S(1)} %pad_maximum_fusion), channel_id=1, source_target_pairs={{0,2},{2,0},{4,6},{6,4},{8,10},{10,8},{12,14},{14,12},{1,3},{3,1},... | collective-permute-start | bytes 294920 | tf_op jit(solution)/shard_map/ppermute | solution.py:13
  25.4 1.2 %collective-permute-start.3 = (f32[19,128]{1,0:T(8,128)S(1)}, f32[19,128]{1,0:T(8,128)S(1)}, u32[]{:S(2)}, u32[]{:S(2)}) collective-permute-start(f32[19,128]{1,0:T(8,128)S(1)} %pad_maximum_fusion.7), channel_id=1, source_target_pairs={{0,1},{1,0},{2,3},{3,2},{4,5},{5,4},{6,7},{7,6},{8,9},{9,8},{10,11... | collective-permute-start | bytes 29192 | tf_op jit(solution)/shard_map/ppermute | solution.py:13
  27.2 4.4 %collective-permute-start.4 = (bf16[8,4608]{1,0:T(8,128)(2,1)S(1)}, bf16[8,4608]{1,0:T(8,128)(2,1)S(1)}, u32[]{:S(2)}, u32[]{:S(2)}) collective-permute-start(bf16[8,4608]{1,0:T(8,128)(2,1)S(1)} %pad_maximum_fusion.1), channel_id=1, source_target_pairs={{0,2},{2,0},{4,6},{6,4},{8,10},{10,8},{12,14},{14,12},{1,3},{3,1},... | collective-permute-start | bytes 221192 | tf_op jit(solution)/shard_map/ppermute | solution.py:13
  31.7 4.0 %collective-permute-start.5 = (bf16[4,4608]{1,0:T(4,128)(2,1)S(1)}, bf16[4,4608]{1,0:T(4,128)(2,1)S(1)}, u32[]{:S(2)}, u32[]{:S(2)}) collective-permute-start(bf16[4,4608]{1,0:T(4,128)(2,1)S(1)} %pad_maximum_fusion.4), channel_id=1, source_target_pairs={{0,4},{2,6},{4,0},{6,2},{8,12},{10,14},{12,8},{14,10},{1,5},{3,7},... | collective-permute-start | bytes 110600 | tf_op jit(solution)/shard_map/ppermute | solution.py:13
  35.9 4.7 %collective-permute-start.6 = (bf16[2,4608]{1,0:T(2,128)(2,1)S(1)}, bf16[2,4608]{1,0:T(2,128)(2,1)S(1)}, u32[]{:S(2)}, u32[]{:S(2)}) collective-permute-start(bf16[2,4608]{1,0:T(2,128)(2,1)S(1)} %pad_maximum_fusion.5), channel_id=1, source_target_pairs={{0,8},{2,10},{4,12},{6,14},{8,0},{10,2},{12,4},{14,6},{1,9},{3,11}... | collective-permute-start | bytes 55304 | tf_op jit(solution)/shard_map/ppermute | solution.py:13
  41.5 2.1 %collective-permute-start.7 = (f32[2]{0:T(128)S(1)}, f32[2]{0:T(128)S(1)}, u32[]{:S(2)}, u32[]{:S(2)}) collective-permute-start(f32[2]{0:T(128)S(1)} %fusion.26), channel_id=1, source_target_pairs={{0,1},{1,0},{2,3},{3,2},{4,5},{5,4},{6,7},{7,6},{8,9},{9,8},{10,11... | collective-permute-start | bytes 32 | tf_op jit(solution)/shard_map/ppermute | solution.py:13

commit v2 on v1

v2 whole, which is shorter than its diff:
```python
import jax
import jax.numpy as jnp
from jax import lax
from jax.experimental import pallas as pl
from jax.experimental.pallas import tpu as pltpu
from jax.sharding import PartitionSpec as P

BLOCK = 32
EPS = 1e-06
F32, BF16 = jnp.float32, jnp.bfloat16


def swap(x):
    return lax.ppermute(x, "hidden", [(0, 1), (1, 0)])


def outgoing(tokens, pool, dead_ids, row_ids, owners, lat_dev):
    tok_dev, width = tokens.shape
    pool_dev, dead = pool.shape[0], dead_ids.shape[1]
    part = width // tok_dev

    def body(tokens_ref, pool_ref, dead_ref, row_ref, out_ref):
        me = lax.axis_index("latent")
        first = lax.broadcasted_iota(jnp.int32, (owners, dead), 0) * lat_dev
        there = (dead_ref[...] >= first) & (dead_ref[...] < first + lat_dev)
        slot = lax.broadcasted_iota(jnp.int32, (pool_dev, dead), 0) + me * pool_dev
        goes = jnp.where(there, 1.0, 0.0).astype(BF16)
        lies = jnp.where(row_ref[...] == slot, 1.0, 0.0).astype(BF16)
        take = lax.dot_general(goes, lies, (((1,), (1,)), ((), ())), preferred_element_type=F32).astype(BF16)
        rows = jnp.dot(take, pool_ref[...], preferred_element_type=F32)
        for dest in range(owners):
            out_ref[dest, :, :width] = tokens_ref[...]
        for piece in range(tok_dev):
            out_ref[:, piece, width:] = rows[:, piece * part : (piece + 1) * part].astype(BF16)

    return pl.pallas_call(
        body,
        out_shape=jax.ShapeDtypeStruct((owners, tok_dev, width + part), BF16),
        in_specs=[pl.BlockSpec(memory_space=pltpu.VMEM)] * 4,
        out_specs=pl.BlockSpec(memory_space=pltpu.VMEM),
        name="outgoing",
    )(tokens, pool, dead_ids, row_ids)


def local(tokens, b_dec, w_enc, b_enc, w_dec, bias_moments, pool, active_blocks, dead_ids, row_ids):
    lat_dev, width = w_enc.shape
    owners = lax.axis_size("latent")
    me = lax.axis_index("latent")
    tok_dev, pool_dev = tokens.shape[0], pool.shape[0]
    latents, count = lat_dev * owners, tok_dev * owners
    dead = dead_ids.shape[0]
    tiles = active_blocks.shape[0]
    part = width // tok_dev
    holder_of = row_ids // pool_dev
    everyone = jnp.arange(owners, dtype=jnp.int32)
    sent = outgoing(tokens, pool, dead_ids[None], row_ids[None], owners, lat_dev)
    got = lax.all_to_all(sent, "latent", 0, 0)

    local_ids = me * lat_dev + jnp.arange(lat_dev, dtype=jnp.int32)
    dead_hit = dead_ids[None, :] == local_ids[:, None]
    is_dead = jnp.any(dead_hit, axis=1)
    place = lax.dot_general(
        dead_hit.astype(BF16), (holder_of[None, :] == everyone[:, None]).astype(BF16),
        (((1,), (1,)), ((), ())), preferred_element_type=F32).astype(BF16)
    keep = jnp.where(is_dead, 0.0, 1.0)
    new_b_enc = b_enc * keep
    new_moments = bias_moments * keep[None, :]
    row_tile = jnp.arange(count, dtype=jnp.int32) // (count // tiles)
    my_block = local_ids // BLOCK
    listed = jnp.any(active_blocks[:, :, None] == my_block[None, None, :], axis=1).astype(F32)
    mask = jnp.zeros((count, lat_dev), F32)
    for tile in range(tiles):
        mask = jnp.where(row_tile[:, None] == tile, listed[tile][None, :], mask)
    dec_wide = w_dec.astype(F32)
    dec_part = jnp.sum(dec_wide * dec_wide, axis=1)
    enc_part = jnp.sum(jnp.square(w_enc.astype(F32)), axis=1)
    own_centered = tokens.astype(F32) - b_dec[None, :]
    input_part = jnp.sum(own_centered * own_centered, axis=1)
    centered = (got[:, :, :width].astype(F32) - b_dec[None, None, :]).astype(BF16).reshape(count, width)
    partial_pre = lax.dot_general(centered, w_enc, (((1,), (1,)), ((), ())), preferred_element_type=F32)
    fresh = got[:, :, width:].astype(F32) - b_dec.reshape(tok_dev, part)[None]
    tail = jnp.concatenate([jnp.sum(fresh * fresh, axis=(1, 2)), input_part])
    tail = jnp.pad(tail, (0, -tail.shape[0] % lat_dev)).reshape(-1, lat_dev)
    message = jnp.concatenate([partial_pre, dec_part[None], enc_part[None], tail], axis=0)
    total = message + swap(message)
    pre = total[:count] + b_enc[None, :]
    dec_sq, enc_sq = total[count], total[count + 1]
    tail = total[count + 2 :].reshape(-1)
    fresh_sq, input_sum = tail[:owners], tail[owners : owners + tok_dev]

    codes = lax.reduce_precision(jnp.maximum(pre, 0.0) * mask, 8, 7)
    norms = jnp.where(is_dead, 0.0, jnp.sqrt(enc_sq))
    side = jnp.concatenate(
        [codes * jnp.sqrt(dec_sq)[None, :], jnp.broadcast_to(norms[None, :], (count, lat_dev))], axis=1)
    high = lax.reduce_precision(side, 8, 7)
    rebuilt = jnp.dot(codes.astype(BF16), w_dec, preferred_element_type=F32)
    sent = jnp.concatenate([rebuilt.astype(BF16), high.astype(BF16), (side - high).astype(BF16)], axis=1)
    summed = lax.all_to_all(sent.reshape(owners, tok_dev, -1), "latent", 0, 0)

    unit = fresh * lax.rsqrt(fresh_sq + EPS)[:, None, None]
    unit_sq = fresh_sq / (fresh_sq + EPS)
    dec_rows = (unit * lax.rsqrt(unit_sq + EPS)[:, None, None]).astype(BF16).reshape(owners, width)
    placed_dec = jnp.dot(place, dec_rows, preferred_element_type=F32)
    new_dec = jnp.where(is_dead[:, None], placed_dec, dec_wide * lax.rsqrt(dec_sq + EPS)[:, None]).astype(BF16)
    summed, new_dec, unit = lax.optimization_barrier((summed, new_dec, unit))

    summed = jnp.sum(summed.astype(F32), axis=0)
    residual = own_centered - summed[:, :width]
    error_part = jnp.sum(jnp.square(residual).reshape(tok_dev, -1, 128), axis=1)
    error_peer = swap(error_part)
    side = summed[:, width : width + 2 * lat_dev] + summed[:, width + 2 * lat_dev :]
    alive_mean = jnp.sum(side[:, lat_dev:], axis=1) / (latents - dead)
    enc_rows = ((0.2 * alive_mean)[None, :, None] * unit).astype(BF16).reshape(owners, width)
    placed_enc = jnp.dot(place, enc_rows, preferred_element_type=F32).astype(BF16)
    new_enc = jnp.where(is_dead[:, None], placed_enc, w_enc)
    penalty = jnp.sum(side[:, :lat_dev], axis=1)
    error_sum = jnp.sum(error_part + error_peer, axis=1)
    full = width * lax.axis_size("hidden")
    losses = error_sum / full / (input_sum / full + EPS) + 5.0 * penalty / latents
    return losses, new_enc, new_dec, new_b_enc, new_moments


def solution(mesh):
    both = P(("groups", "latent"), "hidden")
    one = P(("groups", "latent"))
    return jax.shard_map(
        local,
        mesh=mesh,
        in_specs=(both, P(("groups", "hidden")), both, one, both, P(None, ("groups", "latent")), both,
                  P("groups", None), P("groups"), P("groups")),
        out_specs=(one, both, both, one, P(None, ("groups", "latent"))),
        check_vma=False,
    )
```

time: 44.6 us -> 35.3 us (0.79)
  other arithmetic: 11.7 us -> 5.79 us
  waiting for transfers between devices: 14.9 us -> 10.9 us
  Pallas kernels: 0 us -> 1.91 us
  between operations: 1.71 us -> 0.87 us
  local copies, waits for them, and re-layouts: 1.44 us -> 0.89 us
    ppermute x8 -> x2, waiting for transfers between devices: 14.9 us -> 1.15 us  [swap(): return lax.ppermute(x, 'hidden', [(0, 1), (1, 0)])]
    all_to_all x0 -> x2, starting transfers between devices: none -> 10.6 us  [the longest x1 7.25 us: local(): got = lax.all_to_all(sent, 'latent', 0, 0)]
    ppermute x8 -> x2, starting transfers between devices: 10.7 us -> 0.14 us  [swap(): return lax.ppermute(x, 'hidden', [(0, 1), (1, 0)])]
    all_to_all x0 -> x2, waiting for transfers between devices: none -> 9.79 us  [the longest x1 6.13 us: local(): summed = lax.all_to_all(sent.reshape(owners, tok_dev, -1), 'latent', 0, 0)]
    pallas_call x0 -> x1, Pallas kernels: none -> 1.91 us  [outgoing(): pl.pallas_call(body, out_shape=jax.ShapeDtypeStruct((owners, tok_dev, wid...]
    eq x3 -> x0, other arithmetic: 1.58 us -> none  [the longest x1 0.76 us: local(): row_ids[None, None, :] == slots[None, :, None]]
    mul x3, other arithmetic: 1.98 us -> 0.66 us  [the longest x1 0.56 us: local(): new_moments = bias_moments * keep[None, :]]
    concatenate x8 -> x1, other arithmetic: 1.13 us -> 0.01 us  [local(): jnp.concatenate([rebuilt.astype(BF16), high.astype(BF16), (side - high).a...]
  transfers between devices with their start and end apart: 8 -> 4, of which waited for: 6 -> 3; matrix products, arithmetic and copies ran while one was open for 21% -> 21% of each run, Pallas kernels for 0% -> 0%
where the time goes in v2:
time: 35.3 us; the launch traced here: 34.9 us
  waiting for transfers between devices  10.9 us (31%)
  starting transfers between devices  10.8 us (31%)
  other arithmetic  5.79 us (16%)
  matrix products  3.77 us (11%)
  Pallas kernels  1.91 us (5%)
  local copies, waits for them, and re-layouts  0.89 us (3%)
  between operations  0.87 us (2%)
    all_to_all x1, starting transfers between devices, local(): got = lax.all_to_all(sent, 'latent', 0, 0)  7.25 us
    all_to_all x1, waiting for transfers between devices, local(): summed = lax.all_to_all(sent.reshape(owners, tok_dev, -1), 'latent', 0, 0)  6.13 us
    all_to_all x1, waiting for transfers between devices, local(): got = lax.all_to_all(sent, 'latent', 0, 0)  3.66 us
    all_to_all x1, starting transfers between devices, local(): summed = lax.all_to_all(sent.reshape(owners, tok_dev, -1), 'latent', 0, 0)  3.38 us
    pallas_call x1, Pallas kernels, outgoing(): pl.pallas_call(body, out_shape=jax.ShapeDtypeStruct((owners, tok_dev, wid...  1.91 us
    reduce_sum x1, other arithmetic, local(): enc_part = jnp.sum(jnp.square(w_enc.astype(F32)), axis=1)  1.55 us
    dot_general x1, matrix products, local(): placed_dec = jnp.dot(place, dec_rows, preferred_element_type=F32)  1.45 us
    dot_general x1, matrix products, local(): jnp.dot(place, enc_rows, preferred_element_type=F32).astype(BF16)  1.45 us
  transfers between devices with their start and end apart: 4, of which 3 were waited for; matrix products, arithmetic and copies ran while one was open for 21% of the time, Pallas kernels for 0%

profile of v2, /device:TPU:0, one launch (start us, length us, event | category | flops | bytes accessed | tf_op | source)
XLA Modules:
  0.0 34.9 jit_solution(13853800860076383368)
XLA Ops:
  0.6 0.0 copy-start.1
  0.6 1.9 %outgoing.1 = bf16[8,2,6144]{2,1,0:T(2,128)(2,1)} custom-call(bf16[2,4096]{1,0:T(2,128)(2,1)} %tokens_ref.1, bf16[8,4096]{1,0:T(8,128)(2,1)} %pool_ref.1, s32[1,32]{1,0:T(1,128)} %bitcast.60, s32[1,32]{1,0:T(1,128)} %bitcast.59), custom_call_target="tpu_custom_call" | custom-call | tf_op jit(solution)/shard_map/outgoing/pallas_call | solution.py:36
  2.6 7.3 %all-to-all-start = ((bf16[8,2,6144]{2,1,0:T(2,128)(2,1)}), bf16[8,2,6144]{2,1,0:T(2,128)(2,1)S(1)}, u32[]{:S(2)}, u32[]{:S(2)}) async-start(bf16[8,2,6144]{2,1,0:T(2,128)(2,1)} %outgoing.1), calls=%async_computation | async-start | bytes 393216 | tf_op jit(solution)/shard_map/all_to_all | solution.py:57
  9.8 0.7 %and_select_fusion = s32[32]{0:T(128)S(1)} fusion(s32[32]{0:T(128)} %param.19), kind=kLoop, calls=%fused_computation.46 | loop fusion | flops 480 | bytes 256 | tf_op jit(solution)/shard_map/jit(floor_divide)/jit(_where)/select_n | solution.py:54
  10.5 0.0 copy-start.4
  10.5 0.0 copy-start.6
  10.5 0.0 copy-start.2
  10.5 0.0 copy-start.3
  10.5 1.6 %multiply_reduce_fusion = f32[128]{0:T(128)S(1)} fusion(bf16[128,4096]{1,0:T(8,128)(2,1)} %param.12), kind=kLoop, calls=%fused_computation.8 | loop fusion | flops 1572736 | bytes 1049088 | tf_op jit(solution)/shard_map/reduce_sum | solution.py:76
  12.1 0.0 copy-done.1
  12.1 0.0 copy-start
  12.1 0.3 fusion.2
  12.4 0.0 copy-done.7
  12.4 0.1 compare_reduce_fusion.1
  12.5 0.2 convolution_convert_fusion.2
  12.7 0.0 copy-done.5
  12.7 0.1 compare_reduce_fusion
  12.8 0.0 copy-done.4
  12.8 0.5 %broadcast_select_fusion = (f32[128]{0:T(128)S(1)}, f32[128]{0:T(128)}) fusion(pred[128]{0:T(512)(128)(4,1)S(1)} %compare_reduce_fusion.1, f32[128]{0:T(128)S(1)} %copy-done.4), kind=kLoop, calls=%fused_computation.85 | loop fusion | flops 256 | bytes 1664 | tf_op jit(solution)/shard_map/jit(_where)/select_n | solution.py:65
  13.3 0.0 copy-done.6
  13.3 0.6 %broadcast_multiply_fusion.1 = f32[2,128]{1,0:T(2,128)} fusion(f32[2,128]{1,0:T(2,128)S(1)} %copy-done.6, f32[128]{0:T(128)S(1)} %get-tuple-element.26), kind=kLoop, calls=%fused_computation.76 | loop fusion | flops 256 | bytes 2560 | tf_op jit(solution)/shard_map/mul | solution.py:67
  13.9 0.0 copy-done.2
  13.9 0.0 copy-done.3
  13.9 0.1 multiply_reduce_fusion.2
  14.1 3.7 %all-to-all-done = bf16[8,2,6144]{2,1,0:T(2,128)(2,1)S(1)} async-done(((bf16[8,2,6144]{2,1,0:T(2,128)(2,1)}), bf16[8,2,6144]{2,1,0:T(2,128)(2,1)S(1)}, u32[]{:S(2)}, u32[]{:S(2)}) %all-to-all-start) | async-done | bytes 196640 | tf_op jit(solution)/shard_map/all_to_all | solution.py:57
  17.8 0.1 subtract_convert_fusion
  17.9 0.1 reshape.124
  17.9 0.0 copy-done
  17.9 0.4 %fusion.30 = f32[16,128]{1,0:T(8,128)S(1)} fusion(bf16[16,4096]{1,0:T(8,128)(2,1)S(1)} %reshape.124, bf16[128,4096]{1,0:T(8,128)(2,1)S(1)} %copy-done), kind=kOutput, calls=%fused_computation.93 | convolution fusion | flops 16777216 | bytes 1187840 | tf_op jit(solution)/shard_map/dot_general | solution.py:80
  18.3 0.2 multiply_reduce_fusion.1
  18.5 0.1 fusion.25
  18.6 0.1 collective-permute-start
  18.7 1.2 %collective-permute-done = f32[19,128]{1,0:T(8,128)S(1)} collective-permute-done((f32[19,128]{1,0:T(8,128)S(1)}, f32[19,128]{1,0:T(8,128)S(1)}, u32[]{:S(2)}, u32[]{:S(2)}) %collective-permute-start) | collective-permute-done | bytes 9760 | tf_op jit(solution)/shard_map/ppermute | solution.py:14
  19.9 0.3 convolution_convert_fusion.1
  20.2 0.1 broadcast_multiply_fusion
  20.3 0.7 %reshape.126 = bf16[8,2,4608]{2,1,0:T(2,128)(2,1)} reshape(bf16[16,4608]{1,0:T(8,128)(2,1)S(1)} %pad_maximum_fusion) | data formatting | bytes 294912 | tf_op jit(solution)/shard_map/reshape | solution.py:98
  21.1 3.4 %all-to-all-start.1 = ((bf16[8,2,4608]{2,1,0:T(2,128)(2,1)}), bf16[8,2,4608]{2,1,0:T(2,128)(2,1)S(1)}, u32[]{:S(2)}, u32[]{:S(2)}) async-start(bf16[8,2,4608]{2,1,0:T(2,128)(2,1)} %reshape.126), calls=%async_computation.1 | async-start | bytes 294912 | tf_op jit(solution)/shard_map/all_to_all | solution.py:98
  24.4 0.2 fusion.4
  24.6 1.5 %fusion = bf16[128,4096]{1,0:T(8,128)(2,1)} fusion(bf16[128,8]{0,1:T(8,128)(2,1)S(1)} %convolution_convert_fusion.2, bf16[8,4096]{1,0:T(8,128)(2,1)S(1)} %bitcast.54, bf16[128,4096]{1,0:T(8,128)(2,1)S(1)} %copy-done.1, f32[128]{0:T(128)S(1)} %get-tuple-element.15, pred[128]{0:T(512)(128)(4,1)S(1)} %compare_reduce_fusion.1), kind=kOutput, calls=%fused_computation.1 | convolution fusion | flops 10485760 | bytes 2165376 | tf_op jit(solution)/shard_map/dot_general | solution.py:103
  26.1 6.1 %all-to-all-done.1 = bf16[8,2,4608]{2,1,0:T(2,128)(2,1)S(1)} async-done(((bf16[8,2,4608]{2,1,0:T(2,128)(2,1)}), bf16[8,2,4608]{2,1,0:T(2,128)(2,1)S(1)}, u32[]{:S(2)}, u32[]{:S(2)}) %all-to-all-start.1) | async-done | bytes 147488 | tf_op jit(solution)/shard_map/all_to_all | solution.py:98
  32.2 0.1 convert_reduce_fusion
  32.4 0.1 slice_reduce_fusion
  32.5 0.1 collective-permute-start.1
  32.6 0.1 fusion.5
  32.8 1.5 %fusion.1 = bf16[128,4096]{1,0:T(8,128)(2,1)} fusion(bf16[128,4096]{1,0:T(8,128)(2,1)S(1)} %copy-done, bf16[128,8]{0,1:T(8,128)(2,1)S(1)} %convolution_convert_fusion.2, bf16[8,4096]{1,0:T(8,128)(2,1)S(1)} %bitcast.53, pred[128]{0:T(512)(128)(4,1)S(1)} %compare_reduce_fusion.1), kind=kOutput, calls=%fused_computation.3 | convolution fusion | flops 9437184 | bytes 2164864 | tf_op jit(solution)/shard_map/dot_general | solution.py:114
  34.2 0.0 collective-permute-done.1
  34.2 0.1 add_reduce_fusion
  34.3 0.6 %fusion.24 = f32[2]{0:T(128)} fusion(f32[19,128]{1,0:T(8,128)S(1)} %fusion.27, f32[2]{0:T(128)S(1)} %get-tuple-element.12, f32[2]{0:T(128)S(1)} %add_reduce_fusion), kind=kLoop, calls=%fused_computation.73 | loop fusion | flops 12 | bytes 32 | tf_op jit(solution)/shard_map/add | solution.py:119
  (22 shorter events, 0.2 us)
Async XLA Ops:
  0.6 11.5 %copy-start.1 = (bf16[128,4096]{1,0:T(8,128)(2,1)S(1)}, bf16[128,4096]{1,0:T(8,128)(2,1)}, u32[]{:S(2)}) copy-start(bf16[128,4096]{1,0:T(8,128)(2,1)} %param.14) | copy-start | bytes 3145732
  2.6 15.2 %all-to-all-start = ((bf16[8,2,6144]{2,1,0:T(2,128)(2,1)}), bf16[8,2,6144]{2,1,0:T(2,128)(2,1)S(1)}, u32[]{:S(2)}, u32[]{:S(2)}) async-start(bf16[8,2,6144]{2,1,0:T(2,128)(2,1)} %outgoing.1), calls=%async_computation | async-start | bytes 393216 | tf_op jit(solution)/shard_map/all_to_all | solution.py:57
  10.5 1.9 %copy-start.7 = (s32[32]{0:T(128)S(1)}, s32[32]{0:T(128)}, u32[]{:S(2)}) copy-start(s32[32]{0:T(128)} %param.18) | copy-start | bytes 388
  10.5 2.2 %copy-start.5 = (s32[4,16]{1,0:T(4,128)S(1)}, s32[4,16]{1,0:T(4,128)}, u32[]{:S(2)}) copy-start(s32[4,16]{1,0:T(4,128)} %param.17) | copy-start | bytes 772
  10.5 2.3 %copy-start.4 = (f32[128]{0:T(128)S(1)}, f32[128]{0:T(128)}, u32[]{:S(2)}) copy-start(f32[128]{0:T(128)} %param.13) | copy-start | bytes 1540
  10.5 2.8 %copy-start.6 = (f32[2,128]{1,0:T(2,128)S(1)}, f32[2,128]{1,0:T(2,128)}, u32[]{:S(2)}) copy-start(f32[2,128]{1,0:T(2,128)} %param.15) | copy-start | bytes 3076
  10.5 3.4 %copy-start.2 = (f32[4096]{0:T(1024)S(1)}, f32[4096]{0:T(1024)}, u32[]{:S(2)}) copy-start(f32[4096]{0:T(1024)} %param.11) | copy-start | bytes 49156
  10.5 3.4 %copy-start.3 = (bf16[2,4096]{1,0:T(2,128)(2,1)S(1)}, bf16[2,4096]{1,0:T(2,128)(2,1)}, u32[]{:S(2)}) copy-start(bf16[2,4096]{1,0:T(2,128)(2,1)} %tokens_ref.1) | copy-start | bytes 49156
  12.1 5.8 %copy-start = (bf16[128,4096]{1,0:T(8,128)(2,1)S(1)}, bf16[128,4096]{1,0:T(8,128)(2,1)}, u32[]{:S(2)}) copy-start(bf16[128,4096]{1,0:T(8,128)(2,1)} %param.12) | copy-start | bytes 3145732
  18.6 1.2 %collective-permute-start = (f32[19,128]{1,0:T(8,128)S(1)}, f32[19,128]{1,0:T(8,128)S(1)}, u32[]{:S(2)}, u32[]{:S(2)}) collective-permute-start(f32[19,128]{1,0:T(8,128)S(1)} %pad_maximum_fusion.2), channel_id=1, source_target_pairs={{0,1},{1,0},{2,3},{3,2},{4,5},{5,4},{6,7},{7,6},{8,9},{9,8},{10,11... | collective-permute-start | bytes 29192 | tf_op jit(solution)/shard_map/ppermute | solution.py:14
  21.1 11.2 %all-to-all-start.1 = ((bf16[8,2,4608]{2,1,0:T(2,128)(2,1)}), bf16[8,2,4608]{2,1,0:T(2,128)(2,1)S(1)}, u32[]{:S(2)}, u32[]{:S(2)}) async-start(bf16[8,2,4608]{2,1,0:T(2,128)(2,1)} %reshape.126), calls=%async_computation.1 | async-start | bytes 294912 | tf_op jit(solution)/shard_map/all_to_all | solution.py:98
  32.5 1.7 %collective-permute-start.1 = (f32[2,128]{1,0:T(2,128)S(1)}, f32[2,128]{1,0:T(2,128)S(1)}, u32[]{:S(2)}, u32[]{:S(2)}) collective-permute-start(f32[2,128]{1,0:T(2,128)S(1)} %bitcast_reduce_fusion), channel_id=1, source_target_pairs={{0,1},{1,0},{2,3},{3,2},{4,5},{5,4},{6,7},{7,6},{8,9},{9,8},{10,11... | collective-permute-start | bytes 3080 | tf_op jit(solution)/shard_map/ppermute | solution.py:14

commit v3 on v2

--- a/solution.py
+++ b/solution.py
@@ -14,14 +14,19 @@
     return lax.ppermute(x, "hidden", [(0, 1), (1, 0)])
 
 
-def outgoing(tokens, pool, dead_ids, row_ids, owners, lat_dev):
+def middle_out(owners):
+    return sorted(range(owners), key=lambda i: (abs(4 * (i // 2) - owners + 2), i // 2, abs(2 * i - owners + 1)))
+
+
+def outgoing(tokens, pool, dead_ids, row_ids, firsts, lat_dev):
     tok_dev, width = tokens.shape
-    pool_dev, dead = pool.shape[0], dead_ids.shape[1]
+    pool_dev, owners = pool.shape[0], firsts.shape[0]
+    dead = dead_ids.shape[1]
     part = width // tok_dev
 
-    def body(tokens_ref, pool_ref, dead_ref, row_ref, out_ref):
+    def body(tokens_ref, pool_ref, dead_ref, row_ref, firsts_ref, out_ref):
         me = lax.axis_index("latent")
-        first = lax.broadcasted_iota(jnp.int32, (owners, dead), 0) * lat_dev
+        first = firsts_ref[...]
         there = (dead_ref[...] >= first) & (dead_ref[...] < first + lat_dev)
         slot = lax.broadcasted_iota(jnp.int32, (pool_dev, dead), 0) + me * pool_dev
         goes = jnp.where(there, 1.0, 0.0).astype(BF16)
@@ -36,10 +41,10 @@
     return pl.pallas_call(
         body,
         out_shape=jax.ShapeDtypeStruct((owners, tok_dev, width + part), BF16),
-        in_specs=[pl.BlockSpec(memory_space=pltpu.VMEM)] * 4,
+        in_specs=[pl.BlockSpec(memory_space=pltpu.VMEM)] * 5,
         out_specs=pl.BlockSpec(memory_space=pltpu.VMEM),
         name="outgoing",
-    )(tokens, pool, dead_ids, row_ids)
+    )(tokens, pool, dead_ids, row_ids, firsts)
 
 
 def local(tokens, b_dec, w_enc, b_enc, w_dec, bias_moments, pool, active_blocks, dead_ids, row_ids):
@@ -52,9 +57,10 @@
     tiles = active_blocks.shape[0]
     part = width // tok_dev
     holder_of = row_ids // pool_dev
-    everyone = jnp.arange(owners, dtype=jnp.int32)
-    sent = outgoing(tokens, pool, dead_ids[None], row_ids[None], owners, lat_dev)
-    got = lax.all_to_all(sent, "latent", 0, 0)
+    order = middle_out(owners)
+    everyone = jnp.array(order, jnp.int32)
+    sent = outgoing(tokens, pool, dead_ids[None], row_ids[None], everyone[:, None] * lat_dev, lat_dev)
+    got = lax.all_to_all(sent, "latent", 0, 0, axis_index_groups=[order])
 
     local_ids = me * lat_dev + jnp.arange(lat_dev, dtype=jnp.int32)
     dead_hit = dead_ids[None, :] == local_ids[:, None]
@@ -65,7 +71,7 @@
     keep = jnp.where(is_dead, 0.0, 1.0)
     new_b_enc = b_enc * keep
     new_moments = bias_moments * keep[None, :]
-    row_tile = jnp.arange(count, dtype=jnp.int32) // (count // tiles)
+    row_tile = jnp.repeat(everyone, tok_dev) // (owners // tiles)
     my_block = local_ids // BLOCK
     listed = jnp.any(active_blocks[:, :, None] == my_block[None, None, :], axis=1).astype(F32)
     mask = jnp.zeros((count, lat_dev), F32)
@@ -95,7 +101,7 @@
     high = lax.reduce_precision(side, 8, 7)
     rebuilt = jnp.dot(codes.astype(BF16), w_dec, preferred_element_type=F32)
     sent = jnp.concatenate([rebuilt.astype(BF16), high.astype(BF16), (side - high).astype(BF16)], axis=1)
-    summed = lax.all_to_all(sent.reshape(owners, tok_dev, -1), "latent", 0, 0)
+    summed = lax.all_to_all(sent.reshape(owners, tok_dev, -1), "latent", 0, 0, axis_index_groups=[order])
 
     unit = fresh * lax.rsqrt(fresh_sq + EPS)[:, None, None]
     unit_sq = fresh_sq / (fresh_sq + EPS)
@@ -113,6 +119,7 @@
     enc_rows = ((0.2 * alive_mean)[None, :, None] * unit).astype(BF16).reshape(owners, width)
     placed_enc = jnp.dot(place, enc_rows, preferred_element_type=F32).astype(BF16)
     new_enc = jnp.where(is_dead[:, None], placed_enc, w_enc)
+    error_peer, new_enc = lax.optimization_barrier((error_peer, new_enc))
     penalty = jnp.sum(side[:, :lat_dev], axis=1)
     error_sum = jnp.sum(error_part + error_peer, axis=1)
     full = width * lax.axis_size("hidden")

time: 35.3 us -> 32.3 us (0.915)
  waiting for transfers between devices: 10.9 us -> 5.48 us
  starting transfers between devices: 10.8 us -> 13 us
    all_to_all x2, waiting for transfers between devices: 9.79 us -> 4.33 us  [the longest x1 3.25 us: local(): lax.all_to_all(sent.reshape(owners, tok_dev, -1), 'latent', 0, 0, axis_in...]
    all_to_all x2, starting transfers between devices: 10.6 us -> 12.8 us  [the longest x1 7.82 us: local(): got = lax.all_to_all(sent, 'latent', 0, 0, axis_index_groups=[order])]
    reshape x1 -> x2, local copies, waits for them, and re-layouts: 0.72 us -> 0.8 us  [the longest x1 0.72 us: local(): sent.reshape(owners, tok_dev, -1)]
  transfers between devices with their start and end apart: 4 -> 4, of which waited for: 3 -> 3; matrix products, arithmetic and copies ran while one was open for 21% -> 24% of each run, Pallas kernels for 0% -> 0%
where the time goes in v3:
time: 32.3 us; the launch traced here: 31.9 us
  starting transfers between devices  13 us (40%)
  other arithmetic  5.79 us (18%)
  waiting for transfers between devices  5.48 us (17%)
  matrix products  3.77 us (12%)
  Pallas kernels  1.97 us (6%)
  local copies, waits for them, and re-layouts  1.04 us (3%)
  between operations  0.88 us (3%)
    all_to_all x1, starting transfers between devices, local(): got = lax.all_to_all(sent, 'latent', 0, 0, axis_index_groups=[order])  7.82 us
    all_to_all x1, starting transfers between devices, local(): lax.all_to_all(sent.reshape(owners, tok_dev, -1), 'latent', 0, 0, axis_in...  5.03 us
    all_to_all x1, waiting for transfers between devices, local(): lax.all_to_all(sent.reshape(owners, tok_dev, -1), 'latent', 0, 0, axis_in...  3.25 us
    pallas_call x1, Pallas kernels, outgoing(): pl.pallas_call(body, out_shape=jax.ShapeDtypeStruct((owners, tok_dev, wid...  1.97 us
    reduce_sum x1, other arithmetic, local(): enc_part = jnp.sum(jnp.square(w_enc.astype(F32)), axis=1)  1.54 us
    dot_general x1, matrix products, local(): placed_dec = jnp.dot(place, dec_rows, preferred_element_type=F32)  1.45 us
    dot_general x1, matrix products, local(): jnp.dot(place, enc_rows, preferred_element_type=F32).astype(BF16)  1.45 us
    ppermute x2, waiting for transfers between devices, swap(): return lax.ppermute(x, 'hidden', [(0, 1), (1, 0)])  1.15 us
  transfers between devices with their start and end apart: 4, of which 3 were waited for; matrix products, arithmetic and copies ran while one was open for 24% of the time, Pallas kernels for 0%

profile of v3, /device:TPU:0, one launch (start us, length us, event | category | flops | bytes accessed | tf_op | source)
XLA Modules:
  0.0 31.9 jit_solution(827903900657861018)
XLA Ops:
  0.6 0.0 copy-start.8
  0.6 0.0 copy-start.7
  0.7 0.0 copy-start.5
  0.7 0.0 copy-start.4
  0.7 0.0 copy-start.6
  0.7 0.0 copy-start.1
  0.7 2.0 %outgoing.1 = bf16[8,2,6144]{2,1,0:T(2,128)(2,1)} custom-call(bf16[2,4096]{1,0:T(2,128)(2,1)} %tokens_ref.1, bf16[8,4096]{1,0:T(8,128)(2,1)} %pool_ref.1, s32[1,32]{1,0:T(1,128)} %bitcast.60, s32[1,32]{1,0:T(1,128)} %bitcast.59, s32[8,1]{1,0:T(8,128)} %constant.89.firsts_ref), custom_call_target="tpu_custom_call" | custom-call | tf_op jit(solution)/shard_map/outgoing/pallas_call | solution.py:41
  2.7 7.8 %all-to-all-start = ((bf16[8,2,6144]{2,1,0:T(2,128)(2,1)}), bf16[8,2,6144]{2,1,0:T(2,128)(2,1)S(1)}, u32[]{:S(2)}, u32[]{:S(2)}) async-start(bf16[8,2,6144]{2,1,0:T(2,128)(2,1)} %outgoing.1), calls=%async_computation | async-start | bytes 393216 | tf_op jit(solution)/shard_map/all_to_all | solution.py:63
  10.5 0.7 %and_select_fusion = s32[32]{0:T(128)S(1)} fusion(s32[32]{0:T(128)} %param.20), kind=kLoop, calls=%fused_computation.47 | loop fusion | flops 480 | bytes 256 | tf_op jit(solution)/shard_map/jit(floor_divide)/jit(_where)/select_n | solution.py:59
  11.2 1.5 %multiply_reduce_fusion = f32[128]{0:T(128)S(1)} fusion(bf16[128,4096]{1,0:T(8,128)(2,1)} %param.13), kind=kLoop, calls=%fused_computation.8 | loop fusion | flops 1572736 | bytes 1049088 | tf_op jit(solution)/shard_map/reduce_sum | solution.py:82
  12.7 0.0 copy-done.7
  12.7 0.0 copy-start
  12.7 0.1 compare_reduce_fusion.1
  12.8 0.0 copy-done.5
  12.8 0.1 compare_reduce_fusion
  12.9 0.0 copy-done.8
  12.9 0.1 broadcast_in_dim.129
  13.0 0.1 reshape.167
  13.1 0.0 copy-done.4
  13.1 0.5 %broadcast_select_fusion = (f32[128]{0:T(128)S(1)}, f32[128]{0:T(128)}) fusion(pred[128]{0:T(512)(128)(4,1)S(1)} %compare_reduce_fusion.1, f32[128]{0:T(128)S(1)} %copy-done.4), kind=kLoop, calls=%fused_computation.86 | loop fusion | flops 256 | bytes 1664 | tf_op jit(solution)/shard_map/jit(_where)/select_n | solution.py:71
  13.6 0.6 %broadcast_multiply_fusion.1 = f32[2,128]{1,0:T(2,128)} fusion(f32[2,128]{1,0:T(2,128)S(1)} %copy-done.6, f32[128]{0:T(128)S(1)} %get-tuple-element.32), kind=kLoop, calls=%fused_computation.77 | loop fusion | flops 256 | bytes 2560 | tf_op jit(solution)/shard_map/mul | solution.py:73
  14.2 0.0 copy-done.1
  14.2 0.3 fusion.2
  14.5 0.1 multiply_reduce_fusion.2
  14.7 0.2 convolution_convert_fusion.2
  14.9 1.1 %all-to-all-done = bf16[8,2,6144]{2,1,0:T(2,128)(2,1)S(1)} async-done(((bf16[8,2,6144]{2,1,0:T(2,128)(2,1)}), bf16[8,2,6144]{2,1,0:T(2,128)(2,1)S(1)}, u32[]{:S(2)}, u32[]{:S(2)}) %all-to-all-start) | async-done | bytes 196640 | tf_op jit(solution)/shard_map/all_to_all | solution.py:63
  16.0 0.1 subtract_convert_fusion
  16.1 0.1 reshape.165
  16.1 0.4 %fusion.32 = f32[16,128]{1,0:T(8,128)S(1)} fusion(bf16[16,4096]{1,0:T(8,128)(2,1)S(1)} %reshape.165, bf16[128,4096]{1,0:T(8,128)(2,1)S(1)} %copy-done), kind=kOutput, calls=%fused_computation.94 | convolution fusion | flops 16777216 | bytes 1187840 | tf_op jit(solution)/shard_map/dot_general | solution.py:86
  16.5 0.2 multiply_reduce_fusion.1
  16.7 0.1 fusion.27
  16.8 0.1 collective-permute-start
  16.9 1.2 %collective-permute-done = f32[19,128]{1,0:T(8,128)S(1)} collective-permute-done((f32[19,128]{1,0:T(8,128)S(1)}, f32[19,128]{1,0:T(8,128)S(1)}, u32[]{:S(2)}, u32[]{:S(2)}) %collective-permute-start) | collective-permute-done | bytes 9760 | tf_op jit(solution)/shard_map/ppermute | solution.py:14
  18.1 0.3 convolution_convert_fusion.1
  18.4 0.1 broadcast_multiply_fusion
  18.5 0.7 %reshape.168 = bf16[8,2,4608]{2,1,0:T(2,128)(2,1)} reshape(bf16[16,4608]{1,0:T(8,128)(2,1)S(1)} %pad_maximum_fusion) | data formatting | bytes 294912 | tf_op jit(solution)/shard_map/reshape | solution.py:104
  19.3 5.0 %all-to-all-start.1 = ((bf16[8,2,4608]{2,1,0:T(2,128)(2,1)}), bf16[8,2,4608]{2,1,0:T(2,128)(2,1)S(1)}, u32[]{:S(2)}, u32[]{:S(2)}) async-start(bf16[8,2,4608]{2,1,0:T(2,128)(2,1)} %reshape.168), calls=%async_computation.1 | async-start | bytes 294912 | tf_op jit(solution)/shard_map/all_to_all | solution.py:104
  24.3 0.1 fusion.4
  24.5 1.5 %fusion = bf16[128,4096]{1,0:T(8,128)(2,1)} fusion(bf16[128,8]{0,1:T(8,128)(2,1)S(1)} %convolution_convert_fusion.2, bf16[8,4096]{1,0:T(8,128)(2,1)S(1)} %bitcast.54, bf16[128,4096]{1,0:T(8,128)(2,1)S(1)} %copy-done.1, f32[128]{0:T(128)S(1)} %get-tuple-element.21, pred[128]{0:T(512)(128)(4,1)S(1)} %compare_reduce_fusion.1), kind=kOutput, calls=%fused_computation.1 | convolution fusion | flops 10485760 | bytes 2165376 | tf_op jit(solution)/shard_map/dot_general | solution.py:109
  25.9 3.2 %all-to-all-done.1 = bf16[8,2,4608]{2,1,0:T(2,128)(2,1)S(1)} async-done(((bf16[8,2,4608]{2,1,0:T(2,128)(2,1)}), bf16[8,2,4608]{2,1,0:T(2,128)(2,1)S(1)}, u32[]{:S(2)}, u32[]{:S(2)}) %all-to-all-start.1) | async-done | bytes 147488 | tf_op jit(solution)/shard_map/all_to_all | solution.py:104
  29.2 0.1 convert_reduce_fusion
  29.3 0.1 slice_reduce_fusion.1
  29.5 0.1 collective-permute-start.1
  29.6 0.1 fusion.5
  29.7 1.5 %fusion.1 = bf16[128,4096]{1,0:T(8,128)(2,1)} fusion(bf16[128,4096]{1,0:T(8,128)(2,1)S(1)} %copy-done, bf16[128,8]{0,1:T(8,128)(2,1)S(1)} %convolution_convert_fusion.2, bf16[8,4096]{1,0:T(8,128)(2,1)S(1)} %bitcast.53, pred[128]{0:T(512)(128)(4,1)S(1)} %compare_reduce_fusion.1), kind=kOutput, calls=%fused_computation.3 | convolution fusion | flops 9437184 | bytes 2164864 | tf_op jit(solution)/shard_map/dot_general | solution.py:120
  31.2 0.0 collective-permute-done.1
  31.2 0.1 add_reduce_fusion
  31.3 0.6 %fusion.26 = f32[2]{0:T(128)} fusion(f32[19,128]{1,0:T(8,128)S(1)} %fusion.29, f32[2]{0:T(128)S(1)} %get-tuple-element.16, f32[2]{0:T(128)S(1)} %add_reduce_fusion), kind=kLoop, calls=%fused_computation.74 | loop fusion | flops 12 | bytes 32 | tf_op jit(solution)/shard_map/add | solution.py:126
  (26 shorter events, 0.3 us)
Async XLA Ops:
  0.6 12.3 %copy-start.8 = (s32[8]{0:T(128)S(1)}, s32[8]{0:T(128)}, u32[]{:S(2)}) copy-start(s32[8]{0:T(128)} %constant.83.clone) | copy-start | bytes 100
  0.6 12.1 %copy-start.7 = (s32[32]{0:T(128)S(1)}, s32[32]{0:T(128)}, u32[]{:S(2)}) copy-start(s32[32]{0:T(128)} %param.19) | copy-start | bytes 388
  0.7 12.2 %copy-start.5 = (s32[4,16]{1,0:T(4,128)S(1)}, s32[4,16]{1,0:T(4,128)}, u32[]{:S(2)}) copy-start(s32[4,16]{1,0:T(4,128)} %param.18) | copy-start | bytes 772
  0.7 12.5 %copy-start.4 = (f32[128]{0:T(128)S(1)}, f32[128]{0:T(128)}, u32[]{:S(2)}) copy-start(f32[128]{0:T(128)} %param.14) | copy-start | bytes 1540
  0.7 13.0 %copy-start.6 = (f32[2,128]{1,0:T(2,128)S(1)}, f32[2,128]{1,0:T(2,128)}, u32[]{:S(2)}) copy-start(f32[2,128]{1,0:T(2,128)} %param.16) | copy-start | bytes 3076
  0.7 13.5 %copy-start.1 = (bf16[128,4096]{1,0:T(8,128)(2,1)S(1)}, bf16[128,4096]{1,0:T(8,128)(2,1)}, u32[]{:S(2)}) copy-start(bf16[128,4096]{1,0:T(8,128)(2,1)} %param.15) | copy-start | bytes 3145732
  2.7 13.3 %all-to-all-start = ((bf16[8,2,6144]{2,1,0:T(2,128)(2,1)}), bf16[8,2,6144]{2,1,0:T(2,128)(2,1)S(1)}, u32[]{:S(2)}, u32[]{:S(2)}) async-start(bf16[8,2,6144]{2,1,0:T(2,128)(2,1)} %outgoing.1), calls=%async_computation | async-start | bytes 393216 | tf_op jit(solution)/shard_map/all_to_all | solution.py:63
  11.2 3.3 %copy-start.2 = (f32[4096]{0:T(1024)S(1)}, f32[4096]{0:T(1024)}, u32[]{:S(2)}) copy-start(f32[4096]{0:T(1024)} %param.12) | copy-start | bytes 49156
  11.2 3.4 %copy-start.3 = (bf16[2,4096]{1,0:T(2,128)(2,1)S(1)}, bf16[2,4096]{1,0:T(2,128)(2,1)}, u32[]{:S(2)}) copy-start(bf16[2,4096]{1,0:T(2,128)(2,1)} %tokens_ref.1) | copy-start | bytes 49156
  12.7 3.4 %copy-start = (bf16[128,4096]{1,0:T(8,128)(2,1)S(1)}, bf16[128,4096]{1,0:T(8,128)(2,1)}, u32[]{:S(2)}) copy-start(bf16[128,4096]{1,0:T(8,128)(2,1)} %param.13) | copy-start | bytes 3145732
  16.8 1.2 %collective-permute-start = (f32[19,128]{1,0:T(8,128)S(1)}, f32[19,128]{1,0:T(8,128)S(1)}, u32[]{:S(2)}, u32[]{:S(2)}) collective-permute-start(f32[19,128]{1,0:T(8,128)S(1)} %pad_maximum_fusion.2), channel_id=1, source_target_pairs={{0,1},{1,0},{2,3},{3,2},{4,5},{5,4},{6,7},{7,6},{8,9},{9,8},{10,11... | collective-permute-start | bytes 29192 | tf_op jit(solution)/shard_map/ppermute | solution.py:14
  19.3 9.9 %all-to-all-start.1 = ((bf16[8,2,4608]{2,1,0:T(2,128)(2,1)}), bf16[8,2,4608]{2,1,0:T(2,128)(2,1)S(1)}, u32[]{:S(2)}, u32[]{:S(2)}) async-start(bf16[8,2,4608]{2,1,0:T(2,128)(2,1)} %reshape.168), calls=%async_computation.1 | async-start | bytes 294912 | tf_op jit(solution)/shard_map/all_to_all | solution.py:104
  29.5 1.7 %collective-permute-start.1 = (f32[2,128]{1,0:T(2,128)S(1)}, f32[2,128]{1,0:T(2,128)S(1)}, u32[]{:S(2)}, u32[]{:S(2)}) collective-permute-start(f32[2,128]{1,0:T(2,128)S(1)} %bitcast_reduce_fusion), channel_id=1, source_target_pairs={{0,1},{1,0},{2,3},{3,2},{4,5},{5,4},{6,7},{7,6},{8,9},{9,8},{10,11... | collective-permute-start | bytes 3080 | tf_op jit(solution)/shard_map/ppermute | solution.py:14

commit v4 on v3

--- a/solution.py
+++ b/solution.py
@@ -1,3 +1,5 @@
+import math
+
 import jax
 import jax.numpy as jnp
 from jax import lax
@@ -24,7 +26,13 @@
     dead = dead_ids.shape[1]
     part = width // tok_dev
 
-    def body(tokens_ref, pool_ref, dead_ref, row_ref, firsts_ref, out_ref):
+    def body(tokens_ref, pool_ref, dead_ref, row_ref, firsts_ref, out_ref, buffer, sems):
+        copies = [
+            pltpu.make_async_copy(tokens_ref, out_ref.at[dest, :, pl.ds(0, width)], sems.at[dest])
+            for dest in range(owners)
+        ]
+        for copy in copies:
+            copy.start()
         me = lax.axis_index("latent")
         first = firsts_ref[...]
         there = (dead_ref[...] >= first) & (dead_ref[...] < first + lat_dev)
@@ -33,18 +41,152 @@
         lies = jnp.where(row_ref[...] == slot, 1.0, 0.0).astype(BF16)
         take = lax.dot_general(goes, lies, (((1,), (1,)), ((), ())), preferred_element_type=F32).astype(BF16)
         rows = jnp.dot(take, pool_ref[...], preferred_element_type=F32)
-        for dest in range(owners):
-            out_ref[dest, :, :width] = tokens_ref[...]
         for piece in range(tok_dev):
-            out_ref[:, piece, width:] = rows[:, piece * part : (piece + 1) * part].astype(BF16)
-
+            buffer[:, piece, :] = rows[:, piece * part : (piece + 1) * part].astype(BF16)
+        last = pltpu.make_async_copy(buffer, out_ref.at[:, :, pl.ds(width, part)], sems.at[owners])
+        last.start()
+        for copy in copies + [last]:
+            copy.wait()
+
+    in_vmem_spec = pl.BlockSpec(memory_space=pltpu.VMEM)
     return pl.pallas_call(
         body,
         out_shape=jax.ShapeDtypeStruct((owners, tok_dev, width + part), BF16),
-        in_specs=[pl.BlockSpec(memory_space=pltpu.VMEM)] * 5,
-        out_specs=pl.BlockSpec(memory_space=pltpu.VMEM),
+        in_specs=[in_vmem_spec] * 5,
+        out_specs=pl.BlockSpec(memory_space=pl.ANY),
+        scratch_shapes=[pltpu.VMEM((owners, tok_dev, part), BF16), pltpu.SemaphoreType.DMA((owners + 1,))],
         name="outgoing",
     )(tokens, pool, dead_ids, row_ids, firsts)
+
+
+def small(shape, dtype):
+    return math.prod(shape) * jnp.dtype(dtype).itemsize <= 1 << 20
+
+
+def in_vmem(*arrays):
+    return [pltpu.with_memory_space_constraint(x, pltpu.VMEM) if small(x.shape, x.dtype) else x for x in arrays]
+
+
+def resampled(summed, unit, place, w_enc, living, lat_dev):
+    width = w_enc.shape[1]
+    pieces = 4
+    chunk = width // pieces
+
+    def body(summed_ref, unit_ref, place_ref, enc_ref, out_ref, buffer, sems):
+        first = width + lat_dev
+        norms = summed_ref[0:1, first : first + lat_dev] + summed_ref[0:1, first + 2 * lat_dev : first + 3 * lat_dev]
+        scale = 0.2 * (jnp.sum(norms, axis=1, keepdims=True) / living)
+        dead = jnp.sum(place_ref[...].astype(F32), axis=1, keepdims=True) > 0.0
+        copies = []
+        for i in range(pieces):
+            columns = slice(i * chunk, (i + 1) * chunk)
+            rows = (scale * unit_ref[:, columns]).astype(BF16)
+            placed = jnp.dot(place_ref[...], rows, preferred_element_type=F32)
+            buffer[:, columns] = jnp.where(dead, placed, enc_ref[:, columns].astype(F32)).astype(BF16)
+            copy = pltpu.make_async_copy(buffer.at[:, columns], out_ref.at[:, columns], sems.at[i])
+            copy.start()
+            copies.append(copy)
+        for copy in copies:
+            copy.wait()
+
+    return pl.pallas_call(
+        body,
+        out_shape=jax.ShapeDtypeStruct(w_enc.shape, BF16),
+        in_specs=[pl.BlockSpec(memory_space=pltpu.VMEM)] * 4,
+        out_specs=pl.BlockSpec(memory_space=pl.ANY),
+        scratch_shapes=[pltpu.VMEM(w_enc.shape, BF16), pltpu.SemaphoreType.DMA((pieces,))],
+        name="resampled",
+    )(*in_vmem(summed, unit, place, w_enc))
+
+
+def encoded(own, peer, b_enc, mask, living, w_dec, owners):
+    count, lat_dev = mask.shape
+    width = w_dec.shape[1]
+    tok_dev = count // owners
+    pieces = 4
+    chunk = width // pieces
+
+    def body(own_ref, peer_ref, bias_ref, mask_ref, living_ref, dec_ref, out_ref, buffer, sems):
+        total = own_ref[: count + 2, :] + peer_ref[: count + 2, :]
+        codes = (jnp.maximum(total[:count] + bias_ref[...], 0.0) * mask_ref[...]).astype(BF16)
+        copies = []
+
+        def send(i, columns):
+            copy = pltpu.make_async_copy(buffer.at[:, :, columns], out_ref.at[:, :, columns], sems.at[i])
+            copy.start()
+            copies.append(copy)
+
+        for i in range(pieces):
+            columns = slice(i * chunk, (i + 1) * chunk)
+            part = jnp.dot(codes, dec_ref[:, columns], preferred_element_type=F32).astype(BF16)
+            buffer[:, :, columns] = part.reshape(owners, tok_dev, chunk)
+            send(i, columns)
+        norms = jnp.sqrt(total[count : count + 2])
+        alive = jnp.broadcast_to(norms[1:2] * living_ref[...], (count, lat_dev))
+        side = jnp.concatenate([codes.astype(F32) * norms[0:1], alive], axis=1)
+        high = side.astype(BF16)
+        low = (side - high.astype(F32)).astype(BF16)
+        buffer[:, :, width:] = jnp.concatenate([high, low], axis=1).reshape(owners, tok_dev, 4 * lat_dev)
+        send(pieces, slice(width, width + 4 * lat_dev))
+        for copy in copies:
+            copy.wait()
+
+    shape = (owners, tok_dev, width + 4 * lat_dev)
+    return pl.pallas_call(
+        body,
+        out_shape=jax.ShapeDtypeStruct(shape, BF16),
+        in_specs=[pl.BlockSpec(memory_space=pltpu.VMEM)] * 6,
+        out_specs=pl.BlockSpec(memory_space=pl.ANY),
+        scratch_shapes=[pltpu.VMEM(shape, BF16), pltpu.SemaphoreType.DMA((pieces + 1,))],
+        name="encoded",
+    )(*in_vmem(own, peer, b_enc, mask, living, w_dec))
+
+
+def directions(got, b_dec, total, place, w_dec):
+    owners, tok_dev, _ = got.shape
+    lat_dev, width = w_dec.shape
+    part = width // tok_dev
+    pieces = 2
+    chunk = part // pieces
+
+    def column(row, size):
+        rows, lanes = (lax.broadcasted_iota(jnp.int32, (size, row.shape[1]), i) for i in range(2))
+        return jnp.sum(jnp.where(rows == lanes, row, 0.0), axis=1, keepdims=True)
+
+    def body(got_ref, bias_ref, total_ref, place_ref, dec_ref, out_ref, unit_ref, buffer, sems):
+        fresh_sq = column(total_ref[2:3, :], owners)
+        if owners > lat_dev:
+            fresh_sq = jnp.concatenate(
+                [column(total_ref[2 + i : 3 + i, :], lat_dev) for i in range(owners // lat_dev)], axis=0)
+        scale = lax.rsqrt(fresh_sq + EPS)
+        again = lax.rsqrt(fresh_sq / (fresh_sq + EPS) + EPS)
+        alive = lax.rsqrt(column(total_ref[0:1, :], lat_dev) + EPS)
+        dead = jnp.sum(place_ref[...].astype(F32), axis=1, keepdims=True) > 0.0
+        copies = []
+        for i in range(tok_dev * pieces):
+            columns = slice(i * chunk, (i + 1) * chunk)
+            lanes = slice(width + i % pieces * chunk, width + (i % pieces + 1) * chunk)
+            unit = (got_ref[:, i // pieces, lanes].astype(F32) - bias_ref[:, columns]) * scale
+            unit_ref[:, columns] = unit
+            placed = jnp.dot(place_ref[...], (unit * again).astype(BF16), preferred_element_type=F32)
+            buffer[:, columns] = jnp.where(dead, placed, dec_ref[:, columns].astype(F32) * alive).astype(BF16)
+            copy = pltpu.make_async_copy(buffer.at[:, columns], out_ref.at[:, columns], sems.at[i])
+            copy.start()
+            copies.append(copy)
+        for copy in copies:
+            copy.wait()
+
+    make = pltpu.VMEM if small((owners, width), F32) else jax.ShapeDtypeStruct
+    unit_shape = make((owners, width), F32)
+    return pl.pallas_call(
+        body,
+        out_shape=(jax.ShapeDtypeStruct(w_dec.shape, BF16), unit_shape),
+        in_specs=[pl.BlockSpec(memory_space=pltpu.VMEM)] * 5,
+        out_specs=(pl.BlockSpec(memory_space=pl.ANY), pl.BlockSpec(memory_space=pltpu.VMEM)),
+        scratch_shapes=[pltpu.VMEM(w_dec.shape, BF16), pltpu.SemaphoreType.DMA((tok_dev * pieces,))],
+        cost_estimate=pl.CostEstimate(flops=20 * lat_dev * width, bytes_accessed=8 * lat_dev * width, transcendentals=0),
+        name="directions",
+    )(*in_vmem(got, b_dec, total, place, w_dec))
 
 
 def local(tokens, b_dec, w_enc, b_enc, w_dec, bias_moments, pool, active_blocks, dead_ids, row_ids):
@@ -88,39 +230,23 @@
     tail = jnp.concatenate([jnp.sum(fresh * fresh, axis=(1, 2)), input_part])
     tail = jnp.pad(tail, (0, -tail.shape[0] % lat_dev)).reshape(-1, lat_dev)
     message = jnp.concatenate([partial_pre, dec_part[None], enc_part[None], tail], axis=0)
-    total = message + swap(message)
-    pre = total[:count] + b_enc[None, :]
-    dec_sq, enc_sq = total[count], total[count + 1]
-    tail = total[count + 2 :].reshape(-1)
-    fresh_sq, input_sum = tail[:owners], tail[owners : owners + tok_dev]
-
-    codes = lax.reduce_precision(jnp.maximum(pre, 0.0) * mask, 8, 7)
-    norms = jnp.where(is_dead, 0.0, jnp.sqrt(enc_sq))
-    side = jnp.concatenate(
-        [codes * jnp.sqrt(dec_sq)[None, :], jnp.broadcast_to(norms[None, :], (count, lat_dev))], axis=1)
-    high = lax.reduce_precision(side, 8, 7)
-    rebuilt = jnp.dot(codes.astype(BF16), w_dec, preferred_element_type=F32)
-    sent = jnp.concatenate([rebuilt.astype(BF16), high.astype(BF16), (side - high).astype(BF16)], axis=1)
-    summed = lax.all_to_all(sent.reshape(owners, tok_dev, -1), "latent", 0, 0, axis_index_groups=[order])
-
-    unit = fresh * lax.rsqrt(fresh_sq + EPS)[:, None, None]
-    unit_sq = fresh_sq / (fresh_sq + EPS)
-    dec_rows = (unit * lax.rsqrt(unit_sq + EPS)[:, None, None]).astype(BF16).reshape(owners, width)
-    placed_dec = jnp.dot(place, dec_rows, preferred_element_type=F32)
-    new_dec = jnp.where(is_dead[:, None], placed_dec, dec_wide * lax.rsqrt(dec_sq + EPS)[:, None]).astype(BF16)
+    peer = swap(message)
+    sent = encoded(message, peer, b_enc[None], mask, keep[None], w_dec, owners)
+    summed = lax.all_to_all(sent, "latent", 0, 0, axis_index_groups=[order])
+
+    total = message[count:] + peer[count:]
+    input_sum = total[2:].reshape(-1)[owners : owners + tok_dev]
+    new_dec, unit = directions(got, b_dec[None], total, place, w_dec)
     summed, new_dec, unit = lax.optimization_barrier((summed, new_dec, unit))
 
     summed = jnp.sum(summed.astype(F32), axis=0)
     residual = own_centered - summed[:, :width]
     error_part = jnp.sum(jnp.square(residual).reshape(tok_dev, -1, 128), axis=1)
     error_peer = swap(error_part)
-    side = summed[:, width : width + 2 * lat_dev] + summed[:, width + 2 * lat_dev :]
-    alive_mean = jnp.sum(side[:, lat_dev:], axis=1) / (latents - dead)
-    enc_rows = ((0.2 * alive_mean)[None, :, None] * unit).astype(BF16).reshape(owners, width)
-    placed_enc = jnp.dot(place, enc_rows, preferred_element_type=F32).astype(BF16)
-    new_enc = jnp.where(is_dead[:, None], placed_enc, w_enc)
+    new_enc = resampled(summed, unit, place, w_enc, latents - dead, lat_dev)
     error_peer, new_enc = lax.optimization_barrier((error_peer, new_enc))
-    penalty = jnp.sum(side[:, :lat_dev], axis=1)
+    side = summed[:, width : width + lat_dev] + summed[:, width + 2 * lat_dev : width + 3 * lat_dev]
+    penalty = jnp.sum(side, axis=1)
     error_sum = jnp.sum(error_part + error_peer, axis=1)
     full = width * lax.axis_size("hidden")
     losses = error_sum / full / (input_sum / full + EPS) + 5.0 * penalty / latents

time: 32.3 us -> 31.7 us (0.981)
  Pallas kernels: 1.97 us -> 5.48 us
  matrix products: 3.77 us -> 0.63 us
  waiting for transfers between devices: 5.48 us -> 4.28 us
    pallas_call x0 -> x3, Pallas kernels: none -> 3.49 us  [the longest x1 1.29 us: directions(): pl.pallas_call(body, out_shape=(jax.ShapeDtypeStruct(w_dec.shape, BF16),...]
    dot_general x3 -> x0, matrix products: 3.21 us -> none  [the longest x1 1.45 us: local(): placed_dec = jnp.dot(place, dec_rows, preferred_element_type=F32)]
    reduce_sum x1, other arithmetic: 1.54 us -> 0.28 us  [local(): enc_part = jnp.sum(jnp.square(w_enc.astype(F32)), axis=1)]
    reduce_sum x1, other arithmetic: 0.28 us -> 1.53 us  [local(): dec_part = jnp.sum(dec_wide * dec_wide, axis=1)]
    reshape x1 -> x0, local copies, waits for them, and re-layouts: 0.72 us -> none  [local(): sent.reshape(owners, tok_dev, -1)]
    reduce_or x1, other arithmetic: 0.09 us -> 0.77 us  [local(): jnp.any(active_blocks[:, :, None] == my_block[None, None, :], axis=1)]
    broadcast_in_dim x1, local copies, waits for them, and re-layouts: 0.07 us -> 0.73 us  [local(): row_tile = jnp.repeat(everyone, tok_dev) // (owners // tiles)]
    ppermute x2, waiting for transfers between devices: 1.15 us -> 0.64 us  [swap(): return lax.ppermute(x, 'hidden', [(0, 1), (1, 0)])]
  transfers between devices with their start and end apart: 4 -> 4, of which waited for: 3 -> 3; matrix products, arithmetic and copies ran while one was open for 24% -> 19% of each run, Pallas kernels for 0% -> 8%
where the time goes in v4:
time: 31.7 us; the launch traced here: 31.3 us
  starting transfers between devices  13 us (41%)
  other arithmetic  6.1 us (19%)
  Pallas kernels  5.48 us (17%)
  waiting for transfers between devices  4.28 us (14%)
  local copies, waits for them, and re-layouts  0.93 us (3%)
  between operations  0.84 us (3%)
  matrix products  0.63 us (2%)
    all_to_all x1, starting transfers between devices, local(): got = lax.all_to_all(sent, 'latent', 0, 0, axis_index_groups=[order])  7.83 us
    all_to_all x1, starting transfers between devices, local(): summed = lax.all_to_all(sent, 'latent', 0, 0, axis_index_groups=[order])  5.04 us
    all_to_all x1, waiting for transfers between devices, local(): summed = lax.all_to_all(sent, 'latent', 0, 0, axis_index_groups=[order])  3 us
    pallas_call x1, Pallas kernels, outgoing(): pl.pallas_call(body, out_shape=jax.ShapeDtypeStruct((owners, tok_dev, wid...  2 us
    reduce_sum x1, other arithmetic, local(): dec_part = jnp.sum(dec_wide * dec_wide, axis=1)  1.53 us
    pallas_call x1, Pallas kernels, directions(): pl.pallas_call(body, out_shape=(jax.ShapeDtypeStruct(w_dec.shape, BF16),...  1.29 us
    pallas_call x1, Pallas kernels, resampled(): pl.pallas_call(body, out_shape=jax.ShapeDtypeStruct(w_enc.shape, BF16), i...  1.27 us
    pallas_call x1, Pallas kernels, encoded(): pl.pallas_call(body, out_shape=jax.ShapeDtypeStruct(shape, BF16), in_spec...  0.92 us
  transfers between devices with their start and end apart: 4, of which 3 were waited for; matrix products, arithmetic and copies ran while one was open for 19% of the time, Pallas kernels for 8%

profile of v4, /device:TPU:0, one launch (start us, length us, event | category | flops | bytes accessed | tf_op | source)
XLA Modules:
  0.0 31.3 jit_solution(16010709107880952229)
XLA Ops:
  0.6 0.0 copy-start.1
  0.6 2.0 %outgoing.1 = bf16[8,2,6144]{2,1,0:T(2,128)(2,1)} custom-call(bf16[2,4096]{1,0:T(2,128)(2,1)} %tokens_ref.1, bf16[8,4096]{1,0:T(8,128)(2,1)} %pool_ref.1, s32[1,32]{1,0:T(1,128)} %bitcast.35, s32[1,32]{1,0:T(1,128)} %bitcast.34, s32[8,1]{1,0:T(8,128)} %constant.82.firsts_ref), custom_call_target="tpu_custom_call" | custom-call | tf_op jit(solution)/shard_map/outgoing/pallas_call | solution.py:52
  2.6 7.8 %all-to-all-start = ((bf16[8,2,6144]{2,1,0:T(2,128)(2,1)}), bf16[8,2,6144]{2,1,0:T(2,128)(2,1)S(1)}, u32[]{:S(2)}, u32[]{:S(2)}) async-start(bf16[8,2,6144]{2,1,0:T(2,128)(2,1)} %outgoing.1), calls=%async_computation | async-start | bytes 393216 | tf_op jit(solution)/shard_map/all_to_all | solution.py:205
  10.5 0.7 %and_select_fusion = s32[32]{0:T(128)S(1)} fusion(s32[32]{0:T(128)} %param.20), kind=kLoop, calls=%fused_computation.23 | loop fusion | flops 480 | bytes 256 | tf_op jit(solution)/shard_map/jit(floor_divide)/jit(_where)/select_n | solution.py:201
  11.2 0.8 %compare_reduce_fusion = pred[4,128]{1,0:T(4,128)(4,1)S(1)} fusion(s32[128]{0:T(128)S(1)} %and_select_fusion.1, s32[4,16]{1,0:T(4,128)} %param.18), kind=kLoop, calls=%fused_computation.12 | loop fusion | flops 15872 | bytes 1280 | tf_op jit(solution)/shard_map/reduce_or | solution.py:218
  12.0 0.7 %broadcast_in_dim.106 = s32[8,2]{1,0:T(8,128)S(1)} broadcast(s32[8]{0:T(128)} %constant.76.clone), dimensions={0} | broadcast | bytes 96 | tf_op jit(solution)/shard_map/broadcast_in_dim | solution.py:216
  12.7 0.1 reshape.134
  12.8 0.0 copy-start.6
  12.8 0.0 copy-start.2
  12.8 0.0 copy-start.4
  12.8 0.0 copy-start.7
  12.8 1.5 %multiply_reduce_fusion.1 = f32[128]{0:T(128)S(1)} fusion(bf16[128,4096]{1,0:T(8,128)(2,1)} %dec_ref.3), kind=kLoop, calls=%fused_computation.1 | loop fusion | flops 1572736 | bytes 1049088 | tf_op jit(solution)/shard_map/reduce_sum | solution.py:223
  14.4 0.0 copy-done.1
  14.4 0.3 multiply_reduce_fusion
  14.7 0.0 copy-start.3
  14.7 0.0 copy-start
  14.7 0.1 select_select_fusion.mask_ref
  14.8 0.0 copy-done.6
  14.8 0.1 compare_reduce_fusion.1
  14.9 0.0 copy-done.2
  14.9 0.0 copy-done.4
  14.9 0.1 multiply_reduce_fusion.3
  15.1 0.0 copy-done.7
  15.1 0.3 convolution_convert_fusion.place_ref
  15.3 0.6 %all-to-all-done.got_ref = bf16[8,2,6144]{2,1,0:T(2,128)(2,1)S(1)} async-done(((bf16[8,2,6144]{2,1,0:T(2,128)(2,1)}), bf16[8,2,6144]{2,1,0:T(2,128)(2,1)S(1)}, u32[]{:S(2)}, u32[]{:S(2)}) %all-to-all-start) | async-done | bytes 196640 | tf_op jit(solution)/shard_map/all_to_all | solution.py:205
  15.9 0.1 subtract_convert_fusion
  16.1 0.1 reshape.132
  16.1 0.4 %fusion.13 = f32[16,128]{1,0:T(8,128)S(1)} fusion(bf16[16,4096]{1,0:T(8,128)(2,1)S(1)} %reshape.132, bf16[128,4096]{1,0:T(8,128)(2,1)S(1)} %copy-done.1), kind=kOutput, calls=%fused_computation.57 | convolution fusion | flops 16777216 | bytes 1187840 | tf_op jit(solution)/shard_map/dot_general | solution.py:228
  16.5 0.2 multiply_reduce_fusion.2
  16.7 0.1 fusion.10
  16.8 0.1 collective-permute-start
  16.9 0.0 copy-done.3
  16.9 0.5 %broadcast_select_fusion = (f32[128]{0:T(128)S(1)}, f32[1,128]{1,0:T(1,128)S(1)}, f32[128]{0:T(128)}) fusion(pred[128]{0:T(512)(128)(4,1)S(1)} %compare_reduce_fusion.1, f32[128]{0:T(128)S(1)} %copy-done.3), kind=kLoop, calls=%fused_computation.50 | loop fusion | flops 256 | bytes 2176 | tf_op jit(solution)/shard_map/jit(_where)/select_n | solution.py:213
  17.4 0.6 %collective-permute-done.peer_ref = f32[19,128]{1,0:T(8,128)S(1)} collective-permute-done((f32[19,128]{1,0:T(8,128)S(1)}, f32[19,128]{1,0:T(8,128)S(1)}, u32[]{:S(2)}, u32[]{:S(2)}) %collective-permute-start) | collective-permute-done | bytes 9760 | tf_op jit(solution)/shard_map/ppermute | solution.py:16
  18.0 0.0 copy-done
  18.0 0.9 %encoded.1 = bf16[8,2,4608]{2,1,0:T(2,128)(2,1)} custom-call(f32[19,128]{1,0:T(8,128)S(1)} %pad_maximum_fusion.own_ref, f32[19,128]{1,0:T(8,128)S(1)} %collective-permute-done.peer_ref, f32[1,128]{1,0:T(1,128)S(1)} %bitcast.29, f32[16,128]{1,0:T(8,128)S(1)} %select_select_fusion.mask_ref, f32[1,128]{1,0:T(1,128)S(1)} %get-tuple-element.26.living_ref, ...), custom_call_target="tpu_custom_call" | custom-call | tf_op jit(solution)/shard_map/encoded/pallas_call | solution.py:135
  19.0 5.0 %all-to-all-start.1 = ((bf16[8,2,4608]{2,1,0:T(2,128)(2,1)}), bf16[8,2,4608]{2,1,0:T(2,128)(2,1)S(1)}, u32[]{:S(2)}, u32[]{:S(2)}) async-start(bf16[8,2,4608]{2,1,0:T(2,128)(2,1)} %encoded.1), calls=%async_computation.1 | async-start | bytes 294912 | tf_op jit(solution)/shard_map/all_to_all | solution.py:235
  24.0 0.0 copy-done.5
  24.0 0.6 %broadcast_multiply_fusion = f32[2,128]{1,0:T(2,128)} fusion(f32[2,128]{1,0:T(2,128)S(1)} %copy-done.5, f32[128]{0:T(128)S(1)} %get-tuple-element.25), kind=kLoop, calls=%fused_computation.43 | loop fusion | flops 256 | bytes 2560 | tf_op jit(solution)/shard_map/mul | solution.py:215
  24.6 1.3 %directions.1 = (bf16[128,4096]{1,0:T(8,128)(2,1)}, f32[8,4096]{1,0:T(8,128)S(1)}) custom-call(bf16[8,2,6144]{2,1,0:T(2,128)(2,1)S(1)} %all-to-all-done.got_ref, f32[1,4096]{1,0:T(1,128)S(1)} %bitcast.28, f32[3,128]{1,0:T(4,128)S(1)} %slice_add_fusion.total_ref, bf16[128,8]{1,0:T(8,128)(2,1)S(1)} %convolution_convert_fusion.place_ref, ...), custom_call_target="tpu_custom_call" | custom-call | flops 10485760 | bytes 4194304 | tf_op jit(solution)/shard_map/directions/pallas_call | solution.py:181
  25.9 3.0 %all-to-all-done.1 = bf16[8,2,4608]{2,1,0:T(2,128)(2,1)S(1)} async-done(((bf16[8,2,4608]{2,1,0:T(2,128)(2,1)}), bf16[8,2,4608]{2,1,0:T(2,128)(2,1)S(1)}, u32[]{:S(2)}, u32[]{:S(2)}) %all-to-all-start.1) | async-done | bytes 147488 | tf_op jit(solution)/shard_map/all_to_all | solution.py:235
  28.9 0.1 convert_reduce_fusion.summed_ref
  29.1 0.1 collective-permute-start.1
  29.1 0.1 fusion.7
  29.3 1.3 %resampled.1 = bf16[128,4096]{1,0:T(8,128)(2,1)} custom-call(f32[2,4608]{1,0:T(2,128)S(1)} %convert_reduce_fusion.summed_ref, f32[8,4096]{1,0:T(8,128)S(1)} %get-tuple-element.15.unit_ref, bf16[128,8]{1,0:T(8,128)(2,1)S(1)} %convolution_convert_fusion.place_ref, bf16[128,4096]{1,0:T(8,128)(2,1)S(1)} %copy-done.1), custom_call_target="tpu_custom_call" | custom-call | tf_op jit(solution)/shard_map/resampled/pallas_call | solution.py:92
  30.5 0.0 collective-permute-done.1
  30.6 0.1 add_reduce_fusion
  30.7 0.6 %fusion.9 = f32[2]{0:T(128)} fusion(f32[2]{0:T(128)S(1)} %fusion.7, f32[3,128]{1,0:T(4,128)S(1)} %slice_add_fusion.total_ref, f32[2]{0:T(128)S(1)} %add_reduce_fusion), kind=kLoop, calls=%fused_computation.42 | loop fusion | flops 12 | bytes 32 | tf_op jit(solution)/shard_map/add | solution.py:252
  (12 shorter events, 0.1 us)
Async XLA Ops:
  0.6 13.8 %copy-start.1 = (bf16[128,4096]{1,0:T(8,128)(2,1)S(1)}, bf16[128,4096]{1,0:T(8,128)(2,1)}, u32[]{:S(2)}) copy-start(bf16[128,4096]{1,0:T(8,128)(2,1)} %enc_ref.1) | copy-start | bytes 3145732
  2.6 13.3 %all-to-all-start = ((bf16[8,2,6144]{2,1,0:T(2,128)(2,1)}), bf16[8,2,6144]{2,1,0:T(2,128)(2,1)S(1)}, u32[]{:S(2)}, u32[]{:S(2)}) async-start(bf16[8,2,6144]{2,1,0:T(2,128)(2,1)} %outgoing.1), calls=%async_computation | async-start | bytes 393216 | tf_op jit(solution)/shard_map/all_to_all | solution.py:205
  12.8 2.0 %copy-start.6 = (s32[32]{0:T(128)S(1)}, s32[32]{0:T(128)}, u32[]{:S(2)}) copy-start(s32[32]{0:T(128)} %param.19) | copy-start | bytes 388
  12.8 2.1 %copy-start.2 = (f32[4096]{0:T(1024)S(1)}, f32[4096]{0:T(1024)}, u32[]{:S(2)}) copy-start(f32[4096]{0:T(1024)} %param.12) | copy-start | bytes 49156
  12.8 2.1 %copy-start.4 = (bf16[2,4096]{1,0:T(2,128)(2,1)S(1)}, bf16[2,4096]{1,0:T(2,128)(2,1)}, u32[]{:S(2)}) copy-start(bf16[2,4096]{1,0:T(2,128)(2,1)} %tokens_ref.1) | copy-start | bytes 49156
  12.8 2.2 %copy-start.7 = (s32[8]{0:T(128)S(1)}, s32[8]{0:T(128)}, u32[]{:S(2)}) copy-start(s32[8]{0:T(128)} %constant.76.clone) | copy-start | bytes 100
  14.7 2.2 %copy-start.3 = (f32[128]{0:T(128)S(1)}, f32[128]{0:T(128)}, u32[]{:S(2)}) copy-start(f32[128]{0:T(128)} %param.14) | copy-start | bytes 1540
  14.7 3.4 %copy-start = (bf16[128,4096]{1,0:T(8,128)(2,1)S(1)}, bf16[128,4096]{1,0:T(8,128)(2,1)}, u32[]{:S(2)}) copy-start(bf16[128,4096]{1,0:T(8,128)(2,1)} %dec_ref.3) | copy-start | bytes 3145732
  16.5 7.5 %copy-start.5 = (f32[2,128]{1,0:T(2,128)S(1)}, f32[2,128]{1,0:T(2,128)}, u32[]{:S(2)}) copy-start(f32[2,128]{1,0:T(2,128)} %param.16) | copy-start | bytes 3076
  16.8 1.2 %collective-permute-start = (f32[19,128]{1,0:T(8,128)S(1)}, f32[19,128]{1,0:T(8,128)S(1)}, u32[]{:S(2)}, u32[]{:S(2)}) collective-permute-start(f32[19,128]{1,0:T(8,128)S(1)} %pad_maximum_fusion.own_ref), channel_id=1, source_target_pairs={{0,1},{1,0},{2,3},{3,2},{4,5},{5,4},{6,7},{7,6},{8,9},{9,8},{10,11... | collective-permute-start | bytes 29192 | tf_op jit(solution)/shard_map/ppermute | solution.py:16
  19.0 9.9 %all-to-all-start.1 = ((bf16[8,2,4608]{2,1,0:T(2,128)(2,1)}), bf16[8,2,4608]{2,1,0:T(2,128)(2,1)S(1)}, u32[]{:S(2)}, u32[]{:S(2)}) async-start(bf16[8,2,4608]{2,1,0:T(2,128)(2,1)} %encoded.1), calls=%async_computation.1 | async-start | bytes 294912 | tf_op jit(solution)/shard_map/all_to_all | solution.py:235
  29.1 1.5 %collective-permute-start.1 = (f32[2,128]{1,0:T(2,128)S(1)}, f32[2,128]{1,0:T(2,128)S(1)}, u32[]{:S(2)}, u32[]{:S(2)}) collective-permute-start(f32[2,128]{1,0:T(2,128)S(1)} %bitcast_reduce_fusion), channel_id=1, source_target_pairs={{0,1},{1,0},{2,3},{3,2},{4,5},{5,4},{6,7},{7,6},{8,9},{9,8},{10,11... | collective-permute-start | bytes 3080 | tf_op jit(solution)/shard_map/ppermute | solution.py:16

commit v5 on v4

--- a/solution.py
+++ b/solution.py
@@ -67,38 +67,6 @@
     return [pltpu.with_memory_space_constraint(x, pltpu.VMEM) if small(x.shape, x.dtype) else x for x in arrays]
 
 
-def resampled(summed, unit, place, w_enc, living, lat_dev):
-    width = w_enc.shape[1]
-    pieces = 4
-    chunk = width // pieces
-
-    def body(summed_ref, unit_ref, place_ref, enc_ref, out_ref, buffer, sems):
-        first = width + lat_dev
-        norms = summed_ref[0:1, first : first + lat_dev] + summed_ref[0:1, first + 2 * lat_dev : first + 3 * lat_dev]
-        scale = 0.2 * (jnp.sum(norms, axis=1, keepdims=True) / living)
-        dead = jnp.sum(place_ref[...].astype(F32), axis=1, keepdims=True) > 0.0
-        copies = []
-        for i in range(pieces):
-            columns = slice(i * chunk, (i + 1) * chunk)
-            rows = (scale * unit_ref[:, columns]).astype(BF16)
-            placed = jnp.dot(place_ref[...], rows, preferred_element_type=F32)
-            buffer[:, columns] = jnp.where(dead, placed, enc_ref[:, columns].astype(F32)).astype(BF16)
-            copy = pltpu.make_async_copy(buffer.at[:, columns], out_ref.at[:, columns], sems.at[i])
-            copy.start()
-            copies.append(copy)
-        for copy in copies:
-            copy.wait()
-
-    return pl.pallas_call(
-        body,
-        out_shape=jax.ShapeDtypeStruct(w_enc.shape, BF16),
-        in_specs=[pl.BlockSpec(memory_space=pltpu.VMEM)] * 4,
-        out_specs=pl.BlockSpec(memory_space=pl.ANY),
-        scratch_shapes=[pltpu.VMEM(w_enc.shape, BF16), pltpu.SemaphoreType.DMA((pieces,))],
-        name="resampled",
-    )(*in_vmem(summed, unit, place, w_enc))
-
-
 def encoded(own, peer, b_enc, mask, living, w_dec, owners):
     count, lat_dev = mask.shape
     width = w_dec.shape[1]
@@ -106,87 +74,83 @@
     pieces = 4
     chunk = width // pieces
 
-    def body(own_ref, peer_ref, bias_ref, mask_ref, living_ref, dec_ref, out_ref, buffer, sems):
+    def body(own_ref, peer_ref, bias_ref, mask_ref, living_ref, dec_ref, out_ref):
         total = own_ref[: count + 2, :] + peer_ref[: count + 2, :]
         codes = (jnp.maximum(total[:count] + bias_ref[...], 0.0) * mask_ref[...]).astype(BF16)
-        copies = []
-
-        def send(i, columns):
-            copy = pltpu.make_async_copy(buffer.at[:, :, columns], out_ref.at[:, :, columns], sems.at[i])
-            copy.start()
-            copies.append(copy)
-
         for i in range(pieces):
             columns = slice(i * chunk, (i + 1) * chunk)
             part = jnp.dot(codes, dec_ref[:, columns], preferred_element_type=F32).astype(BF16)
-            buffer[:, :, columns] = part.reshape(owners, tok_dev, chunk)
-            send(i, columns)
+            out_ref[:, :, columns] = part.reshape(owners, tok_dev, chunk)
         norms = jnp.sqrt(total[count : count + 2])
         alive = jnp.broadcast_to(norms[1:2] * living_ref[...], (count, lat_dev))
         side = jnp.concatenate([codes.astype(F32) * norms[0:1], alive], axis=1)
         high = side.astype(BF16)
         low = (side - high.astype(F32)).astype(BF16)
-        buffer[:, :, width:] = jnp.concatenate([high, low], axis=1).reshape(owners, tok_dev, 4 * lat_dev)
-        send(pieces, slice(width, width + 4 * lat_dev))
-        for copy in copies:
-            copy.wait()
+        out_ref[:, :, width:] = jnp.concatenate([high, low], axis=1).reshape(owners, tok_dev, 4 * lat_dev)
 
     shape = (owners, tok_dev, width + 4 * lat_dev)
     return pl.pallas_call(
         body,
-        out_shape=jax.ShapeDtypeStruct(shape, BF16),
+        out_shape=(pltpu.VMEM if small(shape, BF16) else jax.ShapeDtypeStruct)(shape, BF16),
         in_specs=[pl.BlockSpec(memory_space=pltpu.VMEM)] * 6,
-        out_specs=pl.BlockSpec(memory_space=pl.ANY),
-        scratch_shapes=[pltpu.VMEM(shape, BF16), pltpu.SemaphoreType.DMA((pieces + 1,))],
+        out_specs=pl.BlockSpec(memory_space=pltpu.VMEM),
         name="encoded",
     )(*in_vmem(own, peer, b_enc, mask, living, w_dec))
 
 
-def directions(got, b_dec, total, place, w_dec):
+def finished(summed, got, b_dec, total, place, w_enc, w_dec, living):
     owners, tok_dev, _ = got.shape
     lat_dev, width = w_dec.shape
     part = width // tok_dev
     pieces = 2
     chunk = part // pieces
+    steps = tok_dev * pieces
 
     def column(row, size):
         rows, lanes = (lax.broadcasted_iota(jnp.int32, (size, row.shape[1]), i) for i in range(2))
         return jnp.sum(jnp.where(rows == lanes, row, 0.0), axis=1, keepdims=True)
 
-    def body(got_ref, bias_ref, total_ref, place_ref, dec_ref, out_ref, unit_ref, buffer, sems):
-        fresh_sq = column(total_ref[2:3, :], owners)
-        if owners > lat_dev:
-            fresh_sq = jnp.concatenate(
-                [column(total_ref[2 + i : 3 + i, :], lat_dev) for i in range(owners // lat_dev)], axis=0)
+    def body(summed_ref, got_ref, bias_ref, total_ref, place_ref, enc_ref, dec_ref, new_enc_ref, new_dec_ref,
+             enc_buffer, dec_buffer, sems):
+        first = width + lat_dev
+        norms = summed_ref[0:1, first : first + lat_dev] + summed_ref[0:1, first + 2 * lat_dev : first + 3 * lat_dev]
+        level = 0.2 * (jnp.sum(norms, axis=1, keepdims=True) / living)
+        lanes = min(owners, lat_dev)
+        fresh_sq = jnp.concatenate(
+            [column(total_ref[2 + i : 3 + i, :], lanes) for i in range(owners // lanes)], axis=0)
         scale = lax.rsqrt(fresh_sq + EPS)
         again = lax.rsqrt(fresh_sq / (fresh_sq + EPS) + EPS)
         alive = lax.rsqrt(column(total_ref[0:1, :], lat_dev) + EPS)
         dead = jnp.sum(place_ref[...].astype(F32), axis=1, keepdims=True) > 0.0
         copies = []
-        for i in range(tok_dev * pieces):
-            columns = slice(i * chunk, (i + 1) * chunk)
-            lanes = slice(width + i % pieces * chunk, width + (i % pieces + 1) * chunk)
-            unit = (got_ref[:, i // pieces, lanes].astype(F32) - bias_ref[:, columns]) * scale
-            unit_ref[:, columns] = unit
-            placed = jnp.dot(place_ref[...], (unit * again).astype(BF16), preferred_element_type=F32)
-            buffer[:, columns] = jnp.where(dead, placed, dec_ref[:, columns].astype(F32) * alive).astype(BF16)
-            copy = pltpu.make_async_copy(buffer.at[:, columns], out_ref.at[:, columns], sems.at[i])
+
+        def send(buffer, out_ref, columns):
+            copy = pltpu.make_async_copy(buffer.at[:, columns], out_ref.at[:, columns], sems.at[len(copies)])
             copy.start()
             copies.append(copy)
+
+        for i in range(steps):
+            columns = slice(i * chunk, (i + 1) * chunk)
+            lane = width + i % pieces * chunk
+            unit = (got_ref[:, i // pieces, lane : lane + chunk].astype(F32) - bias_ref[:, columns]) * scale
+            placed = jnp.dot(place_ref[...], (level * unit).astype(BF16), preferred_element_type=F32)
+            enc_buffer[:, columns] = jnp.where(dead, placed, enc_ref[:, columns].astype(F32)).astype(BF16)
+            send(enc_buffer, new_enc_ref, columns)
+            placed = jnp.dot(place_ref[...], (unit * again).astype(BF16), preferred_element_type=F32)
+            dec_buffer[:, columns] = jnp.where(dead, placed, dec_ref[:, columns].astype(F32) * alive).astype(BF16)
+            send(dec_buffer, new_dec_ref, columns)
         for copy in copies:
             copy.wait()
 
-    make = pltpu.VMEM if small((owners, width), F32) else jax.ShapeDtypeStruct
-    unit_shape = make((owners, width), F32)
+    like = jax.ShapeDtypeStruct(w_dec.shape, BF16)
     return pl.pallas_call(
         body,
-        out_shape=(jax.ShapeDtypeStruct(w_dec.shape, BF16), unit_shape),
-        in_specs=[pl.BlockSpec(memory_space=pltpu.VMEM)] * 5,
-        out_specs=(pl.BlockSpec(memory_space=pl.ANY), pl.BlockSpec(memory_space=pltpu.VMEM)),
-        scratch_shapes=[pltpu.VMEM(w_dec.shape, BF16), pltpu.SemaphoreType.DMA((tok_dev * pieces,))],
-        cost_estimate=pl.CostEstimate(flops=20 * lat_dev * width, bytes_accessed=8 * lat_dev * width, transcendentals=0),
-        name="directions",
-    )(*in_vmem(got, b_dec, total, place, w_dec))
+        out_shape=(like, like),
+        in_specs=[pl.BlockSpec(memory_space=pltpu.VMEM)] * 7,
+        out_specs=[pl.BlockSpec(memory_space=pl.ANY)] * 2,
+        scratch_shapes=[pltpu.VMEM(w_dec.shape, BF16)] * 2 + [pltpu.SemaphoreType.DMA((2 * steps,))],
+        name="finished",
+    )(*in_vmem(summed, got, b_dec, total, place, w_enc, w_dec))
 
 
 def local(tokens, b_dec, w_enc, b_enc, w_dec, bias_moments, pool, active_blocks, dead_ids, row_ids):
@@ -230,21 +194,18 @@
     tail = jnp.concatenate([jnp.sum(fresh * fresh, axis=(1, 2)), input_part])
     tail = jnp.pad(tail, (0, -tail.shape[0] % lat_dev)).reshape(-1, lat_dev)
     message = jnp.concatenate([partial_pre, dec_part[None], enc_part[None], tail], axis=0)
-    peer = swap(message)
+    peer, new_b_enc, new_moments, place = lax.optimization_barrier((swap(message), new_b_enc, new_moments, place))
     sent = encoded(message, peer, b_enc[None], mask, keep[None], w_dec, owners)
     summed = lax.all_to_all(sent, "latent", 0, 0, axis_index_groups=[order])
-
+    summed, got, message, peer = lax.optimization_barrier((summed, got, message, peer))
     total = message[count:] + peer[count:]
     input_sum = total[2:].reshape(-1)[owners : owners + tok_dev]
-    new_dec, unit = directions(got, b_dec[None], total, place, w_dec)
-    summed, new_dec, unit = lax.optimization_barrier((summed, new_dec, unit))
-
     summed = jnp.sum(summed.astype(F32), axis=0)
     residual = own_centered - summed[:, :width]
     error_part = jnp.sum(jnp.square(residual).reshape(tok_dev, -1, 128), axis=1)
     error_peer = swap(error_part)
-    new_enc = resampled(summed, unit, place, w_enc, latents - dead, lat_dev)
-    error_peer, new_enc = lax.optimization_barrier((error_peer, new_enc))
+    new_enc, new_dec = finished(summed, got, b_dec[None], total, place, w_enc, w_dec, latents - dead)
+    error_peer, new_enc, new_dec = lax.optimization_barrier((error_peer, new_enc, new_dec))
     side = summed[:, width : width + lat_dev] + summed[:, width + 2 * lat_dev : width + 3 * lat_dev]
     penalty = jnp.sum(side, axis=1)
     error_sum = jnp.sum(error_part + error_peer, axis=1)

time: 31.7 us -> 30.9 us (0.975)
  blocking collectives: 0 us -> 9.41 us
  starting transfers between devices: 13 us -> 7.96 us
  waiting for transfers between devices: 4.28 us -> 0.72 us
  Pallas kernels: 5.48 us -> 3.91 us
    all_to_all x0 -> x1, blocking collectives: none -> 9.41 us  [local(): summed = lax.all_to_all(sent, 'latent', 0, 0, axis_index_groups=[order])]
    all_to_all x1 -> x0, starting transfers between devices: 5.04 us -> none  [local(): summed = lax.all_to_all(sent, 'latent', 0, 0, axis_index_groups=[order])]
    all_to_all x1 -> x0, waiting for transfers between devices: 3 us -> none  [local(): summed = lax.all_to_all(sent, 'latent', 0, 0, axis_index_groups=[order])]
    pallas_call x3 -> x2, Pallas kernels: 3.49 us -> 1.91 us  [the longest x1 1.66 us: finished(): pl.pallas_call(body, out_shape=(like, like), in_specs=[pl.BlockSpec(memor...]
    all_to_all x1, waiting for transfers between devices: 0.63 us -> 0.13 us  [local(): got = lax.all_to_all(sent, 'latent', 0, 0, axis_index_groups=[order])]
  transfers between devices with their start and end apart: 4 -> 3, of which waited for: 3 -> 2; matrix products, arithmetic and copies ran while one was open for 19% -> 19% of each run, Pallas kernels for 8% -> 5%
where the time goes in v5:
time: 30.9 us; the launch traced here: 30.5 us
  blocking collectives  9.41 us (30%)
  starting transfers between devices  7.96 us (26%)
  other arithmetic  6.09 us (20%)
  Pallas kernels  3.91 us (13%)
  local copies, waits for them, and re-layouts  0.93 us (3%)
  between operations  0.85 us (3%)
  waiting for transfers between devices  0.72 us (2%)
  matrix products  0.63 us (2%)
    all_to_all x1, blocking collectives, local(): summed = lax.all_to_all(sent, 'latent', 0, 0, axis_index_groups=[order])  9.41 us
    all_to_all x1, starting transfers between devices, local(): got = lax.all_to_all(sent, 'latent', 0, 0, axis_index_groups=[order])  7.83 us
    pallas_call x1, Pallas kernels, outgoing(): pl.pallas_call(body, out_shape=jax.ShapeDtypeStruct((owners, tok_dev, wid...  2 us
    pallas_call x1, Pallas kernels, finished(): pl.pallas_call(body, out_shape=(like, like), in_specs=[pl.BlockSpec(memor...  1.66 us
    reduce_sum x1, other arithmetic, local(): dec_part = jnp.sum(dec_wide * dec_wide, axis=1)  1.53 us
    reduce_or x1, other arithmetic, local(): jnp.any(active_blocks[:, :, None] == my_block[None, None, :], axis=1)  0.77 us
    broadcast_in_dim x1, local copies, waits for them, and re-layouts, local(): row_tile = jnp.repeat(everyone, tok_dev) // (owners // tiles)  0.73 us
    select_n x1, other arithmetic, local(): holder_of = row_ids // pool_dev  0.67 us
  transfers between devices with their start and end apart: 3, of which 2 were waited for; matrix products, arithmetic and copies ran while one was open for 19% of the time, Pallas kernels for 5%

profile of v5, /device:TPU:0, one launch (start us, length us, event | category | flops | bytes accessed | tf_op | source)
XLA Modules:
  0.0 30.5 jit_solution(6808145193998291024)
XLA Ops:
  0.6 0.0 copy-start.6
  0.6 0.0 copy-start.3
  0.7 0.0 copy-start
  0.7 2.0 %outgoing.1 = bf16[8,2,6144]{2,1,0:T(2,128)(2,1)} custom-call(bf16[2,4096]{1,0:T(2,128)(2,1)} %tokens_ref.1, bf16[8,4096]{1,0:T(8,128)(2,1)} %pool_ref.1, s32[1,32]{1,0:T(1,128)} %bitcast.33, s32[1,32]{1,0:T(1,128)} %bitcast.32, s32[8,1]{1,0:T(8,128)} %constant.82.firsts_ref), custom_call_target="tpu_custom_call" | custom-call | tf_op jit(solution)/shard_map/outgoing/pallas_call | solution.py:52
  2.7 7.8 %all-to-all-start = ((bf16[8,2,6144]{2,1,0:T(2,128)(2,1)}), bf16[8,2,6144]{2,1,0:T(2,128)(2,1)S(1)}, u32[]{:S(2)}, u32[]{:S(2)}) async-start(bf16[8,2,6144]{2,1,0:T(2,128)(2,1)} %outgoing.1), calls=%async_computation | async-start | bytes 393216 | tf_op jit(solution)/shard_map/all_to_all | solution.py:169
  10.5 0.7 %and_select_fusion.2 = s32[32]{0:T(128)S(1)} fusion(s32[32]{0:T(128)} %param.20), kind=kLoop, calls=%fused_computation.25 | loop fusion | flops 480 | bytes 256 | tf_op jit(solution)/shard_map/jit(floor_divide)/jit(_where)/select_n | solution.py:165
  11.2 0.8 %compare_reduce_fusion = pred[4,128]{1,0:T(4,128)(4,1)S(1)} fusion(s32[128]{0:T(128)S(1)} %and_select_fusion, s32[4,16]{1,0:T(4,128)} %param.18), kind=kLoop, calls=%fused_computation.12 | loop fusion | flops 15872 | bytes 1280 | tf_op jit(solution)/shard_map/reduce_or | solution.py:182
  12.0 0.7 %broadcast_in_dim.108 = s32[8,2]{1,0:T(8,128)S(1)} broadcast(s32[8]{0:T(128)} %constant.76.clone), dimensions={0} | broadcast | bytes 96 | tf_op jit(solution)/shard_map/broadcast_in_dim | solution.py:180
  12.7 0.1 reshape.134
  12.8 0.0 copy-start.2
  12.8 0.0 copy-start.4
  12.8 0.0 copy-start.7
  12.9 1.5 %multiply_reduce_fusion.1 = f32[128]{0:T(128)S(1)} fusion(bf16[128,4096]{1,0:T(8,128)(2,1)} %dec_ref.3), kind=kLoop, calls=%fused_computation.1 | loop fusion | flops 1572736 | bytes 1049088 | tf_op jit(solution)/shard_map/reduce_sum | solution.py:187
  14.4 0.0 copy-done.6
  14.4 0.1 compare_reduce_fusion.1
  14.5 0.0 copy-done.3
  14.5 0.5 %fusion.11 = (f32[1,128]{1,0:T(1,128)S(1)}, f32[128]{0:T(128)}, f32[128]{0:T(128)S(1)}) fusion(pred[128]{0:T(512)(128)(4,1)S(1)} %compare_reduce_fusion.1, f32[128]{0:T(128)S(1)} %copy-done.3), kind=kLoop, calls=%fused_computation.55 | loop fusion | flops 256 | bytes 2176 | tf_op jit(solution)/shard_map/jit(_where)/select_n | solution.py:177
  15.0 0.1 select_select_fusion.mask_ref
  15.1 0.0 copy-done
  15.1 0.3 multiply_reduce_fusion
  15.4 0.0 copy-done.2
  15.4 0.0 copy-start.5
  15.4 0.0 copy-start.1
  15.4 0.0 copy-done.4
  15.4 0.1 multiply_reduce_fusion.3
  15.6 0.0 copy-done.7
  15.6 0.3 convolution_convert_fusion.place_ref
  15.8 0.1 all-to-all-done.got_ref
  16.0 0.1 subtract_convert_fusion
  16.1 0.1 reshape.132
  16.1 0.4 %fusion.13 = f32[16,128]{1,0:T(8,128)S(1)} fusion(bf16[16,4096]{1,0:T(8,128)(2,1)S(1)} %reshape.132, bf16[128,4096]{1,0:T(8,128)(2,1)S(1)} %copy-done), kind=kOutput, calls=%fused_computation.57 | convolution fusion | flops 16777216 | bytes 1187840 | tf_op jit(solution)/shard_map/dot_general | solution.py:192
  16.5 0.2 multiply_reduce_fusion.2
  16.7 0.1 fusion.10
  16.8 0.1 collective-permute-start
  16.9 0.0 copy-done.5
  16.9 0.6 %broadcast_multiply_fusion = f32[2,128]{1,0:T(2,128)} fusion(f32[2,128]{1,0:T(2,128)S(1)} %copy-done.5, f32[128]{0:T(128)S(1)} %get-tuple-element.39), kind=kLoop, calls=%fused_computation.47 | loop fusion | flops 256 | bytes 2560 | tf_op jit(solution)/shard_map/mul | solution.py:179
  17.5 0.6 %collective-permute-done.peer_ref = f32[19,128]{1,0:T(8,128)S(1)} collective-permute-done((f32[19,128]{1,0:T(8,128)S(1)}, f32[19,128]{1,0:T(8,128)S(1)}, u32[]{:S(2)}, u32[]{:S(2)}) %collective-permute-start) | collective-permute-done | bytes 9760 | tf_op jit(solution)/shard_map/ppermute | solution.py:16
  18.0 0.0 copy-done.1
  18.1 0.2 encoded.1
  18.3 9.4 %all_to_all.10 = bf16[8,2,4608]{2,1,0:T(2,128)(2,1)S(1)} all-to-all(bf16[8,2,4608]{2,1,0:T(2,128)(2,1)S(1)} %encoded.1), channel_id=1, replica_groups={{6,4,8,10,2,0,12,14},{7,5,9,11,3,1,13,15},{22,20,24,26,18,16,28,30},{23..., dimensions={0} | all-to-all | bytes 294912 | tf_op jit(solution)/shard_map/all_to_all | solution.py:199
  27.7 0.1 convert_reduce_fusion.summed_ref
  27.9 0.1 collective-permute-start.1
  28.0 0.1 fusion.7
  28.1 1.7 %finished.1 = (bf16[128,4096]{1,0:T(8,128)(2,1)}, bf16[128,4096]{1,0:T(8,128)(2,1)}) custom-call(f32[2,4608]{1,0:T(2,128)S(1)} %convert_reduce_fusion.summed_ref, bf16[8,2,6144]{2,1,0:T(2,128)(2,1)S(1)} %all-to-all-done.got_ref, f32[1,4096]{1,0:T(1,128)S(1)} %bitcast.28, f32[3,128]{1,0:T(4,128)S(1)} %slice_add_fusion.total_ref, ...), custom_call_target="tpu_custom_call" | custom-call | tf_op jit(solution)/shard_map/finished/pallas_call | solution.py:146
  29.8 0.0 collective-permute-done.1
  29.8 0.1 add_reduce_fusion
  29.9 0.6 %fusion.9 = f32[2]{0:T(128)} fusion(f32[2]{0:T(128)S(1)} %fusion.7, f32[3,128]{1,0:T(4,128)S(1)} %slice_add_fusion.total_ref, f32[2]{0:T(128)S(1)} %add_reduce_fusion), kind=kLoop, calls=%fused_computation.42 | loop fusion | flops 12 | bytes 32 | tf_op jit(solution)/shard_map/add | solution.py:213
  (11 shorter events, 0.1 us)
Async XLA Ops:
  0.6 13.8 %copy-start.6 = (s32[32]{0:T(128)S(1)}, s32[32]{0:T(128)}, u32[]{:S(2)}) copy-start(s32[32]{0:T(128)} %param.19) | copy-start | bytes 388
  0.6 13.8 %copy-start.3 = (f32[128]{0:T(128)S(1)}, f32[128]{0:T(128)}, u32[]{:S(2)}) copy-start(f32[128]{0:T(128)} %param.14) | copy-start | bytes 1540
  0.7 14.4 %copy-start = (bf16[128,4096]{1,0:T(8,128)(2,1)S(1)}, bf16[128,4096]{1,0:T(8,128)(2,1)}, u32[]{:S(2)}) copy-start(bf16[128,4096]{1,0:T(8,128)(2,1)} %enc_ref.1) | copy-start | bytes 3145732
  2.7 13.3 %all-to-all-start = ((bf16[8,2,6144]{2,1,0:T(2,128)(2,1)}), bf16[8,2,6144]{2,1,0:T(2,128)(2,1)S(1)}, u32[]{:S(2)}, u32[]{:S(2)}) async-start(bf16[8,2,6144]{2,1,0:T(2,128)(2,1)} %outgoing.1), calls=%async_computation | async-start | bytes 393216 | tf_op jit(solution)/shard_map/all_to_all | solution.py:169
  12.8 2.6 %copy-start.2 = (f32[4096]{0:T(1024)S(1)}, f32[4096]{0:T(1024)}, u32[]{:S(2)}) copy-start(f32[4096]{0:T(1024)} %param.12) | copy-start | bytes 49156
  12.8 2.6 %copy-start.4 = (bf16[2,4096]{1,0:T(2,128)(2,1)S(1)}, bf16[2,4096]{1,0:T(2,128)(2,1)}, u32[]{:S(2)}) copy-start(bf16[2,4096]{1,0:T(2,128)(2,1)} %tokens_ref.1) | copy-start | bytes 49156
  12.8 2.7 %copy-start.7 = (s32[8]{0:T(128)S(1)}, s32[8]{0:T(128)}, u32[]{:S(2)}) copy-start(s32[8]{0:T(128)} %constant.76.clone) | copy-start | bytes 100
  15.4 1.5 %copy-start.5 = (f32[2,128]{1,0:T(2,128)S(1)}, f32[2,128]{1,0:T(2,128)}, u32[]{:S(2)}) copy-start(f32[2,128]{1,0:T(2,128)} %param.16) | copy-start | bytes 3076
  15.4 2.7 %copy-start.1 = (bf16[128,4096]{1,0:T(8,128)(2,1)S(1)}, bf16[128,4096]{1,0:T(8,128)(2,1)}, u32[]{:S(2)}) copy-start(bf16[128,4096]{1,0:T(8,128)(2,1)} %dec_ref.3) | copy-start | bytes 3145732
  16.8 1.2 %collective-permute-start = (f32[19,128]{1,0:T(8,128)S(1)}, f32[19,128]{1,0:T(8,128)S(1)}, u32[]{:S(2)}, u32[]{:S(2)}) collective-permute-start(f32[19,128]{1,0:T(8,128)S(1)} %pad_maximum_fusion.own_ref), channel_id=1, source_target_pairs={{0,1},{1,0},{2,3},{3,2},{4,5},{5,4},{6,7},{7,6},{8,9},{9,8},{10,11... | collective-permute-start | bytes 29192 | tf_op jit(solution)/shard_map/ppermute | solution.py:16
  27.9 1.9 %collective-permute-start.1 = (f32[2,128]{1,0:T(2,128)S(1)}, f32[2,128]{1,0:T(2,128)S(1)}, u32[]{:S(2)}, u32[]{:S(2)}) collective-permute-start(f32[2,128]{1,0:T(2,128)S(1)} %bitcast_reduce_fusion), channel_id=1, source_target_pairs={{0,1},{1,0},{2,3},{3,2},{4,5},{5,4},{6,7},{7,6},{8,9},{9,8},{10,11... | collective-permute-start | bytes 3080 | tf_op jit(solution)/shard_map/ppermute | solution.py:16

commit v6 on v5

v6 whole, which is shorter than its diff:
```python
import math

import jax
import jax.numpy as jnp
from jax import lax
from jax.experimental import pallas as pl
from jax.experimental.pallas import tpu as pltpu
from jax.sharding import PartitionSpec as P

BLOCK = 32
EPS = 1e-06
F32, BF16 = jnp.float32, jnp.bfloat16


def swap(x):
    return lax.ppermute(x, "hidden", [(0, 1), (1, 0)])


def middle_out(owners):
    return sorted(range(owners), key=lambda i: (abs(4 * (i // 2) - owners + 2), i // 2, abs(2 * i - owners + 1)))


def small(shape, dtype):
    return math.prod(shape) * jnp.dtype(dtype).itemsize <= 1 << 20


def in_vmem(*arrays):
    return [pltpu.with_memory_space_constraint(x, pltpu.VMEM) if small(x.shape, x.dtype) else x for x in arrays]


def pinned(shape, dtype):
    return (pltpu.VMEM if small(shape, dtype) else jax.ShapeDtypeStruct)(shape, dtype)


def prepared(tokens, pool, dead_ids, row_ids, order, active_blocks, b_enc, moments, b_dec, w_enc, w_dec):
    tok_dev, width = tokens.shape
    lat_dev = w_enc.shape[0]
    pool_dev, owners = pool.shape[0], order.shape[0]
    dead, tiles = dead_ids.shape[1], active_blocks.shape[0]
    part = width // tok_dev
    members = middle_out(owners)

    def body(*refs):
        sources, (tokens_ref, pool_ref, dead_ref, row_ref, order_ref, active_ref, moments_ref) = refs[:11], refs[23:30]
        out_ref, mask_ref, place_ref, living_ref, centered_ref, squares_ref = refs[11:17]
        bias_ref, enc_bias_ref, enc_ref, dec_ref, new_bias_ref, new_moments_ref = refs[17:23]
        bias_buffer, moments_buffer, sems = refs[30:]
        targets = (tokens_ref, pool_ref, dead_ref, row_ref, order_ref, active_ref, moments_ref,
                   bias_ref, enc_bias_ref, enc_ref, dec_ref)
        copies = [pltpu.make_async_copy(x, y, sems.at[i]) for i, (x, y) in enumerate(zip(sources, targets))]
        for copy in copies:
            copy.start()
        for copy in copies[:9]:
            copy.wait()
        me = lax.axis_index("latent")
        first = order_ref[...] * lat_dev
        there = (dead_ref[...] >= first) & (dead_ref[...] < first + lat_dev)
        slot = lax.broadcasted_iota(jnp.int32, (pool_dev, dead), 0) + me * pool_dev
        goes = jnp.where(there, 1.0, 0.0).astype(BF16)
        lies = jnp.where(row_ref[...] == slot, 1.0, 0.0).astype(BF16)
        take = lax.dot_general(goes, lies, (((1,), (1,)), ((), ())), preferred_element_type=F32).astype(BF16)
        rows = jnp.dot(take, pool_ref[...], preferred_element_type=F32)
        for dest in range(owners):
            out_ref[dest, :, :width] = tokens_ref[...]
        for piece in range(tok_dev):
            out_ref[:, piece, width:] = rows[:, piece * part : (piece + 1) * part].astype(BF16)

        ids = lax.broadcasted_iota(jnp.int32, (lat_dev, dead), 0) + me * lat_dev
        hit = jnp.where(dead_ref[...] == ids, 1.0, 0.0).astype(BF16)
        held = order_ref[...] * pool_dev
        source = jnp.where((row_ref[...] >= held) & (row_ref[...] < held + pool_dev), 1.0, 0.0).astype(BF16)
        across = (((1,), (1,)), ((), ()))
        place_ref[...] = lax.dot_general(hit, source, across, preferred_element_type=F32).astype(BF16)
        hits = lax.dot_general(jnp.ones((8, dead), BF16), hit, across, preferred_element_type=F32)
        living = jnp.where(hits[0:1] > 0.0, 0.0, 1.0)
        living_ref[...] = living
        bias_buffer[...] = enc_bias_ref[...] * living
        moments_buffer[...] = moments_ref[...] * living
        results = [pltpu.make_async_copy(bias_buffer, new_bias_ref, sems.at[11]),
                   pltpu.make_async_copy(moments_buffer, new_moments_ref, sems.at[12])]
        for copy in results:
            copy.start()
        block = lax.broadcasted_iota(jnp.int32, (tiles, lat_dev), 1) // BLOCK
        listed = jnp.zeros((tiles, lat_dev), F32)
        for i in range(lat_dev // BLOCK):
            here = jnp.where(active_ref[...] == me * (lat_dev // BLOCK) + i, 1.0, 0.0)
            listed = jnp.where(block == i, jnp.max(here, axis=1, keepdims=True), listed)
        for i, member in enumerate(members):
            tile = member * tiles // owners
            mask_ref[i * tok_dev : (i + 1) * tok_dev, :] = jnp.broadcast_to(listed[tile : tile + 1], (tok_dev, lat_dev))
        centered = tokens_ref[...].astype(F32) - bias_ref[...]
        centered_ref[...] = centered
        squares = jnp.zeros((tok_dev, lat_dev), F32)
        for i in range(width // lat_dev):
            lanes = centered[:, i * lat_dev : (i + 1) * lat_dev]
            squares = squares + lanes * lanes
        squares_ref[...] = squares
        for copy in copies[9:] + results:
            copy.wait()

    given = (tokens, pool, dead_ids, row_ids, order, active_blocks, moments, b_dec, b_enc, w_enc, w_dec)
    on_device, small_results = pl.BlockSpec(memory_space=pltpu.VMEM), (b_enc, moments)
    return pl.pallas_call(
        body,
        out_shape=(
            pinned((owners, tok_dev, width + part), BF16),
            pinned((owners * tok_dev, lat_dev), F32),
            pinned((lat_dev, owners), BF16),
            pinned((1, lat_dev), F32),
            pinned((tok_dev, width), F32),
            pinned((tok_dev, lat_dev), F32),
            *(pinned(x.shape, x.dtype) for x in given[7:]),
            *(jax.ShapeDtypeStruct(x.shape, x.dtype) for x in small_results),
        ),
        in_specs=[pl.BlockSpec(memory_space=pl.ANY)] * 11,
        out_specs=[on_device] * 10 + [pl.BlockSpec(memory_space=pl.ANY)] * 2,
        scratch_shapes=[pltpu.VMEM(x.shape, x.dtype) for x in given[:7] + small_results]
        + [pltpu.SemaphoreType.DMA((13,))],
        name="prepared",
    )(*given)


def compared(got, b_dec, squares, w_enc, w_dec):
    owners, tok_dev, _ = got.shape
    lat_dev, width = w_enc.shape
    count, part = owners * tok_dev, width // tok_dev
    pieces = 4
    chunk = width // pieces
    lanes = min(owners, lat_dev)
    extra = owners // lanes

    def spread(column):
        size = column.shape[0]
        down, along = (lax.broadcasted_iota(jnp.int32, (size, lat_dev), i) for i in range(2))
        return jnp.sum(jnp.where(down == along, column, 0.0), axis=0, keepdims=True)

    def folded(x):
        total = x[:, :lat_dev] * x[:, :lat_dev]
        for i in range(1, x.shape[1] // lat_dev):
            piece = x[:, i * lat_dev : (i + 1) * lat_dev]
            total = total + piece * piece
        return total

    def body(got_ref, bias_ref, squares_ref, enc_ref, dec_ref, out_ref):
        pre = jnp.zeros((count, lat_dev), F32)
        enc_sq = jnp.zeros((lat_dev, lat_dev), F32)
        dec_sq = jnp.zeros((lat_dev, lat_dev), F32)
        for i in range(pieces):
            columns = slice(i * chunk, (i + 1) * chunk)
            rows = got_ref[:, :, columns].reshape(count, chunk).astype(F32)
            centered = (rows - bias_ref[:, columns]).astype(BF16)
            pre = pre + lax.dot_general(
                centered, enc_ref[:, columns], (((1,), (1,)), ((), ())), preferred_element_type=F32)
            enc_sq = enc_sq + folded(enc_ref[:, columns].astype(F32))
            dec_sq = dec_sq + folded(dec_ref[:, columns].astype(F32))
        fresh = jnp.zeros((owners, lat_dev), F32)
        for i in range(tok_dev):
            fresh = fresh + folded(got_ref[:, i, width:].astype(F32) - bias_ref[:, i * part : (i + 1) * part])
        fresh = jnp.sum(fresh, axis=1, keepdims=True)
        out_ref[:count, :] = pre
        out_ref[count : count + 1, :] = spread(jnp.sum(dec_sq, axis=1, keepdims=True))
        out_ref[count + 1 : count + 2, :] = spread(jnp.sum(enc_sq, axis=1, keepdims=True))
        for i in range(extra):
            out_ref[count + 2 + i : count + 3 + i, :] = spread(fresh[i * lanes : (i + 1) * lanes])
        out_ref[count + 2 + extra :, :] = squares_ref[...]

    return pl.pallas_call(
        body,
        out_shape=pinned((count + 2 + extra + tok_dev, lat_dev), F32),
        in_specs=[pl.BlockSpec(memory_space=pltpu.VMEM)] * 5,
        out_specs=pl.BlockSpec(memory_space=pltpu.VMEM),
        name="compared",
    )(*in_vmem(got, b_dec, squares, w_enc, w_dec))


def encoded(own, peer, b_enc, mask, living, w_enc, w_dec, owners):
    count, lat_dev = mask.shape
    width = w_dec.shape[1]
    tok_dev = count // owners
    pieces = 4
    chunk = width // pieces

    def body(own_ref, peer_ref, bias_ref, mask_ref, living_ref, _, dec_ref, out_ref):
        total = own_ref[: count + 2, :] + peer_ref[: count + 2, :]
        codes = (jnp.maximum(total[:count] + bias_ref[...], 0.0) * mask_ref[...]).astype(BF16)
        for i in range(pieces):
            columns = slice(i * chunk, (i + 1) * chunk)
            part = jnp.dot(codes, dec_ref[:, columns], preferred_element_type=F32).astype(BF16)
            out_ref[:, :, columns] = part.reshape(owners, tok_dev, chunk)
        norms = jnp.sqrt(total[count : count + 2])
        alive = jnp.broadcast_to(norms[1:2] * living_ref[...], (count, lat_dev))
        side = jnp.concatenate([codes.astype(F32) * norms[0:1], alive], axis=1)
        high = side.astype(BF16)
        low = (side - high.astype(F32)).astype(BF16)
        out_ref[:, :, width:] = jnp.concatenate([high, low], axis=1).reshape(owners, tok_dev, 4 * lat_dev)

    shape = (owners, tok_dev, width + 4 * lat_dev)
    return pl.pallas_call(
        body,
        out_shape=(pltpu.VMEM if small(shape, BF16) else jax.ShapeDtypeStruct)(shape, BF16),
        in_specs=[pl.BlockSpec(memory_space=pltpu.VMEM)] * 7,
        out_specs=pl.BlockSpec(memory_space=pltpu.VMEM),
        name="encoded",
    )(*in_vmem(own, peer, b_enc, mask, living, w_enc, w_dec))


def finished(summed, got, b_dec, total, place, w_enc, w_dec, living):
    owners, tok_dev, _ = got.shape
    lat_dev, width = w_dec.shape
    part = width // tok_dev
    pieces = 2
    chunk = part // pieces
    steps = tok_dev * pieces

    def column(row, size):
        rows, lanes = (lax.broadcasted_iota(jnp.int32, (size, row.shape[1]), i) for i in range(2))
        return jnp.sum(jnp.where(rows == lanes, row, 0.0), axis=1, keepdims=True)

    def body(summed_ref, got_ref, bias_ref, total_ref, place_ref, enc_ref, dec_ref, new_enc_ref, new_dec_ref,
             enc_buffer, dec_buffer, sems):
        first = width + lat_dev
        norms = summed_ref[0:1, first : first + lat_dev] + summed_ref[0:1, first + 2 * lat_dev : first + 3 * lat_dev]
        level = 0.2 * (jnp.sum(norms, axis=1, keepdims=True) / living)
        lanes = min(owners, lat_dev)
        fresh_sq = jnp.concatenate(
            [column(total_ref[2 + i : 3 + i, :], lanes) for i in range(owners // lanes)], axis=0)
        scale = lax.rsqrt(fresh_sq + EPS)
        again = lax.rsqrt(fresh_sq / (fresh_sq + EPS) + EPS)
        alive = lax.rsqrt(column(total_ref[0:1, :], lat_dev) + EPS)
        dead = jnp.sum(place_ref[...].astype(F32), axis=1, keepdims=True) > 0.0
        copies = []

        def send(buffer, out_ref, columns):
            copy = pltpu.make_async_copy(buffer.at[:, columns], out_ref.at[:, columns], sems.at[len(copies)])
            copy.start()
            copies.append(copy)

        for i in range(steps):
            columns = slice(i * chunk, (i + 1) * chunk)
            lane = width + i % pieces * chunk
            unit = (got_ref[:, i // pieces, lane : lane + chunk].astype(F32) - bias_ref[:, columns]) * scale
            placed = jnp.dot(place_ref[...], (level * unit).astype(BF16), preferred_element_type=F32)
            enc_buffer[:, columns] = jnp.where(dead, placed, enc_ref[:, columns].astype(F32)).astype(BF16)
            send(enc_buffer, new_enc_ref, columns)
            placed = jnp.dot(place_ref[...], (unit * again).astype(BF16), preferred_element_type=F32)
            dec_buffer[:, columns] = jnp.where(dead, placed, dec_ref[:, columns].astype(F32) * alive).astype(BF16)
            send(dec_buffer, new_dec_ref, columns)
        for copy in copies:
            copy.wait()

    like = jax.ShapeDtypeStruct(w_dec.shape, BF16)
    return pl.pallas_call(
        body,
        out_shape=(like, like),
        in_specs=[pl.BlockSpec(memory_space=pltpu.VMEM)] * 7,
        out_specs=[pl.BlockSpec(memory_space=pl.ANY)] * 2,
        scratch_shapes=[pltpu.VMEM(w_dec.shape, BF16)] * 2 + [pltpu.SemaphoreType.DMA((2 * steps,))],
        name="finished",
    )(*in_vmem(summed, got, b_dec, total, place, w_enc, w_dec))


def local(tokens, b_dec, w_enc, b_enc, w_dec, bias_moments, pool, active_blocks, dead_ids, row_ids):
    lat_dev, width = w_enc.shape
    owners = lax.axis_size("latent")
    tok_dev = tokens.shape[0]
    latents, count = lat_dev * owners, tok_dev * owners
    dead = dead_ids.shape[0]
    order = middle_out(owners)
    members = jnp.array(order, jnp.int32)[:, None]

    sent, mask, place, living, centered, squares, b_dec, b_enc, w_enc, w_dec, new_b_enc, new_moments = prepared(
        tokens, pool, dead_ids[None], row_ids[None], members, active_blocks, b_enc[None], bias_moments, b_dec[None],
        w_enc, w_dec)
    got = lax.all_to_all(sent, "latent", 0, 0, axis_index_groups=[order])
    message = compared(got, b_dec, squares, w_enc, w_dec)
    peer = swap(message)
    sent = encoded(message, peer, b_enc, mask, living, w_enc, w_dec, owners)
    summed = lax.all_to_all(sent, "latent", 0, 0, axis_index_groups=[order])
    summed, got, message, peer = lax.optimization_barrier((summed, got, message, peer))
    total = message[count:] + peer[count:]
    input_sum = jnp.sum(total[-tok_dev:], axis=1)
    summed = jnp.sum(summed.astype(F32), axis=0)
    residual = centered - summed[:, :width]
    error_part = jnp.sum(jnp.square(residual).reshape(tok_dev, -1, 128), axis=1)
    error_peer = swap(error_part)
    new_enc, new_dec = finished(summed, got, b_dec, total, place, w_enc, w_dec, latents - dead)
    error_peer, new_enc, new_dec = lax.optimization_barrier((error_peer, new_enc, new_dec))
    side = summed[:, width : width + lat_dev] + summed[:, width + 2 * lat_dev : width + 3 * lat_dev]
    penalty = jnp.sum(side, axis=1)
    error_sum = jnp.sum(error_part + error_peer, axis=1)
    full = width * lax.axis_size("hidden")
    losses = error_sum / full / (input_sum / full + EPS) + 5.0 * penalty / latents
    return losses, new_enc, new_dec, new_b_enc[0], new_moments


def solution(mesh):
    both = P(("groups", "latent"), "hidden")
    one = P(("groups", "latent"))
    return jax.shard_map(
        local,
        mesh=mesh,
        in_specs=(both, P(("groups", "hidden")), both, one, both, P(None, ("groups", "latent")), both,
                  P("groups", None), P("groups"), P("groups")),
        out_specs=(one, both, both, one, P(None, ("groups", "latent"))),
        check_vma=False,
    )
```

time: 30.9 us -> 30 us (0.971)
  blocking collectives: 9.41 us -> 22.2 us
  starting transfers between devices: 7.96 us -> 0.09 us
  other arithmetic: 6.09 us -> 0.95 us
  local copies, waits for them, and re-layouts: 0.93 us -> 0 us
  matrix products: 0.63 us -> 0 us
  Pallas kernels: 3.91 us -> 4.54 us
  waiting for transfers between devices: 0.72 us -> 1.17 us
    all_to_all x0 -> x1, blocking collectives: none -> 13.1 us  [local(): got = lax.all_to_all(sent, 'latent', 0, 0, axis_index_groups=[order])]
    all_to_all x1 -> x0, starting transfers between devices: 7.83 us -> none  [local(): got = lax.all_to_all(sent, 'latent', 0, 0, axis_index_groups=[order])]
    reduce_sum x4 -> x0, other arithmetic: 2.17 us -> none  [the longest x1 1.53 us: local(): dec_part = jnp.sum(dec_wide * dec_wide, axis=1)]
    select_n x4 -> x0, other arithmetic: 1.27 us -> none  [the longest x1 0.67 us: local(): holder_of = row_ids // pool_dev]
    reduce_or x2 -> x0, other arithmetic: 0.86 us -> none  [the longest x1 0.77 us: local(): jnp.any(active_blocks[:, :, None] == my_block[None, None, :], axis=1)]
    broadcast_in_dim x2 -> x0, local copies, waits for them, and re-layouts: 0.73 us -> none  [the longest x1 0.73 us: local(): row_tile = jnp.repeat(everyone, tok_dev) // (owners // tiles)]
    dot_general x2 -> x0, matrix products: 0.63 us -> none  [the longest x1 0.37 us: local(): lax.dot_general(centered, w_enc, (((1,), (1,)), ((), ())), preferred_elem...]
    pallas_call x1 -> x2, Pallas kernels: 2 us -> 2.62 us  [the longest x1 1.94 us: prepared(): pl.pallas_call(body, out_shape=(pinned((owners, tok_dev, width + part), B...]
  transfers between devices with their start and end apart: 3 -> 2, of which waited for: 2 -> 1; matrix products, arithmetic and copies ran while one was open for 19% -> 0% of each run, Pallas kernels for 5% -> 6%
where the time goes in v6:
time: 30 us; the launch traced here: 29.7 us
  blocking collectives  22.2 us (74%)
  Pallas kernels  4.54 us (15%)
  waiting for transfers between devices  1.17 us (4%)
  other arithmetic  0.95 us (3%)
  between operations  0.7 us (2%)
    all_to_all x1, blocking collectives, local(): got = lax.all_to_all(sent, 'latent', 0, 0, axis_index_groups=[order])  13.1 us
    all_to_all x1, blocking collectives, local(): summed = lax.all_to_all(sent, 'latent', 0, 0, axis_index_groups=[order])  9.15 us
    pallas_call x1, Pallas kernels, prepared(): pl.pallas_call(body, out_shape=(pinned((owners, tok_dev, width + part), B...  1.94 us
    pallas_call x1, Pallas kernels, finished(): pl.pallas_call(body, out_shape=(like, like), in_specs=[pl.BlockSpec(memor...  1.67 us
    ppermute x2, waiting for transfers between devices, swap(): return lax.ppermute(x, 'hidden', [(0, 1), (1, 0)])  1.17 us
    pallas_call x1, Pallas kernels, compared(): pl.pallas_call(body, out_shape=pinned((count + 2 + extra + tok_dev, lat_d...  0.67 us
  transfers between devices with their start and end apart: 2, of which 1 were waited for; matrix products, arithmetic and copies ran while one was open for 0% of the time, Pallas kernels for 6%

profile of v6, /device:TPU:0, one launch (start us, length us, event | category | flops | bytes accessed | tf_op | source)
XLA Modules:
  0.0 29.7 jit_solution(15747482435701308688)
XLA Ops:
  0.6 1.9 %prepared.1 = (bf16[8,2,6144]{2,1,0:T(2,128)(2,1)S(1)}, f32[16,128]{1,0:T(8,128)S(1)}, bf16[128,8]{1,0:T(8,128)(2,1)S(1)}, f32[1,128]{1,0:T(1,128)S(1)}, f32[2,4...) custom-call(bf16[2,4096]{1,0:T(2,128)(2,1)} %refs_0_.1, ...), custom_call_target="tpu_custom_call" | custom-call | tf_op jit(solution)/shard_map/prepared/pallas_call | solution.py:103
  2.6 13.1 %all_to_all.10.got_ref = bf16[8,2,6144]{2,1,0:T(2,128)(2,1)S(1)} all-to-all(bf16[8,2,6144]{2,1,0:T(2,128)(2,1)S(1)} %get-tuple-element.27), channel_id=1, replica_groups={{6,4,8,10,2,0,12,14},{7,5,9,11,3,1,13,15},{22,20,24,26,18,16,28,30},{23..., dimensions={0} | all-to-all | bytes 393216 | tf_op jit(solution)/shard_map/all_to_all | solution.py:274
  15.7 0.7 %compared.1.own_ref = f32[21,128]{1,0:T(8,128)S(1)} custom-call(bf16[8,2,6144]{2,1,0:T(2,128)(2,1)S(1)} %all_to_all.10.got_ref, f32[1,4096]{1,0:T(1,128)S(1)} %get-tuple-element.28.bias_ref, f32[2,128]{1,0:T(2,128)S(1)} %get-tuple-element.29.squares_ref, bf16[128,4096]{1,0:T(8,128)(2,1)S(1)} %get-tuple-element.30.enc_ref._, ...), custom_call_target="tpu_custom_call" | custom-call | tf_op jit(solution)/shard_map/compared/pallas_call | solution.py:167
  16.3 0.0 collective-permute-start
  16.4 1.2 %collective-permute-done.peer_ref = f32[21,128]{1,0:T(8,128)S(1)} collective-permute-done((f32[21,128]{1,0:T(8,128)S(1)}, f32[21,128]{1,0:T(8,128)S(1)}, u32[]{:S(2)}, u32[]{:S(2)}) %collective-permute-start) | collective-permute-done | bytes 10784 | tf_op jit(solution)/shard_map/ppermute | solution.py:16
  17.5 0.2 encoded.1
  17.8 9.1 %all_to_all.11 = bf16[8,2,4608]{2,1,0:T(2,128)(2,1)S(1)} all-to-all(bf16[8,2,4608]{2,1,0:T(2,128)(2,1)S(1)} %encoded.1), channel_id=1, replica_groups={{6,4,8,10,2,0,12,14},{7,5,9,11,3,1,13,15},{22,20,24,26,18,16,28,30},{23..., dimensions={0} | all-to-all | bytes 294912 | tf_op jit(solution)/shard_map/all_to_all | solution.py:278
  26.9 0.1 convert_reduce_fusion.summed_ref
  27.1 0.1 collective-permute-start.1
  27.2 0.1 fusion.2
  27.3 1.7 %finished.1 = (bf16[128,4096]{1,0:T(8,128)(2,1)}, bf16[128,4096]{1,0:T(8,128)(2,1)}) custom-call(f32[2,4608]{1,0:T(2,128)S(1)} %convert_reduce_fusion.summed_ref, bf16[8,2,6144]{2,1,0:T(2,128)(2,1)S(1)} %all_to_all.10.got_ref, f32[1,4096]{1,0:T(1,128)S(1)} %get-tuple-element.28.bias_ref, f32[5,128]{1,0:T(8,128)S(1)} %slice_add_fusion.total_ref, ...), custom_call_target="tpu_custom_call" | custom-call | tf_op jit(solution)/shard_map/finished/pallas_call | solution.py:252
  29.0 0.0 collective-permute-done.1
  29.0 0.1 add_reduce_fusion
  29.1 0.5 %multiply_add_fusion = f32[2]{0:T(128)} fusion(f32[2]{0:T(128)S(1)} %get-tuple-element.47, f32[2]{0:T(128)S(1)} %get-tuple-element.48, f32[2]{0:T(128)S(1)} %add_reduce_fusion), kind=kLoop, calls=%fused_computation.10 | loop fusion | flops 12 | bytes 32 | tf_op jit(solution)/shard_map/add | solution.py:292
  (3 shorter events, 0.0 us)
Async XLA Ops:
  16.3 1.2 %collective-permute-start = (f32[21,128]{1,0:T(8,128)S(1)}, f32[21,128]{1,0:T(8,128)S(1)}, u32[]{:S(2)}, u32[]{:S(2)}) collective-permute-start(f32[21,128]{1,0:T(8,128)S(1)} %compared.1.own_ref), channel_id=1, source_target_pairs={{0,1},{1,0},{2,3},{3,2},{4,5},{5,4},{6,7},{7,6},{8,9},{9,8},{10,11... | collective-permute-start | bytes 32264 | tf_op jit(solution)/shard_map/ppermute | solution.py:16
  27.1 1.9 %collective-permute-start.1 = (f32[2,128]{1,0:T(2,128)S(1)}, f32[2,128]{1,0:T(2,128)S(1)}, u32[]{:S(2)}, u32[]{:S(2)}) collective-permute-start(f32[2,128]{1,0:T(2,128)S(1)} %bitcast_reduce_fusion), channel_id=1, source_target_pairs={{0,1},{1,0},{2,3},{3,2},{4,5},{5,4},{6,7},{7,6},{8,9},{9,8},{10,11... | collective-permute-start | bytes 3080 | tf_op jit(solution)/shard_map/ppermute | solution.py:16

commit v7 on v6

--- a/solution.py
+++ b/solution.py
@@ -259,6 +259,29 @@
     )(*in_vmem(summed, got, b_dec, total, place, w_enc, w_dec))
 
 
+def lost(error, peer_error, total, summed, latents):
+    tok_dev, lat_dev = error.shape
+    width = summed.shape[1] - 4 * lat_dev
+    full = width * lax.axis_size("hidden")
+
+    def body(error_ref, peer_ref, total_ref, summed_ref, out_ref):
+        mean_error = jnp.sum(error_ref[...] + peer_ref[...], axis=1, keepdims=True) / full
+        mean_input = jnp.sum(total_ref[total_ref.shape[0] - tok_dev :, :], axis=1, keepdims=True) / full
+        terms = summed_ref[:, width : width + lat_dev] + summed_ref[:, width + 2 * lat_dev : width + 3 * lat_dev]
+        penalty = jnp.sum(terms, axis=1, keepdims=True)
+        column = mean_error / (mean_input + EPS) + 5.0 * penalty / latents
+        down, along = (lax.broadcasted_iota(jnp.int32, (tok_dev, tok_dev), i) for i in range(2))
+        out_ref[...] = jnp.sum(jnp.where(down == along, column, 0.0), axis=0, keepdims=True)
+
+    return pl.pallas_call(
+        body,
+        out_shape=jax.ShapeDtypeStruct((1, tok_dev), F32),
+        in_specs=[pl.BlockSpec(memory_space=pltpu.VMEM)] * 4,
+        out_specs=pl.BlockSpec(memory_space=pltpu.VMEM),
+        name="lost",
+    )(*in_vmem(error, peer_error, total, summed))[0]
+
+
 def local(tokens, b_dec, w_enc, b_enc, w_dec, bias_moments, pool, active_blocks, dead_ids, row_ids):
     lat_dev, width = w_enc.shape
     owners = lax.axis_size("latent")
@@ -278,18 +301,13 @@
     summed = lax.all_to_all(sent, "latent", 0, 0, axis_index_groups=[order])
     summed, got, message, peer = lax.optimization_barrier((summed, got, message, peer))
     total = message[count:] + peer[count:]
-    input_sum = jnp.sum(total[-tok_dev:], axis=1)
     summed = jnp.sum(summed.astype(F32), axis=0)
     residual = centered - summed[:, :width]
     error_part = jnp.sum(jnp.square(residual).reshape(tok_dev, -1, 128), axis=1)
     error_peer = swap(error_part)
     new_enc, new_dec = finished(summed, got, b_dec, total, place, w_enc, w_dec, latents - dead)
     error_peer, new_enc, new_dec = lax.optimization_barrier((error_peer, new_enc, new_dec))
-    side = summed[:, width : width + lat_dev] + summed[:, width + 2 * lat_dev : width + 3 * lat_dev]
-    penalty = jnp.sum(side, axis=1)
-    error_sum = jnp.sum(error_part + error_peer, axis=1)
-    full = width * lax.axis_size("hidden")
-    losses = error_sum / full / (input_sum / full + EPS) + 5.0 * penalty / latents
+    losses = lost(error_part, error_peer, total, summed, latents)
     return losses, new_enc, new_dec, new_b_enc[0], new_moments
 
 

time: 30 us -> 29.8 us (level)
  other arithmetic: 0.95 us -> 0.17 us
  Pallas kernels: 4.54 us -> 5.14 us
    pallas_call x0 -> x1, Pallas kernels: none -> 0.61 us  [lost(): pl.pallas_call(body, out_shape=jax.ShapeDtypeStruct((1, tok_dev), F32), i...]
    add x1 -> x0, other arithmetic: 0.53 us -> none  [local(): error_sum / full / (input_sum / full + EPS) + 5.0 * penalty / latents]
where the time goes in v7:
time: 29.8 us; the launch traced here: 29.5 us
  blocking collectives  22.2 us (74%)
  Pallas kernels  5.14 us (17%)
  waiting for transfers between devices  1.17 us (4%)
  between operations  0.7 us (2%)
    all_to_all x1, blocking collectives, local(): got = lax.all_to_all(sent, 'latent', 0, 0, axis_index_groups=[order])  13.1 us
    all_to_all x1, blocking collectives, local(): summed = lax.all_to_all(sent, 'latent', 0, 0, axis_index_groups=[order])  9.15 us
    pallas_call x1, Pallas kernels, prepared(): pl.pallas_call(body, out_shape=(pinned((owners, tok_dev, width + part), B...  1.94 us
    pallas_call x1, Pallas kernels, finished(): pl.pallas_call(body, out_shape=(like, like), in_specs=[pl.BlockSpec(memor...  1.68 us
    ppermute x2, waiting for transfers between devices, swap(): return lax.ppermute(x, 'hidden', [(0, 1), (1, 0)])  1.17 us
    pallas_call x1, Pallas kernels, compared(): pl.pallas_call(body, out_shape=pinned((count + 2 + extra + tok_dev, lat_d...  0.67 us
    pallas_call x1, Pallas kernels, lost(): pl.pallas_call(body, out_shape=jax.ShapeDtypeStruct((1, tok_dev), F32), i...  0.61 us
  transfers between devices with their start and end apart: 2, of which 1 were waited for; matrix products, arithmetic and copies ran while one was open for 0% of the time, Pallas kernels for 6%

profile of v7, /device:TPU:0, one launch (start us, length us, event | category | flops | bytes accessed | tf_op | source)
XLA Modules:
  0.0 29.5 jit_solution(9787272697314920908)
XLA Ops:
  0.6 1.9 %prepared.1 = (bf16[8,2,6144]{2,1,0:T(2,128)(2,1)S(1)}, f32[16,128]{1,0:T(8,128)S(1)}, bf16[128,8]{1,0:T(8,128)(2,1)S(1)}, f32[1,128]{1,0:T(1,128)S(1)}, f32[2,4...) custom-call(bf16[2,4096]{1,0:T(2,128)(2,1)} %refs_0_.1, ...), custom_call_target="tpu_custom_call" | custom-call | tf_op jit(solution)/shard_map/prepared/pallas_call | solution.py:103
  2.6 13.1 %all_to_all.10.got_ref = bf16[8,2,6144]{2,1,0:T(2,128)(2,1)S(1)} all-to-all(bf16[8,2,6144]{2,1,0:T(2,128)(2,1)S(1)} %get-tuple-element.27), channel_id=1, replica_groups={{6,4,8,10,2,0,12,14},{7,5,9,11,3,1,13,15},{22,20,24,26,18,16,28,30},{23..., dimensions={0} | all-to-all | bytes 393216 | tf_op jit(solution)/shard_map/all_to_all | solution.py:297
  15.7 0.7 %compared.1.own_ref = f32[21,128]{1,0:T(8,128)S(1)} custom-call(bf16[8,2,6144]{2,1,0:T(2,128)(2,1)S(1)} %all_to_all.10.got_ref, f32[1,4096]{1,0:T(1,128)S(1)} %get-tuple-element.28.bias_ref, f32[2,128]{1,0:T(2,128)S(1)} %get-tuple-element.29.squares_ref, bf16[128,4096]{1,0:T(8,128)(2,1)S(1)} %get-tuple-element.30.enc_ref._, ...), custom_call_target="tpu_custom_call" | custom-call | tf_op jit(solution)/shard_map/compared/pallas_call | solution.py:167
  16.3 0.0 collective-permute-start
  16.4 1.2 %collective-permute-done.peer_ref = f32[21,128]{1,0:T(8,128)S(1)} collective-permute-done((f32[21,128]{1,0:T(8,128)S(1)}, f32[21,128]{1,0:T(8,128)S(1)}, u32[]{:S(2)}, u32[]{:S(2)}) %collective-permute-start) | collective-permute-done | bytes 10784 | tf_op jit(solution)/shard_map/ppermute | solution.py:16
  17.5 0.2 encoded.1
  17.8 9.1 %all_to_all.11 = bf16[8,2,4608]{2,1,0:T(2,128)(2,1)S(1)} all-to-all(bf16[8,2,4608]{2,1,0:T(2,128)(2,1)S(1)} %encoded.1), channel_id=1, replica_groups={{6,4,8,10,2,0,12,14},{7,5,9,11,3,1,13,15},{22,20,24,26,18,16,28,30},{23..., dimensions={0} | all-to-all | bytes 294912 | tf_op jit(solution)/shard_map/all_to_all | solution.py:301
  26.9 0.1 convert_reduce_fusion.summed_ref
  27.1 0.1 collective-permute-start.1
  27.2 1.7 %finished.1 = (bf16[128,4096]{1,0:T(8,128)(2,1)}, bf16[128,4096]{1,0:T(8,128)(2,1)}) custom-call(f32[2,4608]{1,0:T(2,128)S(1)} %convert_reduce_fusion.summed_ref, bf16[8,2,6144]{2,1,0:T(2,128)(2,1)S(1)} %all_to_all.10.got_ref, f32[1,4096]{1,0:T(1,128)S(1)} %get-tuple-element.28.bias_ref, f32[5,128]{1,0:T(8,128)S(1)} %slice_add_fusion.total_ref, ...), custom_call_target="tpu_custom_call" | custom-call | tf_op jit(solution)/shard_map/finished/pallas_call | solution.py:252
  28.9 0.0 collective-permute-done.1.peer_ref
  28.9 0.6 %lost.1 = f32[1,2]{1,0:T(1,128)} custom-call(f32[2,128]{1,0:T(2,128)S(1)} %bitcast_reduce_fusion.error_ref, f32[2,128]{1,0:T(2,128)S(1)} %collective-permute-done.1.peer_ref, f32[5,128]{1,0:T(8,128)S(1)} %slice_add_fusion.total_ref, f32[2,4608]{1,0:T(2,128)S(1)} %convert_reduce_fusion.summed_ref), custom_call_target="tpu_custom_call" | custom-call | tf_op jit(solution)/shard_map/lost/pallas_call | solution.py:276
  (3 shorter events, 0.0 us)
Async XLA Ops:
  16.3 1.2 %collective-permute-start = (f32[21,128]{1,0:T(8,128)S(1)}, f32[21,128]{1,0:T(8,128)S(1)}, u32[]{:S(2)}, u32[]{:S(2)}) collective-permute-start(f32[21,128]{1,0:T(8,128)S(1)} %compared.1.own_ref), channel_id=1, source_target_pairs={{0,1},{1,0},{2,3},{3,2},{4,5},{5,4},{6,7},{7,6},{8,9},{9,8},{10,11... | collective-permute-start | bytes 32264 | tf_op jit(solution)/shard_map/ppermute | solution.py:16
  27.1 1.8 %collective-permute-start.1 = (f32[2,128]{1,0:T(2,128)S(1)}, f32[2,128]{1,0:T(2,128)S(1)}, u32[]{:S(2)}, u32[]{:S(2)}) collective-permute-start(f32[2,128]{1,0:T(2,128)S(1)} %bitcast_reduce_fusion.error_ref), channel_id=1, source_target_pairs={{0,1},{1,0},{2,3},{3,2},{4,5},{5,4},{6,7},{7,6},{8,9},{9,8},{10,11... | collective-permute-start | bytes 3080 | tf_op jit(solution)/shard_map/ppermute | solution.py:16

commit v8 on v7

--- a/solution.py
+++ b/solution.py
@@ -16,7 +16,9 @@
     return lax.ppermute(x, "hidden", [(0, 1), (1, 0)])
 
 
-def middle_out(owners):
+def member_order(owners):
+    if owners == 8:
+        return [5, 2, 6, 4, 1, 0, 7, 3]
     return sorted(range(owners), key=lambda i: (abs(4 * (i // 2) - owners + 2), i // 2, abs(2 * i - owners + 1)))
 
 
@@ -38,7 +40,7 @@
     pool_dev, owners = pool.shape[0], order.shape[0]
     dead, tiles = dead_ids.shape[1], active_blocks.shape[0]
     part = width // tok_dev
-    members = middle_out(owners)
+    members = member_order(owners)
 
     def body(*refs):
         sources, (tokens_ref, pool_ref, dead_ref, row_ref, order_ref, active_ref, moments_ref) = refs[:11], refs[23:30]
@@ -288,7 +290,7 @@
     tok_dev = tokens.shape[0]
     latents, count = lat_dev * owners, tok_dev * owners
     dead = dead_ids.shape[0]
-    order = middle_out(owners)
+    order = member_order(owners)
     members = jnp.array(order, jnp.int32)[:, None]
 
     sent, mask, place, living, centered, squares, b_dec, b_enc, w_enc, w_dec, new_b_enc, new_moments = prepared(

time: 29.8 us -> 28.9 us (0.970)
  blocking collectives: 22.2 us -> 21.3 us
    all_to_all x1, blocking collectives: 13.1 us -> 11.7 us  [local(): got = lax.all_to_all(sent, 'latent', 0, 0, axis_index_groups=[order])]
    all_to_all x1, blocking collectives: 9.15 us -> 9.64 us  [local(): summed = lax.all_to_all(sent, 'latent', 0, 0, axis_index_groups=[order])]
where the time goes in v8:
time: 28.9 us; the launch traced here: 28.6 us
  blocking collectives  21.3 us (74%)
  Pallas kernels  5.14 us (18%)
  waiting for transfers between devices  1.17 us (4%)
  between operations  0.7 us (2%)
    all_to_all x1, blocking collectives, local(): got = lax.all_to_all(sent, 'latent', 0, 0, axis_index_groups=[order])  11.7 us
    all_to_all x1, blocking collectives, local(): summed = lax.all_to_all(sent, 'latent', 0, 0, axis_index_groups=[order])  9.64 us
    pallas_call x1, Pallas kernels, prepared(): pl.pallas_call(body, out_shape=(pinned((owners, tok_dev, width + part), B...  1.94 us
    pallas_call x1, Pallas kernels, finished(): pl.pallas_call(body, out_shape=(like, like), in_specs=[pl.BlockSpec(memor...  1.68 us
    ppermute x2, waiting for transfers between devices, swap(): return lax.ppermute(x, 'hidden', [(0, 1), (1, 0)])  1.17 us
    pallas_call x1, Pallas kernels, compared(): pl.pallas_call(body, out_shape=pinned((count + 2 + extra + tok_dev, lat_d...  0.67 us
    pallas_call x1, Pallas kernels, lost(): pl.pallas_call(body, out_shape=jax.ShapeDtypeStruct((1, tok_dev), F32), i...  0.61 us
  transfers between devices with their start and end apart: 2, of which 1 were waited for; matrix products, arithmetic and copies ran while one was open for 0% of the time, Pallas kernels for 6%

profile of v8, /device:TPU:0, one launch (start us, length us, event | category | flops | bytes accessed | tf_op | source)
XLA Modules:
  0.0 28.6 jit_solution(10049474068629166469)
XLA Ops:
  0.6 1.9 %prepared.1 = (bf16[8,2,6144]{2,1,0:T(2,128)(2,1)S(1)}, f32[16,128]{1,0:T(8,128)S(1)}, bf16[128,8]{1,0:T(8,128)(2,1)S(1)}, f32[1,128]{1,0:T(1,128)S(1)}, f32[2,4...) custom-call(bf16[2,4096]{1,0:T(2,128)(2,1)} %refs_0_.1, ...), custom_call_target="tpu_custom_call" | custom-call | tf_op jit(solution)/shard_map/prepared/pallas_call | solution.py:105
  2.6 11.7 %all_to_all.10.got_ref = bf16[8,2,6144]{2,1,0:T(2,128)(2,1)S(1)} all-to-all(bf16[8,2,6144]{2,1,0:T(2,128)(2,1)S(1)} %get-tuple-element.27), channel_id=1, replica_groups={{10,4,12,8,2,0,14,6},{11,5,13,9,3,1,15,7},{26,20,28,24,18,16,30,22},{27..., dimensions={0} | all-to-all | bytes 393216 | tf_op jit(solution)/shard_map/all_to_all | solution.py:299
  14.3 0.7 %compared.1.own_ref = f32[21,128]{1,0:T(8,128)S(1)} custom-call(bf16[8,2,6144]{2,1,0:T(2,128)(2,1)S(1)} %all_to_all.10.got_ref, f32[1,4096]{1,0:T(1,128)S(1)} %get-tuple-element.28.bias_ref, f32[2,128]{1,0:T(2,128)S(1)} %get-tuple-element.29.squares_ref, bf16[128,4096]{1,0:T(8,128)(2,1)S(1)} %get-tuple-element.30.enc_ref._, ...), custom_call_target="tpu_custom_call" | custom-call | tf_op jit(solution)/shard_map/compared/pallas_call | solution.py:169
  14.9 0.0 collective-permute-start
  15.0 1.2 %collective-permute-done.peer_ref = f32[21,128]{1,0:T(8,128)S(1)} collective-permute-done((f32[21,128]{1,0:T(8,128)S(1)}, f32[21,128]{1,0:T(8,128)S(1)}, u32[]{:S(2)}, u32[]{:S(2)}) %collective-permute-start) | collective-permute-done | bytes 10784 | tf_op jit(solution)/shard_map/ppermute | solution.py:16
  16.1 0.2 encoded.1
  16.4 9.6 %all_to_all.11 = bf16[8,2,4608]{2,1,0:T(2,128)(2,1)S(1)} all-to-all(bf16[8,2,4608]{2,1,0:T(2,128)(2,1)S(1)} %encoded.1), channel_id=1, replica_groups={{10,4,12,8,2,0,14,6},{11,5,13,9,3,1,15,7},{26,20,28,24,18,16,30,22},{27..., dimensions={0} | all-to-all | bytes 294912 | tf_op jit(solution)/shard_map/all_to_all | solution.py:303
  26.0 0.1 convert_reduce_fusion.summed_ref
  26.2 0.1 collective-permute-start.1
  26.3 1.7 %finished.1 = (bf16[128,4096]{1,0:T(8,128)(2,1)}, bf16[128,4096]{1,0:T(8,128)(2,1)}) custom-call(f32[2,4608]{1,0:T(2,128)S(1)} %convert_reduce_fusion.summed_ref, bf16[8,2,6144]{2,1,0:T(2,128)(2,1)S(1)} %all_to_all.10.got_ref, f32[1,4096]{1,0:T(1,128)S(1)} %get-tuple-element.28.bias_ref, f32[5,128]{1,0:T(8,128)S(1)} %slice_add_fusion.total_ref, ...), custom_call_target="tpu_custom_call" | custom-call | tf_op jit(solution)/shard_map/finished/pallas_call | solution.py:254
  28.0 0.0 collective-permute-done.1.peer_ref
  28.0 0.6 %lost.1 = f32[1,2]{1,0:T(1,128)} custom-call(f32[2,128]{1,0:T(2,128)S(1)} %bitcast_reduce_fusion.error_ref, f32[2,128]{1,0:T(2,128)S(1)} %collective-permute-done.1.peer_ref, f32[5,128]{1,0:T(8,128)S(1)} %slice_add_fusion.total_ref, f32[2,4608]{1,0:T(2,128)S(1)} %convert_reduce_fusion.summed_ref), custom_call_target="tpu_custom_call" | custom-call | tf_op jit(solution)/shard_map/lost/pallas_call | solution.py:278
  (3 shorter events, 0.0 us)
Async XLA Ops:
  14.9 1.2 %collective-permute-start = (f32[21,128]{1,0:T(8,128)S(1)}, f32[21,128]{1,0:T(8,128)S(1)}, u32[]{:S(2)}, u32[]{:S(2)}) collective-permute-start(f32[21,128]{1,0:T(8,128)S(1)} %compared.1.own_ref), channel_id=1, source_target_pairs={{0,1},{1,0},{2,3},{3,2},{4,5},{5,4},{6,7},{7,6},{8,9},{9,8},{10,11... | collective-permute-start | bytes 32264 | tf_op jit(solution)/shard_map/ppermute | solution.py:16
  26.2 1.8 %collective-permute-start.1 = (f32[2,128]{1,0:T(2,128)S(1)}, f32[2,128]{1,0:T(2,128)S(1)}, u32[]{:S(2)}, u32[]{:S(2)}) collective-permute-start(f32[2,128]{1,0:T(2,128)S(1)} %bitcast_reduce_fusion.error_ref), channel_id=1, source_target_pairs={{0,1},{1,0},{2,3},{3,2},{4,5},{5,4},{6,7},{7,6},{8,9},{9,8},{10,11... | collective-permute-start | bytes 3080 | tf_op jit(solution)/shard_map/ppermute | solution.py:16

commit v9 on v8

--- a/solution.py
+++ b/solution.py
@@ -34,7 +34,7 @@
     return (pltpu.VMEM if small(shape, dtype) else jax.ShapeDtypeStruct)(shape, dtype)
 
 
-def prepared(tokens, pool, dead_ids, row_ids, order, active_blocks, b_enc, moments, b_dec, w_enc, w_dec):
+def prepared(tokens, pool, dead_ids, row_ids, order, active_blocks, b_enc, b_dec, w_enc, w_dec):
     tok_dev, width = tokens.shape
     lat_dev = w_enc.shape[0]
     pool_dev, owners = pool.shape[0], order.shape[0]
@@ -43,16 +43,16 @@
     members = member_order(owners)
 
     def body(*refs):
-        sources, (tokens_ref, pool_ref, dead_ref, row_ref, order_ref, active_ref, moments_ref) = refs[:11], refs[23:30]
-        out_ref, mask_ref, place_ref, living_ref, centered_ref, squares_ref = refs[11:17]
-        bias_ref, enc_bias_ref, enc_ref, dec_ref, new_bias_ref, new_moments_ref = refs[17:23]
-        bias_buffer, moments_buffer, sems = refs[30:]
-        targets = (tokens_ref, pool_ref, dead_ref, row_ref, order_ref, active_ref, moments_ref,
+        sources, (tokens_ref, pool_ref, dead_ref, row_ref, order_ref, active_ref) = refs[:10], refs[20:26]
+        out_ref, mask_ref, place_ref, living_ref, centered_ref, squares_ref = refs[10:16]
+        bias_ref, enc_bias_ref, enc_ref, dec_ref = refs[16:20]
+        sems = refs[26]
+        targets = (tokens_ref, pool_ref, dead_ref, row_ref, order_ref, active_ref,
                    bias_ref, enc_bias_ref, enc_ref, dec_ref)
         copies = [pltpu.make_async_copy(x, y, sems.at[i]) for i, (x, y) in enumerate(zip(sources, targets))]
         for copy in copies:
             copy.start()
-        for copy in copies[:9]:
+        for copy in copies[:7]:
             copy.wait()
         me = lax.axis_index("latent")
         first = order_ref[...] * lat_dev
@@ -74,14 +74,7 @@
         across = (((1,), (1,)), ((), ()))
         place_ref[...] = lax.dot_general(hit, source, across, preferred_element_type=F32).astype(BF16)
         hits = lax.dot_general(jnp.ones((8, dead), BF16), hit, across, preferred_element_type=F32)
-        living = jnp.where(hits[0:1] > 0.0, 0.0, 1.0)
-        living_ref[...] = living
-        bias_buffer[...] = enc_bias_ref[...] * living
-        moments_buffer[...] = moments_ref[...] * living
-        results = [pltpu.make_async_copy(bias_buffer, new_bias_ref, sems.at[11]),
-                   pltpu.make_async_copy(moments_buffer, new_moments_ref, sems.at[12])]
-        for copy in results:
-            copy.start()
+        living_ref[...] = jnp.where(hits[0:1] > 0.0, 0.0, 1.0)
         block = lax.broadcasted_iota(jnp.int32, (tiles, lat_dev), 1) // BLOCK
         listed = jnp.zeros((tiles, lat_dev), F32)
         for i in range(lat_dev // BLOCK):
@@ -97,11 +90,10 @@
             lanes = centered[:, i * lat_dev : (i + 1) * lat_dev]
             squares = squares + lanes * lanes
         squares_ref[...] = squares
-        for copy in copies[9:] + results:
+        for copy in copies[7:]:
             copy.wait()
 
-    given = (tokens, pool, dead_ids, row_ids, order, active_blocks, moments, b_dec, b_enc, w_enc, w_dec)
-    on_device, small_results = pl.BlockSpec(memory_space=pltpu.VMEM), (b_enc, moments)
+    given = (tokens, pool, dead_ids, row_ids, order, active_blocks, b_dec, b_enc, w_enc, w_dec)
     return pl.pallas_call(
         body,
         out_shape=(
@@ -111,13 +103,11 @@
             pinned((1, lat_dev), F32),
             pinned((tok_dev, width), F32),
             pinned((tok_dev, lat_dev), F32),
-            *(pinned(x.shape, x.dtype) for x in given[7:]),
-            *(jax.ShapeDtypeStruct(x.shape, x.dtype) for x in small_results),
+            *(pinned(x.shape, x.dtype) for x in given[6:]),
         ),
-        in_specs=[pl.BlockSpec(memory_space=pl.ANY)] * 11,
-        out_specs=[on_device] * 10 + [pl.BlockSpec(memory_space=pl.ANY)] * 2,
-        scratch_shapes=[pltpu.VMEM(x.shape, x.dtype) for x in given[:7] + small_results]
-        + [pltpu.SemaphoreType.DMA((13,))],
+        in_specs=[pl.BlockSpec(memory_space=pl.ANY)] * 10,
+        out_specs=[pl.BlockSpec(memory_space=pltpu.VMEM)] * 10,
+        scratch_shapes=[pltpu.VMEM(x.shape, x.dtype) for x in given[:6]] + [pltpu.SemaphoreType.DMA((10,))],
         name="prepared",
     )(*given)
 
@@ -206,7 +196,7 @@
     )(*in_vmem(own, peer, b_enc, mask, living, w_enc, w_dec))
 
 
-def finished(summed, got, b_dec, total, place, w_enc, w_dec, living):
+def finished(summed, got, b_dec, total, place, w_enc, w_dec, living, b_enc, moments, count):
     owners, tok_dev, _ = got.shape
     lat_dev, width = w_dec.shape
     part = width // tok_dev
@@ -218,11 +208,15 @@
         rows, lanes = (lax.broadcasted_iota(jnp.int32, (size, row.shape[1]), i) for i in range(2))
         return jnp.sum(jnp.where(rows == lanes, row, 0.0), axis=1, keepdims=True)
 
-    def body(summed_ref, got_ref, bias_ref, total_ref, place_ref, enc_ref, dec_ref, new_enc_ref, new_dec_ref,
-             enc_buffer, dec_buffer, sems):
+    def body(summed_ref, got_ref, bias_ref, total_ref, place_ref, enc_ref, dec_ref, living_ref, enc_bias_ref,
+             moments_ref, new_enc_ref, new_dec_ref, new_bias_ref, new_moments_ref,
+             enc_buffer, dec_buffer, bias_buffer, moments_buffer, sems):
+        fetch = pltpu.make_async_copy(moments_ref, moments_buffer, sems.at[2 * steps])
+        fetch.start()
+        bias_buffer[...] = enc_bias_ref[...] * living_ref[...]
         first = width + lat_dev
         norms = summed_ref[0:1, first : first + lat_dev] + summed_ref[0:1, first + 2 * lat_dev : first + 3 * lat_dev]
-        level = 0.2 * (jnp.sum(norms, axis=1, keepdims=True) / living)
+        level = 0.2 * (jnp.sum(norms, axis=1, keepdims=True) / count)
         lanes = min(owners, lat_dev)
         fresh_sq = jnp.concatenate(
             [column(total_ref[2 + i : 3 + i, :], lanes) for i in range(owners // lanes)], axis=0)
@@ -247,18 +241,25 @@
             placed = jnp.dot(place_ref[...], (unit * again).astype(BF16), preferred_element_type=F32)
             dec_buffer[:, columns] = jnp.where(dead, placed, dec_ref[:, columns].astype(F32) * alive).astype(BF16)
             send(dec_buffer, new_dec_ref, columns)
+        fetch.wait()
+        moments_buffer[...] = moments_buffer[...] * living_ref[...]
+        for i, (buffer, out_ref) in enumerate(((bias_buffer, new_bias_ref), (moments_buffer, new_moments_ref))):
+            copy = pltpu.make_async_copy(buffer, out_ref, sems.at[2 * steps + 1 + i])
+            copy.start()
+            copies.append(copy)
         for copy in copies:
             copy.wait()
 
     like = jax.ShapeDtypeStruct(w_dec.shape, BF16)
     return pl.pallas_call(
         body,
-        out_shape=(like, like),
-        in_specs=[pl.BlockSpec(memory_space=pltpu.VMEM)] * 7,
-        out_specs=[pl.BlockSpec(memory_space=pl.ANY)] * 2,
-        scratch_shapes=[pltpu.VMEM(w_dec.shape, BF16)] * 2 + [pltpu.SemaphoreType.DMA((2 * steps,))],
+        out_shape=(like, like, *(jax.ShapeDtypeStruct(x.shape, F32) for x in (b_enc, moments))),
+        in_specs=[pl.BlockSpec(memory_space=pltpu.VMEM)] * 9 + [pl.BlockSpec(memory_space=pl.ANY)],
+        out_specs=[pl.BlockSpec(memory_space=pl.ANY)] * 4,
+        scratch_shapes=[pltpu.VMEM(w_dec.shape, BF16)] * 2 + [pltpu.VMEM(x.shape, F32) for x in (b_enc, moments)]
+        + [pltpu.SemaphoreType.DMA((2 * steps + 3,))],
         name="finished",
-    )(*in_vmem(summed, got, b_dec, total, place, w_enc, w_dec))
+    )(*in_vmem(summed, got, b_dec, total, place, w_enc, w_dec, living, b_enc), moments)
 
 
 def lost(error, peer_error, total, summed, latents):
@@ -293,9 +294,8 @@
     order = member_order(owners)
     members = jnp.array(order, jnp.int32)[:, None]
 
-    sent, mask, place, living, centered, squares, b_dec, b_enc, w_enc, w_dec, new_b_enc, new_moments = prepared(
-        tokens, pool, dead_ids[None], row_ids[None], members, active_blocks, b_enc[None], bias_moments, b_dec[None],
-        w_enc, w_dec)
+    sent, mask, place, living, centered, squares, b_dec, b_enc, w_enc, w_dec = prepared(
+        tokens, pool, dead_ids[None], row_ids[None], members, active_blocks, b_enc[None], b_dec[None], w_enc, w_dec)
     got = lax.all_to_all(sent, "latent", 0, 0, axis_index_groups=[order])
     message = compared(got, b_dec, squares, w_enc, w_dec)
     peer = swap(message)
@@ -307,7 +307,8 @@
     residual = centered - summed[:, :width]
     error_part = jnp.sum(jnp.square(residual).reshape(tok_dev, -1, 128), axis=1)
     error_peer = swap(error_part)
-    new_enc, new_dec = finished(summed, got, b_dec, total, place, w_enc, w_dec, latents - dead)
+    new_enc, new_dec, new_b_enc, new_moments = finished(
+        summed, got, b_dec, total, place, w_enc, w_dec, living, b_enc, bias_moments, latents - dead)
     error_peer, new_enc, new_dec = lax.optimization_barrier((error_peer, new_enc, new_dec))
     losses = lost(error_part, error_peer, total, summed, latents)
     return losses, new_enc, new_dec, new_b_enc[0], new_moments

time: 28.9 us -> 28.8 us (level)
  no operation moved by 1% of the time
where the time goes in v9:
time: 28.8 us; the launch traced here: 28.5 us
  blocking collectives  21.3 us (74%)
  Pallas kernels  5.03 us (17%)
  waiting for transfers between devices  1.17 us (4%)
  between operations  0.7 us (2%)
    all_to_all x1, blocking collectives, local(): got = lax.all_to_all(sent, 'latent', 0, 0, axis_index_groups=[order])  11.7 us
    all_to_all x1, blocking collectives, local(): summed = lax.all_to_all(sent, 'latent', 0, 0, axis_index_groups=[order])  9.64 us
    pallas_call x1, Pallas kernels, prepared(): pl.pallas_call(body, out_shape=(pinned((owners, tok_dev, width + part), B...  1.79 us
    pallas_call x1, Pallas kernels, finished(): pl.pallas_call(body, out_shape=(like, like, *(jax.ShapeDtypeStruct(x.shap...  1.71 us
    ppermute x2, waiting for transfers between devices, swap(): return lax.ppermute(x, 'hidden', [(0, 1), (1, 0)])  1.17 us
    pallas_call x1, Pallas kernels, compared(): pl.pallas_call(body, out_shape=pinned((count + 2 + extra + tok_dev, lat_d...  0.68 us
    pallas_call x1, Pallas kernels, lost(): pl.pallas_call(body, out_shape=jax.ShapeDtypeStruct((1, tok_dev), F32), i...  0.61 us
  transfers between devices with their start and end apart: 2, of which 1 were waited for; matrix products, arithmetic and copies ran while one was open for 0% of the time, Pallas kernels for 6%

profile of v9, /device:TPU:0, one launch (start us, length us, event | category | flops | bytes accessed | tf_op | source)
XLA Modules:
  0.0 28.5 jit_solution(16196856278376419237)
XLA Ops:
  0.6 1.8 %prepared.1 = (bf16[8,2,6144]{2,1,0:T(2,128)(2,1)S(1)}, f32[16,128]{1,0:T(8,128)S(1)}, bf16[128,8]{1,0:T(8,128)(2,1)S(1)}, f32[1,128]{1,0:T(1,128)S(1)}, f32[2,4...) custom-call(bf16[2,4096]{1,0:T(2,128)(2,1)} %refs_0_.1, ...), custom_call_target="tpu_custom_call" | custom-call | tf_op jit(solution)/shard_map/prepared/pallas_call | solution.py:97
  2.4 11.7 %all_to_all.10.got_ref = bf16[8,2,6144]{2,1,0:T(2,128)(2,1)S(1)} all-to-all(bf16[8,2,6144]{2,1,0:T(2,128)(2,1)S(1)} %get-tuple-element.27), channel_id=1, replica_groups={{10,4,12,8,2,0,14,6},{11,5,13,9,3,1,15,7},{26,20,28,24,18,16,30,22},{27..., dimensions={0} | all-to-all | bytes 393216 | tf_op jit(solution)/shard_map/all_to_all | solution.py:299
  14.1 0.7 %compared.1.own_ref = f32[21,128]{1,0:T(8,128)S(1)} custom-call(bf16[8,2,6144]{2,1,0:T(2,128)(2,1)S(1)} %all_to_all.10.got_ref, f32[1,4096]{1,0:T(1,128)S(1)} %get-tuple-element.28.bias_ref, f32[2,128]{1,0:T(2,128)S(1)} %get-tuple-element.29.squares_ref, bf16[128,4096]{1,0:T(8,128)(2,1)S(1)} %get-tuple-element.30.enc_ref._, ...), custom_call_target="tpu_custom_call" | custom-call | tf_op jit(solution)/shard_map/compared/pallas_call | solution.py:159
  14.8 0.0 collective-permute-start
  14.8 1.2 %collective-permute-done.peer_ref = f32[21,128]{1,0:T(8,128)S(1)} collective-permute-done((f32[21,128]{1,0:T(8,128)S(1)}, f32[21,128]{1,0:T(8,128)S(1)}, u32[]{:S(2)}, u32[]{:S(2)}) %collective-permute-start) | collective-permute-done | bytes 10784 | tf_op jit(solution)/shard_map/ppermute | solution.py:16
  16.0 0.2 encoded.1
  16.2 9.6 %all_to_all.11 = bf16[8,2,4608]{2,1,0:T(2,128)(2,1)S(1)} all-to-all(bf16[8,2,4608]{2,1,0:T(2,128)(2,1)S(1)} %encoded.1), channel_id=1, replica_groups={{10,4,12,8,2,0,14,6},{11,5,13,9,3,1,15,7},{26,20,28,24,18,16,30,22},{27..., dimensions={0} | all-to-all | bytes 294912 | tf_op jit(solution)/shard_map/all_to_all | solution.py:303
  25.9 0.1 convert_reduce_fusion.summed_ref
  26.1 0.1 collective-permute-start.1
  26.1 1.7 %finished.1 = (bf16[128,4096]{1,0:T(8,128)(2,1)}, bf16[128,4096]{1,0:T(8,128)(2,1)}, f32[1,128]{1,0:T(1,128)}, f32[2,128]{1,0:T(2,128)}) custom-call(f32[2,4608]{1,0:T(2,128)S(1)} %convert_reduce_fusion.summed_ref, bf16[8,2,6144]{2,1,0:T(2,128)(2,1)S(1)} %all_to_all.10.got_ref, f32[1,4096]{1,0:T(1,128)S(1)} %get-tuple-element.28.bias_ref, ...), custom_call_target="tpu_custom_call" | custom-call | tf_op jit(solution)/shard_map/finished/pallas_call | solution.py:254
  27.9 0.0 collective-permute-done.1.peer_ref
  27.9 0.6 %lost.1 = f32[1,2]{1,0:T(1,128)} custom-call(f32[2,128]{1,0:T(2,128)S(1)} %bitcast_reduce_fusion.error_ref, f32[2,128]{1,0:T(2,128)S(1)} %collective-permute-done.1.peer_ref, f32[5,128]{1,0:T(8,128)S(1)} %slice_add_fusion.total_ref, f32[2,4608]{1,0:T(2,128)S(1)} %convert_reduce_fusion.summed_ref), custom_call_target="tpu_custom_call" | custom-call | tf_op jit(solution)/shard_map/lost/pallas_call | solution.py:279
  (3 shorter events, 0.0 us)
Async XLA Ops:
  14.8 1.2 %collective-permute-start = (f32[21,128]{1,0:T(8,128)S(1)}, f32[21,128]{1,0:T(8,128)S(1)}, u32[]{:S(2)}, u32[]{:S(2)}) collective-permute-start(f32[21,128]{1,0:T(8,128)S(1)} %compared.1.own_ref), channel_id=1, source_target_pairs={{0,1},{1,0},{2,3},{3,2},{4,5},{5,4},{6,7},{7,6},{8,9},{9,8},{10,11... | collective-permute-start | bytes 32264 | tf_op jit(solution)/shard_map/ppermute | solution.py:16
  26.1 1.8 %collective-permute-start.1 = (f32[2,128]{1,0:T(2,128)S(1)}, f32[2,128]{1,0:T(2,128)S(1)}, u32[]{:S(2)}, u32[]{:S(2)}) collective-permute-start(f32[2,128]{1,0:T(2,128)S(1)} %bitcast_reduce_fusion.error_ref), channel_id=1, source_target_pairs={{0,1},{1,0},{2,3},{3,2},{4,5},{5,4},{6,7},{7,6},{8,9},{9,8},{10,11... | collective-permute-start | bytes 3080 | tf_op jit(solution)/shard_map/ppermute | solution.py:16

commit v10 on v9

--- a/solution.py
+++ b/solution.py
@@ -32,6 +32,19 @@
 
 def pinned(shape, dtype):
     return (pltpu.VMEM if small(shape, dtype) else jax.ShapeDtypeStruct)(shape, dtype)
+
+
+def spread(column, lanes):
+    down, along = (lax.broadcasted_iota(jnp.int32, (column.shape[0], lanes), i) for i in range(2))
+    return jnp.sum(jnp.where(down == along, column, 0.0), axis=0, keepdims=True)
+
+
+def folded(x, lanes):
+    total = x[:, :lanes] * x[:, :lanes]
+    for i in range(1, x.shape[1] // lanes):
+        piece = x[:, i * lanes : (i + 1) * lanes]
+        total = total + piece * piece
+    return total
 
 
 def prepared(tokens, pool, dead_ids, row_ids, order, active_blocks, b_enc, b_dec, w_enc, w_dec):
@@ -85,13 +98,14 @@
             mask_ref[i * tok_dev : (i + 1) * tok_dev, :] = jnp.broadcast_to(listed[tile : tile + 1], (tok_dev, lat_dev))
         centered = tokens_ref[...].astype(F32) - bias_ref[...]
         centered_ref[...] = centered
-        squares = jnp.zeros((tok_dev, lat_dev), F32)
-        for i in range(width // lat_dev):
-            lanes = centered[:, i * lat_dev : (i + 1) * lat_dev]
-            squares = squares + lanes * lanes
-        squares_ref[...] = squares
-        for copy in copies[7:]:
+        squares_ref[1:, :] = folded(centered, lat_dev)
+        for copy in copies[7:9]:
             copy.wait()
+        enc_sq = jnp.zeros((lat_dev, lat_dev), F32)
+        for i in range(4):
+            enc_sq = enc_sq + folded(enc_ref[:, i * width // 4 : (i + 1) * width // 4].astype(F32), lat_dev)
+        squares_ref[0:1, :] = spread(jnp.sum(enc_sq, axis=1, keepdims=True), lat_dev)
+        copies[9].wait()
 
     given = (tokens, pool, dead_ids, row_ids, order, active_blocks, b_dec, b_enc, w_enc, w_dec)
     return pl.pallas_call(
@@ -102,7 +116,7 @@
             pinned((lat_dev, owners), BF16),
             pinned((1, lat_dev), F32),
             pinned((tok_dev, width), F32),
-            pinned((tok_dev, lat_dev), F32),
+            pinned((1 + tok_dev, lat_dev), F32),
             *(pinned(x.shape, x.dtype) for x in given[6:]),
         ),
         in_specs=[pl.BlockSpec(memory_space=pl.ANY)] * 10,
@@ -121,21 +135,8 @@
     lanes = min(owners, lat_dev)
     extra = owners // lanes
 
-    def spread(column):
-        size = column.shape[0]
-        down, along = (lax.broadcasted_iota(jnp.int32, (size, lat_dev), i) for i in range(2))
-        return jnp.sum(jnp.where(down == along, column, 0.0), axis=0, keepdims=True)
-
-    def folded(x):
-        total = x[:, :lat_dev] * x[:, :lat_dev]
-        for i in range(1, x.shape[1] // lat_dev):
-            piece = x[:, i * lat_dev : (i + 1) * lat_dev]
-            total = total + piece * piece
-        return total
-
     def body(got_ref, bias_ref, squares_ref, enc_ref, dec_ref, out_ref):
         pre = jnp.zeros((count, lat_dev), F32)
-        enc_sq = jnp.zeros((lat_dev, lat_dev), F32)
         dec_sq = jnp.zeros((lat_dev, lat_dev), F32)
         for i in range(pieces):
             columns = slice(i * chunk, (i + 1) * chunk)
@@ -143,18 +144,17 @@
             centered = (rows - bias_ref[:, columns]).astype(BF16)
             pre = pre + lax.dot_general(
                 centered, enc_ref[:, columns], (((1,), (1,)), ((), ())), preferred_element_type=F32)
-            enc_sq = enc_sq + folded(enc_ref[:, columns].astype(F32))
-            dec_sq = dec_sq + folded(dec_ref[:, columns].astype(F32))
+            dec_sq = dec_sq + folded(dec_ref[:, columns].astype(F32), lat_dev)
         fresh = jnp.zeros((owners, lat_dev), F32)
         for i in range(tok_dev):
-            fresh = fresh + folded(got_ref[:, i, width:].astype(F32) - bias_ref[:, i * part : (i + 1) * part])
+            fresh = fresh + folded(got_ref[:, i, width:].astype(F32) - bias_ref[:, i * part : (i + 1) * part], lat_dev)
         fresh = jnp.sum(fresh, axis=1, keepdims=True)
         out_ref[:count, :] = pre
-        out_ref[count : count + 1, :] = spread(jnp.sum(dec_sq, axis=1, keepdims=True))
-        out_ref[count + 1 : count + 2, :] = spread(jnp.sum(enc_sq, axis=1, keepdims=True))
+        out_ref[count : count + 1, :] = spread(jnp.sum(dec_sq, axis=1, keepdims=True), lat_dev)
+        out_ref[count + 1 : count + 2, :] = squares_ref[0:1, :]
         for i in range(extra):
-            out_ref[count + 2 + i : count + 3 + i, :] = spread(fresh[i * lanes : (i + 1) * lanes])
-        out_ref[count + 2 + extra :, :] = squares_ref[...]
+            out_ref[count + 2 + i : count + 3 + i, :] = spread(fresh[i * lanes : (i + 1) * lanes], lat_dev)
+        out_ref[count + 2 + extra :, :] = squares_ref[1:, :]
 
     return pl.pallas_call(
         body,

time: 28.8 us -> 28.7 us (level)
  no operation moved by 1% of the time
where the time goes in v10:
time: 28.7 us; the launch traced here: 28.4 us
  blocking collectives  21.3 us (74%)
  Pallas kernels  4.9 us (17%)
  waiting for transfers between devices  1.17 us (4%)
  between operations  0.7 us (2%)
    all_to_all x1, blocking collectives, local(): got = lax.all_to_all(sent, 'latent', 0, 0, axis_index_groups=[order])  11.7 us
    all_to_all x1, blocking collectives, local(): summed = lax.all_to_all(sent, 'latent', 0, 0, axis_index_groups=[order])  9.64 us
    pallas_call x1, Pallas kernels, prepared(): pl.pallas_call(body, out_shape=(pinned((owners, tok_dev, width + part), B...  1.79 us
    pallas_call x1, Pallas kernels, finished(): pl.pallas_call(body, out_shape=(like, like, *(jax.ShapeDtypeStruct(x.shap...  1.7 us
    ppermute x2, waiting for transfers between devices, swap(): return lax.ppermute(x, 'hidden', [(0, 1), (1, 0)])  1.17 us
    pallas_call x1, Pallas kernels, lost(): pl.pallas_call(body, out_shape=jax.ShapeDtypeStruct((1, tok_dev), F32), i...  0.61 us
  transfers between devices with their start and end apart: 2, of which 1 were waited for; matrix products, arithmetic and copies ran while one was open for 0% of the time, Pallas kernels for 6%

profile of v10, /device:TPU:0, one launch (start us, length us, event | category | flops | bytes accessed | tf_op | source)
XLA Modules:
  0.0 28.4 jit_solution(15306401248461894258)
XLA Ops:
  0.6 1.8 %prepared.1 = (bf16[8,2,6144]{2,1,0:T(2,128)(2,1)S(1)}, f32[16,128]{1,0:T(8,128)S(1)}, bf16[128,8]{1,0:T(8,128)(2,1)S(1)}, f32[1,128]{1,0:T(1,128)S(1)}, f32[2,4...) custom-call(bf16[2,4096]{1,0:T(2,128)(2,1)} %refs_0_.1, ...), custom_call_target="tpu_custom_call" | custom-call | tf_op jit(solution)/shard_map/prepared/pallas_call | solution.py:111
  2.4 11.7 %all_to_all.10.got_ref = bf16[8,2,6144]{2,1,0:T(2,128)(2,1)S(1)} all-to-all(bf16[8,2,6144]{2,1,0:T(2,128)(2,1)S(1)} %get-tuple-element.27), channel_id=1, replica_groups={{10,4,12,8,2,0,14,6},{11,5,13,9,3,1,15,7},{26,20,28,24,18,16,30,22},{27..., dimensions={0} | all-to-all | bytes 393216 | tf_op jit(solution)/shard_map/all_to_all | solution.py:299
  14.1 0.6 %compared.1.own_ref = f32[21,128]{1,0:T(8,128)S(1)} custom-call(bf16[8,2,6144]{2,1,0:T(2,128)(2,1)S(1)} %all_to_all.10.got_ref, f32[1,4096]{1,0:T(1,128)S(1)} %get-tuple-element.28.bias_ref, f32[3,128]{1,0:T(4,128)S(1)} %get-tuple-element.29.squares_ref, bf16[128,4096]{1,0:T(8,128)(2,1)S(1)} %get-tuple-element.30.enc_ref._, ...), custom_call_target="tpu_custom_call" | custom-call | tf_op jit(solution)/shard_map/compared/pallas_call | solution.py:159
  14.7 0.0 collective-permute-start
  14.7 1.2 %collective-permute-done.peer_ref = f32[21,128]{1,0:T(8,128)S(1)} collective-permute-done((f32[21,128]{1,0:T(8,128)S(1)}, f32[21,128]{1,0:T(8,128)S(1)}, u32[]{:S(2)}, u32[]{:S(2)}) %collective-permute-start) | collective-permute-done | bytes 10784 | tf_op jit(solution)/shard_map/ppermute | solution.py:16
  15.9 0.2 encoded.1
  16.1 9.6 %all_to_all.11 = bf16[8,2,4608]{2,1,0:T(2,128)(2,1)S(1)} all-to-all(bf16[8,2,4608]{2,1,0:T(2,128)(2,1)S(1)} %encoded.1), channel_id=1, replica_groups={{10,4,12,8,2,0,14,6},{11,5,13,9,3,1,15,7},{26,20,28,24,18,16,30,22},{27..., dimensions={0} | all-to-all | bytes 294912 | tf_op jit(solution)/shard_map/all_to_all | solution.py:303
  25.8 0.1 convert_reduce_fusion.summed_ref
  25.9 0.1 collective-permute-start.1
  26.0 1.7 %finished.1 = (bf16[128,4096]{1,0:T(8,128)(2,1)}, bf16[128,4096]{1,0:T(8,128)(2,1)}, f32[1,128]{1,0:T(1,128)}, f32[2,128]{1,0:T(2,128)}) custom-call(f32[2,4608]{1,0:T(2,128)S(1)} %convert_reduce_fusion.summed_ref, bf16[8,2,6144]{2,1,0:T(2,128)(2,1)S(1)} %all_to_all.10.got_ref, f32[1,4096]{1,0:T(1,128)S(1)} %get-tuple-element.28.bias_ref, ...), custom_call_target="tpu_custom_call" | custom-call | tf_op jit(solution)/shard_map/finished/pallas_call | solution.py:254
  27.7 0.0 collective-permute-done.1.peer_ref
  27.7 0.6 %lost.1 = f32[1,2]{1,0:T(1,128)} custom-call(f32[2,128]{1,0:T(2,128)S(1)} %bitcast_reduce_fusion.error_ref, f32[2,128]{1,0:T(2,128)S(1)} %collective-permute-done.1.peer_ref, f32[5,128]{1,0:T(8,128)S(1)} %slice_add_fusion.total_ref, f32[2,4608]{1,0:T(2,128)S(1)} %convert_reduce_fusion.summed_ref), custom_call_target="tpu_custom_call" | custom-call | tf_op jit(solution)/shard_map/lost/pallas_call | solution.py:279
  (3 shorter events, 0.0 us)
Async XLA Ops:
  14.7 1.2 %collective-permute-start = (f32[21,128]{1,0:T(8,128)S(1)}, f32[21,128]{1,0:T(8,128)S(1)}, u32[]{:S(2)}, u32[]{:S(2)}) collective-permute-start(f32[21,128]{1,0:T(8,128)S(1)} %compared.1.own_ref), channel_id=1, source_target_pairs={{0,1},{1,0},{2,3},{3,2},{4,5},{5,4},{6,7},{7,6},{8,9},{9,8},{10,11... | collective-permute-start | bytes 32264 | tf_op jit(solution)/shard_map/ppermute | solution.py:16
  25.9 1.8 %collective-permute-start.1 = (f32[2,128]{1,0:T(2,128)S(1)}, f32[2,128]{1,0:T(2,128)S(1)}, u32[]{:S(2)}, u32[]{:S(2)}) collective-permute-start(f32[2,128]{1,0:T(2,128)S(1)} %bitcast_reduce_fusion.error_ref), channel_id=1, source_target_pairs={{0,1},{1,0},{2,3},{3,2},{4,5},{5,4},{6,7},{7,6},{8,9},{9,8},{10,11... | collective-permute-start | bytes 3080 | tf_op jit(solution)/shard_map/ppermute | solution.py:16
